TPU v7x, 512 devices: a whole 4x8x8 slice. The times are simulated.
512 devices in a mesh: ctx: 8 (over z_lo, core), ch: 64 (over z_hi, x, y).
Axes of the slice: x: 4, y: 8, z: 8 (z_hi: 2, z_lo: 4; z = z_hi * 4 + z_lo), core: 2. Of those that a mesh axis runs over, the one named last changes fastest.
Arguments:
- mamba_in: bfloat16 [4096, 16384], P('ctx', 'ch'), may hold values from -6 to 6
- mamba_gate: bfloat16 [4096, 16384], P('ctx', 'ch'), may hold values from -6 to 6
- conv_weight: float32 [4, 16384], P(None, 'ch'), may hold values from -3 to 3
- conv_bias: float32 [16384], P('ch'), may hold values from -0.5 to 0.5
- proj_delta: bfloat16 [16384, 512], P('ch'), may hold values from -0.046875 to 0.046875
- proj_select: bfloat16 [16384, 32], P('ch'), may hold values from -0.046875 to 0.046875
- delta_weight: bfloat16 [512, 16384], P(None, 'ch'), may hold values from -0.25 to 0.25
- delta_bias: float32 [16384], P('ch'), may hold values from -4.6 to -2.3
- decay_log: float32 [16, 16384], P(None, 'ch'), may hold values from -9 to 0
- skip_gain: float32 [16384], P('ch'), may hold values from 0.5 to 1.5
Outputs:
- mamba_out: bfloat16 [4096, 16384], P('ctx', 'ch')
All inputs are finite; a program needn't handle non-finite values.
Results may differ from a plain program's by a relative error of at most 0.0051.
Values may be sent and summed in bfloat16 or wider, within the bound.
No kernel may reach another device: no remote copies, remote signals or barrier semaphores. Data moves between devices by JAX's collectives and lax.ppermute only.
A program may use at most 64 MiB of HBM per device.

v0:
```python
import jax
import jax.numpy as jnp
from jax import lax
from jax.sharding import PartitionSpec as P

STATE = 16
KWIDTH = 4


NEG_LARGE = -1e30


def shifted(value, axis, steps):
    count = lax.axis_size(axis)
    initial, last = (max(0, -steps), min(count, count - steps))
    return lax.ppermute(value, axis, [(source, source + steps) for source in range(initial, last)])


def on_device(
    mamba_in,
    mamba_gate,
    conv_weight,
    conv_bias,
    proj_delta,
    proj_select,
    delta_weight,
    delta_bias,
    decay_log,
    skip_gain,
):
    row_count = mamba_in.shape[0]
    tail_rows = shifted(mamba_in[row_count - (KWIDTH - 1) :], "ctx", 1)
    extended = jnp.concatenate([tail_rows, mamba_in], axis=0)
    conv_sum = conv_bias[None, :]
    for offset in range(KWIDTH):
        conv_sum = conv_sum + conv_weight[offset][None, :] * extended[
            offset : offset + row_count
        ].astype(jnp.float32)
    inner_act = jax.nn.silu(conv_sum)
    inner_low = inner_act.astype(jnp.bfloat16)
    delta_low, selected = lax.psum(
        (
            jnp.dot(inner_low, proj_delta, preferred_element_type=jnp.float32),
            jnp.dot(inner_low, proj_select, preferred_element_type=jnp.float32),
        ),
        "ch",
    )
    delta_round = delta_low.astype(jnp.bfloat16)
    delta_rate = jax.nn.softplus(
        jnp.dot(delta_round, delta_weight, preferred_element_type=jnp.float32) + delta_bias[None, :]
    )
    decay_rate = -jnp.exp(decay_log)
    b_map = selected[:, :STATE]
    c_map = selected[:, STATE:]
    row_block = 16
    blocks = row_count // row_block
    row_ids = jnp.arange(row_block, dtype=jnp.int32)
    lower_mask = (row_ids[:, None] >= row_ids[None, :])[:, :, None, None]

    def split_rows(tensor):
        return tensor.reshape((blocks, row_block) + tensor.shape[1:])

    def local_pass(carried, block_inputs):
        delta_block, inner_block, b_block, c_block = block_inputs
        cum_log = jnp.cumsum(delta_block, axis=0)[:, None, :] * decay_rate[None]
        gap = cum_log[:, None] - cum_log[None, :]
        kernel = jnp.exp(jnp.where(lower_mask, gap, NEG_LARGE))
        driven = delta_block * inner_block
        pair_weight = c_block[:, None, :] * b_block[None, :, :]
        mixed = jnp.sum(kernel * pair_weight[..., None], axis=2)
        within = jnp.sum(mixed * driven[None], axis=1)
        from_carry = jnp.sum(c_block[:, :, None] * (jnp.exp(cum_log) * carried[None]), axis=1)
        end_state = (
            jnp.sum(kernel[-1] * (b_block[:, :, None] * driven[:, None, :]), axis=0)
            + jnp.exp(cum_log[-1]) * carried
        )
        return (end_state, within + from_carry)

    def correct_pass(carried, block_inputs):
        delta_block, c_block = block_inputs
        cum_delta = jnp.cumsum(delta_block, axis=0)
        decayed = jnp.exp(cum_delta[:, None, :] * decay_rate[None]) * carried[None]
        return (decayed[-1], jnp.sum(c_block[:, :, None] * decayed, axis=1))

    zero_state = jnp.zeros(decay_rate.shape, jnp.float32)
    block_end, local_out = lax.scan(
        local_pass,
        zero_state,
        (split_rows(delta_rate), split_rows(inner_act), split_rows(b_map), split_rows(c_map)),
    )
    block_decay = jnp.exp(decay_rate * jnp.sum(delta_rate, axis=0)[None, :])

    def relay_turn(turn_index, arriving):
        return shifted(block_decay * arriving + block_end, "ctx", 1)

    incoming = lax.fori_loop(0, lax.axis_size("ctx") - 1, relay_turn, zero_state)
    ignored_end, carried_out = lax.scan(
        correct_pass, incoming, (split_rows(delta_rate), split_rows(c_map))
    )
    scan_out = (local_out + carried_out).reshape(row_count, -1) + skip_gain[None, :] * inner_act
    return (scan_out * jax.nn.silu(mamba_gate.astype(jnp.float32))).astype(jnp.bfloat16)


def solution(mesh):
    return jax.shard_map(
        on_device,
        mesh=mesh,
        in_specs=(
            P("ctx", "ch"),
            P("ctx", "ch"),
            P(None, "ch"),
            P("ch"),
            P("ch", None),
            P("ch", None),
            P(None, "ch"),
            P("ch"),
            P(None, "ch"),
            P("ch"),
        ),
        out_specs=P("ctx", "ch"),
        check_vma=False,
    )
```

profile of v0, /device:TPU:1, one launch (start us, length us, event | category | flops | bytes accessed | tf_op | source)
XLA Modules:
  0.0 1395.0 jit_solution(1162831369867782513)
XLA Ops:
  7.3 5.4 collective-permute-start.1
  13.6 2.6 collective-permute-done.1
  16.1 1.8 divide_multiply_fusion
  18.2 396.0 %all-reduce.4 = bf16[512,512]{1,0:T(8,128)(2,1)S(1)} all-reduce(f32[512,512]{1,0:T(8,128)S(1)} %fusion.18), channel_id=1, replica_groups=mesh['ctx'=8,'ch'=64] {'ch'}, use_global_device_ids=true, to_apply=%region_0.1 | all-reduce | flops 262144 | bytes 1572864 | tf_op jit(solution)/shard_map/psum | solution.py:41
  416.5 775.1 %all-reduce.3.cloned.1.call-done = f32[512,32]{0,1:T(8,128)} async-done(((f32[512,32]{0,1:T(8,128)}), f32[512,32]{0,1:T(8,128)}) %all-reduce.3.cloned.1.call-update) | async-done | bytes 65552 | tf_op jit(solution)/shard_map/psum | solution.py:41
  1192.7 113.0 %while.37 = (s32[]{:T(128)}, f32[16,256]{1,0:T(8,128)S(1)}, f32[32,16,256]{2,1,0:T(8,128)S(1)}, f32[32,16,256]{2,1,0:T(8,128)}, f32[16,256]{1,0:T(8,128)S(1)}, /...) while((s32[]{:T(128)}, f32[16,256]{1,0:T(8,128)S(1)}, ...), condition=%wide.region_8.9_spmd.clone, body=%wide.region_2.8_spmd.clone.sunk | while | flops 4862211 | bytes 5989003 | solution.py:86
  1193.5 1.6 multiply_reduce_fusion.9
  1197.0 1.6 multiply_reduce_fusion.9
  1200.6 1.6 multiply_reduce_fusion.9
  1204.1 1.6 multiply_reduce_fusion.9
  1207.6 1.6 multiply_reduce_fusion.9
  1211.2 1.6 multiply_reduce_fusion.9
  1214.7 1.6 multiply_reduce_fusion.9
  1218.2 1.6 multiply_reduce_fusion.9
  1221.8 1.6 multiply_reduce_fusion.9
  1305.7 51.0 %while.35 = (s32[]{:T(128)}, f32[16,256]{1,0:T(8,128)S(1)}, f32[16,256]{1,0:T(8,128)S(1)}, f32[16,256]{1,0:T(8,128)S(1)}, s32[]{:T(128)}) while((s32[]{:T(128)}, f32[16,256]{1,0:T(8,128)S(1)}, f32[16,256]{1,0:T(8,128)S(1)}, f32[16,256]{1,0:T(8,128)S(1)}, s32[]{:T(128)}) %tuple.78), condition=%wide.region_11.12_spmd, body=%wide.region_10.11_spmd.sunk | while | flops 8194 | bytes 131173 | solution.py:96
  1305.7 19.8 %collective-permute-start = (f32[16,256]{1,0:T(8,128)S(1)}, f32[16,256]{1,0:T(8,128)S(1)}, u32[]{:S(2)}, u32[]{:S(2)}) collective-permute-start(f32[16,256]{1,0:T(8,128)S(1)} %multiply_add_fusion.2), channel_id=1, source_target_pairs={{0,64},{64,128},{128,192},{192,256},{256,320},{320,384},{384,448},... | collective-permute-start | bytes 49160 | tf_op jit(solution)/shard_map/while/body/eval_jaxpr/ppermute | solution.py:16
  1326.3 4.2 collective-permute-start
  1331.4 4.2 collective-permute-start
  1336.5 4.2 collective-permute-start
  1341.5 4.2 collective-permute-start
  1346.6 4.2 collective-permute-start
  1351.6 4.2 collective-permute-start
  1356.7 30.4 %while.36 = (s32[]{:T(128)}, f32[16,256]{1,0:T(8,128)S(1)}, f32[32,16,256]{2,1,0:T(8,128)S(1)}, f32[32,16,256]{2,1,0:T(8,128)}, f32[16,256]{1,0:T(8,128)S(1)}, /...) while((s32[]{:T(128)}, f32[16,256]{1,0:T(8,128)S(1)}, f32[32,16,256]{2,1,0:T(8,128)S(1)}, ...), condition=%wide.region_15.16_spmd, body=%wide.region_12.15_spmd.sunk | while | flops 319490 | bytes 461925 | solution.py:97
  (644 shorter events, 137.0 us)
Async XLA Ops:
  6.5 11.4 copy-start
  6.5 407.7 %copy-start.2 = (bf16[256,32]{0,1:T(8,128)(2,1)S(1)}, bf16[256,32]{0,1:T(8,128)(2,1)}, u32[]{:S(2)}) copy-start(bf16[256,32]{0,1:T(8,128)(2,1)} %param.21) | copy-start | bytes 49156
  6.5 408.6 %copy-start.5 = (bf16[512,256]{1,0:T(8,128)(2,1)S(1)}, bf16[512,256]{1,0:T(8,128)(2,1)}, u32[]{:S(2)}) copy-start(bf16[512,256]{1,0:T(8,128)(2,1)} %param.22) | copy-start | bytes 786436
  6.5 408.6 %copy-start.6 = (f32[256]{0:T(256)S(1)}, f32[256]{0:T(256)}, u32[]{:S(2)}) copy-start(f32[256]{0:T(256)} %param.23) | copy-start | bytes 3076
  6.5 409.9 %copy-start.3 = (f32[16,256]{1,0:T(8,128)S(1)}, f32[16,256]{1,0:T(8,128)}, u32[]{:S(2)}) copy-start(f32[16,256]{1,0:T(8,128)} %param.24) | copy-start | bytes 49156
  6.5 1185.0 %all-reduce.3.cloned.1.call-start = ((), (), s32[]{:S(2)}) async-start(), calls=%async_computation | async-start | bytes 131072 | tf_op jit(solution)/shard_map/psum | solution.py:41
  7.3 8.8 collective-permute-start.1
  1305.6 81.6 %copy-start.1 = (bf16[512,256]{1,0:T(8,128)(2,1)S(1)}, bf16[512,256]{1,0:T(8,128)(2,1)}, u32[]{:S(2)}) copy-start(bf16[512,256]{1,0:T(8,128)(2,1)} %param.17) | copy-start | bytes 786436
  1305.6 81.6 %copy-start.4 = (f32[256]{0:T(256)S(1)}, f32[256]{0:T(256)}, u32[]{:S(2)}) copy-start(f32[256]{0:T(256)} %param.25) | copy-start | bytes 3076
  1305.7 20.7 %collective-permute-start = (f32[16,256]{1,0:T(8,128)S(1)}, f32[16,256]{1,0:T(8,128)S(1)}, u32[]{:S(2)}, u32[]{:S(2)}) collective-permute-start(f32[16,256]{1,0:T(8,128)S(1)} %multiply_add_fusion.2), channel_id=1, source_target_pairs={{0,64},{64,128},{128,192},{192,256},{256,320},{320,384},{384,448},... | collective-permute-start | bytes 49160 | tf_op jit(solution)/shard_map/while/body/eval_jaxpr/ppermute | solution.py:16
  1326.3 5.0 collective-permute-start
  1331.4 5.0 collective-permute-start
  1336.5 5.0 collective-permute-start
  1341.5 5.0 collective-permute-start
  1346.6 5.0 collective-permute-start
  1351.6 5.0 collective-permute-start
Sparse Core Ops, SparseCore 0:
  415.2 776.2 all-reduce.2
where the time goes:
time: 1400 us; the launch traced here: 1390 us
  waiting for transfers between devices  784 us (56%)
  blocking collectives  396 us (28%)
  other arithmetic  118 us (8%)
  starting transfers between devices  50.4 us (4%)
  local copies, waits for them, and re-layouts  26.8 us (2%)
    psum x1, waiting for transfers between devices, on_device(): lax.psum((jnp.dot(inner_low, proj_delta, preferred_element_type=jnp.float...  775 us
    psum x1, blocking collectives, on_device(): lax.psum((jnp.dot(inner_low, proj_delta, preferred_element_type=jnp.float...  396 us
    reduce_sum x32, other arithmetic, local_pass(): mixed = jnp.sum(kernel * pair_weight[..., None], axis=2)  51.1 us
    ppermute x8, starting transfers between devices, shifted(): lax.ppermute(value, axis, [(source, source + steps) for source in range(i...  50.3 us
  transfers between devices with their start and end apart: 9, of which 9 were waited for; matrix products, arithmetic and copies ran while one was open for 0% of the time, Pallas kernels for 0%

commit v1 on v0

v1 whole, which is shorter than its diff:
```python
import functools
import math

import jax
import jax.numpy as jnp
from jax import lax
from jax.experimental import pallas as pl
from jax.experimental.pallas import tpu as pltpu
from jax.sharding import PartitionSpec as P

STATE = 16
KWIDTH = 4
LANES = 128
CHUNKS = 8
LOG2E = 1.0 / math.log(2.0)
MIB = 1 << 20
F32 = jnp.float32
BF16 = jnp.bfloat16


def vmem(count):
    return [pl.BlockSpec(memory_space=pltpu.VMEM)] * count


def project_kernel(x_ref, halo_ref, weight_ref, bias_ref, pd_ref, ps_ref, act_ref, part_ref, xs, xp, low, sel):
    rows, width = x_ref.shape
    steps = rows // CHUNKS
    rank = pd_ref.shape[1]
    halves = width // LANES
    for half in range(halves):
        cols = slice(half * LANES, (half + 1) * LANES)
        xs[half, 0:8, :] = halo_ref[...].astype(F32)[-8:, cols]
        xs[half, 8 : 8 + rows, :] = x_ref[:, cols].astype(F32)
        for step in range(-(KWIDTH - 1), steps):
            to = (step + KWIDTH - 1) * CHUNKS
            xp[half, to : to + CHUNKS, :] = xs[half, pl.ds(8 + step, CHUNKS, stride=steps), :]
    block = min(rows, 64)
    for half in range(halves):
        cols = slice(half * LANES, (half + 1) * LANES)
        for start in range(0, rows, block):
            value = bias_ref[:, cols]
            for tap in range(KWIDTH):
                at = start + tap * CHUNKS
                value = value + weight_ref[tap : tap + 1, cols] * xp[half, at : at + block, :]
            value = value / (1.0 + jnp.exp(-value))
            act_ref[start : start + block, cols] = value
            low[start : start + block, cols] = value.astype(BF16)
    maps = ps_ref.shape[1]
    sel[...] = jnp.zeros_like(sel)
    sel[:, 0:maps] = ps_ref[...]
    sel[:, maps : 2 * maps] = ps_ref[...]
    part_ref[:, 0:rank] = jnp.dot(low[...], pd_ref[...], preferred_element_type=F32).astype(BF16)
    both = jnp.dot(low[...], sel[...], preferred_element_type=F32)
    high = both.astype(BF16)
    rest = (both - high.astype(F32)).astype(BF16)
    lane = lax.broadcasted_iota(jnp.int32, both.shape, 1)
    part_ref[:, rank : rank + LANES] = jnp.where(lane < maps, high.astype(F32), rest.astype(F32)).astype(BF16)


def total_kernel(rank, maps, parts_ref, out_ref):
    devices, rows, width = parts_ref.shape
    total = parts_ref[0].astype(F32)
    for source in range(1, devices):
        total = total + parts_ref[source].astype(F32)
    chosen = total[:, rank:]
    lane = lax.broadcasted_iota(jnp.int32, chosen.shape, 1)
    summed = chosen + pltpu.roll(chosen, LANES - maps, 1)
    twice = jnp.where(lane < maps, summed, pltpu.roll(summed, maps, 1))
    high = twice.astype(BF16).astype(F32)
    rest = jnp.where(lane < 2 * maps, twice - high, 0.0)
    mixed = jnp.where(lane < maps, high, rest)
    row = jnp.concatenate([total[:, :rank], mixed], axis=1).astype(BF16)
    for target in range(devices):
        out_ref[target] = row


def spread(first, maps):
    shape = (LANES, STATE * LANES)
    source = lax.broadcasted_iota(jnp.int32, shape, 0)
    group = lax.broadcasted_iota(jnp.int32, shape, 1) >> 7
    hit = (source == group + first) | (source == group + (first + maps))
    return jnp.where(hit, 1.0, 0.0).astype(BF16)


def scan_kernel(
    rank, me_ref, g_ref, act_ref, dw_ref, bias_ref, log_ref,
    y_ref, cum_ref, inside_ref, before_ref, pay_ref,
    delta, drive, b_all, c_all, rate, ends,
):
    rows, width = act_ref.shape
    steps = rows // CHUNKS
    halves = width // LANES
    maps = 2 * STATE
    z = jnp.dot(g_ref[:, :rank], dw_ref[...], preferred_element_type=F32) + bias_ref[...]
    step_size = jnp.maximum(z, 0.0) + jnp.log1p(jnp.exp(-jnp.abs(z)))
    delta[...] = step_size
    drive[...] = step_size * act_ref[...]
    b_all[...] = jnp.dot(g_ref[:, rank:], spread(0, maps), preferred_element_type=F32)
    c_all[...] = jnp.dot(g_ref[:, rank:], spread(STATE, maps), preferred_element_type=F32)
    rate[...] = -jnp.exp(log_ref[...]) * LOG2E
    chunk = lax.broadcasted_iota(jnp.int32, (CHUNKS, LANES), 0)

    for half in range(halves):
        cols = slice(half * LANES, (half + 1) * LANES)
        rates = [jnp.broadcast_to(rate[n : n + 1, cols], (CHUNKS, LANES)) for n in range(STATE)]

        def advance(step, carried, cols=cols, rates=rates):
            states, total = carried
            at = pl.ds(pl.multiple_of(step * CHUNKS, CHUNKS), CHUNKS)
            size = delta[at, cols]
            push = drive[at, cols]
            total = total + size
            out = jnp.zeros((CHUNKS, LANES), F32)
            later = []
            for n in range(STATE):
                group = slice(n * LANES, (n + 1) * LANES)
                now = jnp.exp2(size * rates[n]) * states[n] + push * b_all[at, group]
                out = out + c_all[at, group] * now
                later.append(now)
            y_ref[at, cols] = out
            cum_ref[at, cols] = total
            return later, total

        zero = jnp.zeros((CHUNKS, LANES), F32)
        states, total = lax.fori_loop(0, steps, advance, ([zero] * STATE, zero))
        sums = [total]
        shift = 1
        while shift < CHUNKS:
            sums.append(sums[-1] + jnp.where(chunk >= shift, pltpu.roll(sums[-1], shift, 0), 0.0))
            shift *= 2
        for n in range(STATE):
            end = states[n]
            shift = 1
            for level in range(len(sums) - 1):
                end = end + jnp.exp2(rates[n] * sums[level]) * jnp.where(
                    chunk >= shift, pltpu.roll(end, shift, 0), 0.0
                )
                shift *= 2
            inside_ref[n, :, cols] = jnp.where(chunk >= 1, pltpu.roll(end, 1, 0), 0.0)
            ends[n : n + 1, cols] = end[CHUNKS - 1 :, :]
        before_ref[:, cols] = jnp.where(chunk >= 1, pltpu.roll(sums[-1], 1, 0), 0.0)
        ends[STATE : STATE + 1, cols] = sums[-1][CHUNKS - 1 :, :]

    me = me_ref[0]
    value = ends[0:STATE, :]
    high = value.astype(BF16).astype(F32)
    total = jnp.broadcast_to(ends[STATE : STATE + 1, :], value.shape)
    total_high = total.astype(BF16).astype(F32)
    first = lax.broadcasted_iota(jnp.int32, value.shape, 0) == 0
    tail = jnp.where(first, total_high, total - total_high)
    for target in range(pay_ref.shape[0]):
        use = target > me
        pay_ref[target, 0:16, :] = jnp.where(use, high, 0.0).astype(BF16)
        pay_ref[target, 16:32, :] = jnp.where(use, value - high, 0.0).astype(BF16)
        pay_ref[target, 32:48, :] = jnp.where(use, tail, 0.0).astype(BF16)


def finish_kernel(
    rank, got_ref, g_ref, act_ref, y_ref, cum_ref, inside_ref, before_ref, log_ref, gain_ref, gate_ref,
    out_ref, c_all, rate, carry, ys,
):
    rows, width = act_ref.shape
    steps = rows // CHUNKS
    halves = width // LANES
    c_all[...] = jnp.dot(g_ref[:, rank:], spread(STATE, 2 * STATE), preferred_element_type=F32)
    rate[...] = -jnp.exp(log_ref[...]) * LOG2E
    incoming = jnp.zeros((STATE, width), F32)
    for source in range(got_ref.shape[0] - 1):
        value = got_ref[source, 0:16, :].astype(F32) + got_ref[source, 16:32, :].astype(F32)
        tail = got_ref[source, 32:48, :].astype(F32)
        incoming = jnp.exp2(rate[...] * (tail[0:1, :] + tail[1:2, :])) * incoming + value
    carry[...] = incoming
    for half in range(halves):
        cols = slice(half * LANES, (half + 1) * LANES)
        rates = [jnp.broadcast_to(rate[n : n + 1, cols], (CHUNKS, LANES)) for n in range(STATE)]
        before = before_ref[:, cols]
        entering = [
            inside_ref[n, :, cols] + jnp.exp2(rates[n] * before) * carry[n : n + 1, cols] for n in range(STATE)
        ]
        gain = gain_ref[:, cols]

        def correct(step, _, half=half, cols=cols, rates=rates, entering=entering, gain=gain):
            at = pl.ds(pl.multiple_of(step * CHUNKS, CHUNKS), CHUNKS)
            total = cum_ref[at, cols]
            out = y_ref[at, cols] + gain * act_ref[at, cols]
            for n in range(STATE):
                group = slice(n * LANES, (n + 1) * LANES)
                out = out + (c_all[at, group] * entering[n]) * jnp.exp2(total * rates[n])
            ys[half, pl.ds(step, CHUNKS, stride=steps), :] = out
            return 0

        lax.fori_loop(0, steps, correct, 0)
        gate = gate_ref[:, cols].astype(F32)
        out_ref[:, cols] = (ys[half] * (gate / (1.0 + jnp.exp(-gate)))).astype(BF16)


def on_device(
    mamba_in, mamba_gate, conv_weight, conv_bias, proj_delta, proj_select, delta_weight, delta_bias, decay_log, skip_gain,
):
    rows, width = mamba_in.shape
    rank = proj_delta.shape[1]
    maps = proj_select.shape[1]
    halves = width // LANES
    steps = rows // CHUNKS
    n_ctx, n_ch = lax.axis_size("ctx"), lax.axis_size("ch")
    wide = rank + LANES
    me = lax.axis_index("ctx").astype(jnp.int32).reshape(1)

    halo = lax.ppermute(mamba_in[rows - 16 :], "ctx", [(i, i + 1) for i in range(n_ctx - 1)])
    act, part = pl.pallas_call(
        project_kernel,
        out_shape=(
            jax.ShapeDtypeStruct((rows, width), F32),
            jax.ShapeDtypeStruct((rows, wide), BF16),
        ),
        in_specs=vmem(6),
        out_specs=tuple(vmem(2)),
        scratch_shapes=[
            pltpu.VMEM((halves, rows + 8, LANES), F32),
            pltpu.VMEM((halves, (steps + KWIDTH - 1) * CHUNKS, LANES), F32),
            pltpu.VMEM((rows, width), BF16),
            pltpu.VMEM((width, LANES), BF16),
        ],
        compiler_params=pltpu.CompilerParams(vmem_limit_bytes=16 * MIB),
        name="project",
    )(mamba_in, halo, conv_weight, conv_bias[None, :], proj_delta, proj_select)

    parts = lax.all_to_all(part.reshape(n_ch, rows // n_ch, wide), "ch", 0, 0)
    totals = pl.pallas_call(
        functools.partial(total_kernel, rank, maps),
        out_shape=jax.ShapeDtypeStruct(parts.shape, BF16),
        in_specs=vmem(1),
        out_specs=vmem(1)[0],
        compiler_params=pltpu.CompilerParams(vmem_limit_bytes=16 * MIB),
        name="total",
    )(parts)
    gathered = lax.all_to_all(totals, "ch", 0, 0).reshape(rows, wide)

    y_local, cum, inside, before, pay = pl.pallas_call(
        functools.partial(scan_kernel, rank),
        out_shape=(
            jax.ShapeDtypeStruct((rows, width), F32),
            jax.ShapeDtypeStruct((rows, width), F32),
            jax.ShapeDtypeStruct((STATE, CHUNKS, width), F32),
            jax.ShapeDtypeStruct((CHUNKS, width), F32),
            jax.ShapeDtypeStruct((n_ctx, 3 * STATE, width), BF16),
        ),
        in_specs=[pl.BlockSpec(memory_space=pltpu.SMEM)] + vmem(5),
        out_specs=tuple(vmem(5)),
        scratch_shapes=[
            pltpu.VMEM((rows, width), F32),
            pltpu.VMEM((rows, width), F32),
            pltpu.VMEM((rows, STATE * LANES), F32),
            pltpu.VMEM((rows, STATE * LANES), F32),
            pltpu.VMEM((STATE, width), F32),
            pltpu.VMEM((STATE + 8, width), F32),
        ],
        compiler_params=pltpu.CompilerParams(vmem_limit_bytes=24 * MIB),
        name="local_scan",
    )(me, gathered, act, delta_weight, delta_bias[None, :], decay_log)

    got = lax.all_to_all(pay, "ctx", 0, 0)
    return pl.pallas_call(
        functools.partial(finish_kernel, rank),
        out_shape=jax.ShapeDtypeStruct((rows, width), BF16),
        in_specs=vmem(10),
        out_specs=vmem(1)[0],
        scratch_shapes=[
            pltpu.VMEM((rows, STATE * LANES), F32),
            pltpu.VMEM((STATE, width), F32),
            pltpu.VMEM((STATE, width), F32),
            pltpu.VMEM((halves, rows, LANES), F32),
        ],
        compiler_params=pltpu.CompilerParams(vmem_limit_bytes=24 * MIB),
        name="finish",
    )(got, gathered, act, y_local, cum, inside, before, decay_log, skip_gain[None, :], mamba_gate)


def solution(mesh):
    return jax.shard_map(
        on_device,
        mesh=mesh,
        in_specs=(
            P("ctx", "ch"),
            P("ctx", "ch"),
            P(None, "ch"),
            P("ch"),
            P("ch", None),
            P("ch", None),
            P(None, "ch"),
            P("ch"),
            P(None, "ch"),
            P("ch"),
        ),
        out_specs=P("ctx", "ch"),
        check_vma=False,
    )
```

time: 1400 us -> 107 us (0.08)
  waiting for transfers between devices: 784 us -> 26.5 us
  blocking collectives: 396 us -> 51.1 us
  other arithmetic: 118 us -> 0 us
  starting transfers between devices: 50.4 us -> 11.5 us
  local copies, waits for them, and re-layouts: 26.8 us -> 4.11 us
    psum x1 -> x0, waiting for transfers between devices: 775 us -> none  [on_device(): lax.psum((jnp.dot(inner_low, proj_delta, preferred_element_type=jnp.float...]
    psum x1 -> x0, blocking collectives: 396 us -> none  [on_device(): lax.psum((jnp.dot(inner_low, proj_delta, preferred_element_type=jnp.float...]
    reduce_sum x160 -> x0, other arithmetic: 64.3 us -> none  [the longest x32 51.1 us: local_pass(): mixed = jnp.sum(kernel * pair_weight[..., None], axis=2)]
    all_to_all x0 -> x2, blocking collectives: none -> 51.1 us  [the longest x1 39 us: on_device(): parts = lax.all_to_all(part.reshape(n_ch, rows // n_ch, wide), 'ch', 0, 0)]
    mul x129 -> x0, other arithmetic: 49.5 us -> none  [the longest x32 23.3 us: local_pass(): within = jnp.sum(mixed * driven[None], axis=1)]
    ppermute x8 -> x1, starting transfers between devices: 50.3 us -> 5.38 us  [on_device(): lax.ppermute(mamba_in[rows - 16:], 'ctx', [(i, i + 1) for i in range(n_ct...]
    all_to_all x0 -> x1, waiting for transfers between devices: none -> 23.2 us  [on_device(): gathered = lax.all_to_all(totals, 'ch', 0, 0).reshape(rows, wide)]
    another operation x34 -> x0, local copies, waits for them, and re-layouts: 23.2 us -> none  [the longest x32 23.1 us: correct_pass(): cum_delta = jnp.cumsum(delta_block, axis=0)]
  transfers between devices with their start and end apart: 9 -> 2, of which waited for: 9 -> 2; matrix products, arithmetic and copies ran while one was open for 0% -> 0% of each run, Pallas kernels for 0% -> 0%
where the time goes in v1:
time: 107 us; the launch traced here: 106 us
  blocking collectives  51.1 us (48%)
  waiting for transfers between devices  26.5 us (25%)
  Pallas kernels  12.8 us (12%)
  starting transfers between devices  11.5 us (11%)
  local copies, waits for them, and re-layouts  4.11 us (4%)
    all_to_all x1, blocking collectives, on_device(): parts = lax.all_to_all(part.reshape(n_ch, rows // n_ch, wide), 'ch', 0, 0)  39 us
    all_to_all x1, waiting for transfers between devices, on_device(): gathered = lax.all_to_all(totals, 'ch', 0, 0).reshape(rows, wide)  23.2 us
    all_to_all x1, blocking collectives, on_device(): got = lax.all_to_all(pay, 'ctx', 0, 0)  12.1 us
    all_to_all x1, starting transfers between devices, on_device(): gathered = lax.all_to_all(totals, 'ch', 0, 0).reshape(rows, wide)  6.13 us
    pallas_call x1, Pallas kernels, on_device(): pl.pallas_call(functools.partial(scan_kernel, rank), out_shape=(jax.Shape...  5.54 us
    pallas_call x1, Pallas kernels, on_device(): pl.pallas_call(functools.partial(finish_kernel, rank), out_shape=jax.Shap...  5.4 us
    ppermute x1, starting transfers between devices, on_device(): lax.ppermute(mamba_in[rows - 16:], 'ctx', [(i, i + 1) for i in range(n_ct...  5.38 us
    unnamed x21, local copies, waits for them, and re-layouts  3.4 us
  transfers between devices with their start and end apart: 2, of which 2 were waited for; matrix products, arithmetic and copies ran while one was open for 0% of the time, Pallas kernels for 0%

profile of v1, /device:TPU:1, one launch (start us, length us, event | category | flops | bytes accessed | tf_op | source)
XLA Modules:
  0.0 106.1 jit_solution(241854882848373461)
XLA Ops:
  0.0 0.7 slice.3
  0.7 5.4 %collective-permute-start = (bf16[16,256]{1,0:T(8,128)(2,1)S(1)}, bf16[16,256]{1,0:T(8,128)(2,1)S(1)}, u32[]{:S(2)}, u32[]{:S(2)}) collective-permute-start(bf16[16,256]{1,0:T(8,128)(2,1)S(1)} %slice.3), channel_id=1, source_target_pairs={{0,64},{64,128},{128,192},{192,256},{256,320},{320,384},{384,448},... | collective-permute-start | bytes 24584 | tf_op jit(solution)/shard_map/ppermute | solution.py:209
  6.1 0.0 copy-done.9
  6.1 0.0 copy-start.5
  6.1 0.1 copy.11.ps_ref
  6.2 0.0 copy-start.6
  6.3 3.3 %collective-permute-done.halo_ref = bf16[16,256]{1,0:T(8,128)(2,1)S(1)} collective-permute-done((bf16[16,256]{1,0:T(8,128)(2,1)S(1)}, bf16[16,256]{1,0:T(8,128)(2,1)S(1)}, u32[]{:S(2)}, u32[]{:S(2)}) %collective-permute-start) | collective-permute-done | bytes 8224 | tf_op jit(solution)/shard_map/ppermute | solution.py:209
  9.5 0.0 copy-done.5
  9.5 0.0 copy-done.6
  9.5 0.9 copy-done
  10.5 0.9 copy-done.2
  11.4 0.8 project.1
  12.2 39.0 %all_to_all.15.parts_ref = bf16[64,8,640]{2,1,0:T(8,128)(2,1)S(1)} all-to-all(bf16[64,8,640]{2,1,0:T(8,128)(2,1)S(1)} %bitcast.8), channel_id=1, replica_groups=mesh['ctx'=8,'ch'=64] {'ch'}, dimensions={0} | all-to-all | bytes 1310720 | tf_op jit(solution)/shard_map/all_to_all | solution.py:228
  51.2 1.1 %total.1 = bf16[64,8,640]{2,1,0:T(8,128)(2,1)} custom-call(bf16[64,8,640]{2,1,0:T(8,128)(2,1)S(1)} %all_to_all.15.parts_ref), custom_call_target="tpu_custom_call" | custom-call | tf_op jit(solution)/shard_map/total/pallas_call | solution.py:229
  52.3 6.1 %all-to-all-start.1 = ((bf16[64,8,640]{2,1,0:T(8,128)(2,1)}), bf16[64,8,640]{2,1,0:T(8,128)(2,1)S(1)}, u32[]{:S(2)}, u32[]{:S(2)}) async-start(bf16[64,8,640]{2,1,0:T(8,128)(2,1)} %total.1), calls=%async_computation.1 | async-start | bytes 1310720 | tf_op jit(solution)/shard_map/all_to_all | solution.py:237
  58.4 23.2 %all-to-all-done.1 = bf16[64,8,640]{2,1,0:T(8,128)(2,1)S(1)} async-done(((bf16[64,8,640]{2,1,0:T(8,128)(2,1)}), bf16[64,8,640]{2,1,0:T(8,128)(2,1)S(1)}, u32[]{:S(2)}, u32[]{:S(2)}) %all-to-all-start.1) | async-done | bytes 655392 | tf_op jit(solution)/shard_map/all_to_all | solution.py:237
  81.7 0.0 copy-done.3
  81.7 0.0 copy-done.4
  81.7 0.7 copy-done.7
  82.3 5.5 %local_scan.1 = (f32[512,256]{1,0:T(8,128)S(1)}, f32[512,256]{1,0:T(8,128)S(1)}, f32[16,8,256]{2,1,0:T(8,128)S(1)}, f32[8,256]{1,0:T(8,128)S(1)}, bf16[8,48,256]{2,1,0:T(8,128)(2,1)S(1)}) custom-call(s32[1]{0:T(128)} %bitcast.me_ref, bf16[512,640]{1,0:T(8,128)(2,1)S(1)} %bitcast.6, f32[512,256]{1,0:T(8,128)S(1)} %get-tuple-element.13.act_ref, ...), custom_call_target="tpu_custom_call" | custom-call | tf_op jit(solution)/shard_map/local_scan/pallas_call | solution.py:239
  87.9 0.0 copy-start.1
  87.9 12.1 %all_to_all.16.got_ref = bf16[8,48,256]{2,1,0:T(8,128)(2,1)S(1)} all-to-all(bf16[8,48,256]{2,1,0:T(8,128)(2,1)S(1)} %get-tuple-element.14), channel_id=1, replica_groups=mesh['ctx'=8,'ch'=64] {'ctx'}, dimensions={0} | all-to-all | bytes 393216 | tf_op jit(solution)/shard_map/all_to_all | solution.py:262
  100.0 0.7 copy-done.8
  100.7 5.4 %finish.1 = bf16[512,256]{1,0:T(8,128)(2,1)} custom-call(bf16[8,48,256]{2,1,0:T(8,128)(2,1)S(1)} %all_to_all.16.got_ref, bf16[512,640]{1,0:T(8,128)(2,1)S(1)} %bitcast.7, f32[512,256]{1,0:T(8,128)S(1)} %get-tuple-element.13.act_ref, f32[512,256]{1,0:T(8,128)S(1)} %get-tuple-element.15.y_ref, f32[512,256]{1,0:T(8,128)S(1)} %get-tuple-element.16.cum_ref, ...), custom_call_target="tpu_custom_call" | custom-call | tf_op jit(solution)/shard_map/finish/pallas_call | solution.py:263
  (8 shorter events, 0.0 us)
Async XLA Ops:
  0.0 6.1 %copy-start.9 = (bf16[256,32]{0,1:T(8,128)(2,1)S(1)}, bf16[256,32]{0,1:T(8,128)(2,1)}, u32[]{:S(2)}) copy-start(bf16[256,32]{0,1:T(8,128)(2,1)} %param.15) | copy-start | bytes 49156
  0.7 8.8 %collective-permute-start = (bf16[16,256]{1,0:T(8,128)(2,1)S(1)}, bf16[16,256]{1,0:T(8,128)(2,1)S(1)}, u32[]{:S(2)}, u32[]{:S(2)}) collective-permute-start(bf16[16,256]{1,0:T(8,128)(2,1)S(1)} %slice.3), channel_id=1, source_target_pairs={{0,64},{64,128},{128,192},{192,256},{256,320},{320,384},{384,448},... | collective-permute-start | bytes 24584 | tf_op jit(solution)/shard_map/ppermute | solution.py:209
  6.1 3.4 %copy-start.5 = (f32[4,256]{1,0:T(4,128)S(1)}, f32[4,256]{1,0:T(4,128)}, u32[]{:S(2)}) copy-start(f32[4,256]{1,0:T(4,128)} %weight_ref.1) | copy-start | bytes 12292
  6.2 3.3 %copy-start.6 = (f32[256]{0:T(256)S(1)}, f32[256]{0:T(256)}, u32[]{:S(2)}) copy-start(f32[256]{0:T(256)} %param.13) | copy-start | bytes 3076
  9.5 1.0 copy-start
  10.5 0.9 copy-start.2
  52.3 29.4 %copy-start.3 = (bf16[512,256]{1,0:T(8,128)(2,1)S(1)}, bf16[512,256]{1,0:T(8,128)(2,1)}, u32[]{:S(2)}) copy-start(bf16[512,256]{1,0:T(8,128)(2,1)} %dw_ref.1) | copy-start | bytes 786436
  52.3 29.4 %copy-start.4 = (f32[16,256]{1,0:T(8,128)S(1)}, f32[16,256]{1,0:T(8,128)}, u32[]{:S(2)}) copy-start(f32[16,256]{1,0:T(8,128)} %log_ref.3) | copy-start | bytes 49156
  52.3 29.4 %all-to-all-start.1 = ((bf16[64,8,640]{2,1,0:T(8,128)(2,1)}), bf16[64,8,640]{2,1,0:T(8,128)(2,1)S(1)}, u32[]{:S(2)}, u32[]{:S(2)}) async-start(bf16[64,8,640]{2,1,0:T(8,128)(2,1)} %total.1), calls=%async_computation.1 | async-start | bytes 1310720 | tf_op jit(solution)/shard_map/all_to_all | solution.py:237
  81.7 0.7 copy-start.7
  87.9 12.1 %copy-start.1 = (bf16[512,256]{1,0:T(8,128)(2,1)S(1)}, bf16[512,256]{1,0:T(8,128)(2,1)}, u32[]{:S(2)}) copy-start(bf16[512,256]{1,0:T(8,128)(2,1)} %gate_ref.1) | copy-start | bytes 786436
  100.0 0.7 copy-start.8

commit v2 on v1

v2 whole, which is shorter than its diff:
```python
import functools
import math

import jax
import jax.numpy as jnp
from jax import lax
from jax.experimental import pallas as pl
from jax.experimental.pallas import tpu as pltpu
from jax.sharding import PartitionSpec as P

STATE = 16
KWIDTH = 4
LANES = 128
CHUNKS = 8
HEAD = 32
LOG2E = 1.0 / math.log(2.0)
MIB = 1 << 20
F32 = jnp.float32
BF16 = jnp.bfloat16


def vmem(count):
    return [pl.BlockSpec(memory_space=pltpu.VMEM)] * count


def hbm(count):
    return [pl.BlockSpec(memory_space=pltpu.HBM)] * count


def stay(*arrays):
    return [pltpu.with_memory_space_constraint(array, pltpu.HBM) for array in arrays]


def silu(value):
    return value / (1.0 + jnp.exp(-value))


def put_products(low, pd, sel, maps, rank, part_ref, rows):
    part_ref[rows, 0:rank] = jnp.dot(low, pd, preferred_element_type=F32).astype(BF16)
    both = lax.dot_general(low, sel, (((1,), (1,)), ((), ())), preferred_element_type=F32)
    high = both.astype(BF16).astype(F32)
    lane = lax.broadcasted_iota(jnp.int32, both.shape, 1)
    part_ref[rows, rank : rank + LANES] = jnp.where(lane < maps, high, both - high).astype(BF16)


def project_kernel(
    x_hbm, pd_hbm, ps_hbm, weight_hbm, bias_hbm, dw_hbm, log_hbm, dbias_hbm, gain_hbm,
    act_ref, part_ref, head_ref, pd_ref, sel_ref, taps_ref, dw_ref, rate_ref, vecs_ref,
    x_ref, log_ref, weight_ref, bias_ref, ps_ref, xs, xp, low, sems,
):
    rows, width = x_ref.shape
    steps = rows // CHUNKS
    rank = pd_ref.shape[1]
    maps = ps_ref.shape[0]
    halves = width // LANES
    pairs = (
        (x_hbm, x_ref), (weight_hbm, weight_ref), (bias_hbm, bias_ref), (ps_hbm, ps_ref), (pd_hbm, pd_ref),
        (log_hbm, log_ref), (dw_hbm, dw_ref), (dbias_hbm, vecs_ref.at[0:1]), (gain_hbm, vecs_ref.at[1:2]),
    )
    copies = [pltpu.make_async_copy(source, target, sems.at[i]) for i, (source, target) in enumerate(pairs)]
    for copy in copies:
        copy.start()
    copies[0].wait()
    head_ref[...] = x_ref[0:16, :].astype(F32)[0:8, :]
    for half in range(halves):
        cols = slice(half * LANES, (half + 1) * LANES)
        xs[half, 0:8, :] = jnp.zeros((8, LANES), F32)
        xs[half, 8 : 8 + rows, :] = x_ref[:, cols].astype(F32)
        for step in range(-(KWIDTH - 1), steps):
            to = (step + KWIDTH - 1) * CHUNKS
            xp[half, to : to + CHUNKS, :] = xs[half, pl.ds(8 + step, CHUNKS, stride=steps), :]
    copies[1].wait()
    copies[2].wait()
    taps_ref[0:KWIDTH, :] = weight_ref[...]
    taps_ref[KWIDTH : KWIDTH + 1, :] = bias_ref[...]
    block = min(rows, 64)
    for half in range(halves):
        cols = slice(half * LANES, (half + 1) * LANES)
        for start in range(0, rows, block):
            value = bias_ref[:, cols]
            for tap in range(KWIDTH):
                at = start + tap * CHUNKS
                value = value + weight_ref[tap : tap + 1, cols] * xp[half, at : at + block, :]
            value = silu(value)
            act_ref[start : start + block, cols] = value
            low[start : start + block, cols] = value.astype(BF16)
    copies[3].wait()
    sel_ref[...] = jnp.zeros_like(sel_ref)
    sel_ref[0:maps, :] = ps_ref[...]
    sel_ref[maps : 2 * maps, :] = ps_ref[...]
    copies[4].wait()
    put_products(low[...], pd_ref[...], sel_ref[...], maps, rank, part_ref, slice(0, rows))
    copies[5].wait()
    rate_ref[...] = -jnp.exp(log_ref[...]) * LOG2E
    for copy in copies[6:]:
        copy.wait()


def head_kernel(maps, halo_ref, head_ref, taps_ref, pd_ref, sel_ref, act_in, part_in, act_ref, part_ref, ext):
    rank = pd_ref.shape[1]
    ext[0:8, :] = halo_ref[...].astype(F32)[-8:, :]
    ext[8:16, :] = head_ref[...]
    value = taps_ref[KWIDTH : KWIDTH + 1, :]
    for tap in range(KWIDTH):
        at = 8 - (KWIDTH - 1) + tap
        value = value + taps_ref[tap : tap + 1, :] * ext[at : at + 8, :]
    value = silu(value)
    act_ref[...] = act_in[...]
    part_ref[...] = part_in[...]
    for token in range(KWIDTH - 1):
        act_ref[token * CHUNKS : token * CHUNKS + 1, :] = value[token : token + 1, :]
    low = act_ref[0:HEAD, :].astype(BF16)
    put_products(low, pd_ref[...], sel_ref[...], maps, rank, part_ref, slice(0, HEAD))


def total_kernel(rank, maps, parts_ref, out_ref):
    devices, rows, width = parts_ref.shape
    total = parts_ref[0].astype(F32)
    for source in range(1, devices):
        total = total + parts_ref[source].astype(F32)
    chosen = total[:, rank:]
    lane = lax.broadcasted_iota(jnp.int32, chosen.shape, 1)
    summed = chosen + pltpu.roll(chosen, LANES - maps, 1)
    twice = jnp.where(lane < maps, summed, pltpu.roll(summed, maps, 1))
    high = twice.astype(BF16).astype(F32)
    rest = jnp.where(lane < 2 * maps, twice - high, 0.0)
    mixed = jnp.where(lane < maps, high, rest)
    row = jnp.concatenate([total[:, :rank], mixed], axis=1).astype(BF16)
    for target in range(devices):
        out_ref[target] = row


def spread(first, maps):
    shape = (LANES, STATE * LANES)
    source = lax.broadcasted_iota(jnp.int32, shape, 0)
    group = lax.broadcasted_iota(jnp.int32, shape, 1) >> 7
    hit = (source == group + first) | (source == group + (first + maps))
    return jnp.where(hit, 1.0, 0.0).astype(BF16)


def step_rows(step):
    return pl.ds(pl.multiple_of(step * CHUNKS, CHUNKS), CHUNKS)


def ends_kernel(
    rank, me_ref, g_ref, act_ref, dw_ref, vecs_ref, rate,
    delta_hbm, inside_hbm, before_hbm, pay_hbm,
    delta, inside_ref, before_ref, pay_ref, drive, b_all, cum_ref, ends, sems,
):
    rows, width = act_ref.shape
    steps = rows // CHUNKS
    halves = width // LANES
    z = jnp.dot(g_ref[:, :rank], dw_ref[...], preferred_element_type=F32) + vecs_ref[0:1, :]
    step_size = jnp.maximum(z, 0.0) + jnp.log1p(jnp.exp(-jnp.abs(z)))
    delta[...] = step_size
    pairs = ((delta, delta_hbm), (inside_ref, inside_hbm), (before_ref, before_hbm), (pay_ref, pay_hbm))
    copies = [pltpu.make_async_copy(source, target, sems.at[i]) for i, (source, target) in enumerate(pairs)]
    copies[0].start()
    drive[...] = step_size * act_ref[...]
    b_all[...] = jnp.dot(g_ref[:, rank:], spread(0, 2 * STATE), preferred_element_type=F32)
    chunk = lax.broadcasted_iota(jnp.int32, (CHUNKS, LANES), 0)
    zero = jnp.zeros((CHUNKS, LANES), F32)

    def add(step, totals):
        at = step_rows(step)
        totals = [totals[half] + delta[at, half * LANES : (half + 1) * LANES] for half in range(halves)]
        for half in range(halves):
            cum_ref[at, half * LANES : (half + 1) * LANES] = totals[half]
        return totals

    totals = lax.fori_loop(0, steps, add, [zero] * halves, unroll=8)
    for half in range(halves):
        cols = slice(half * LANES, (half + 1) * LANES)
        rates = [jnp.broadcast_to(rate[n : n + 1, cols], (CHUNKS, LANES)) for n in range(STATE)]
        total = totals[half]

        def gather(step, states, cols=cols, rates=rates, total=total):
            at = step_rows(step)
            left = total - cum_ref[at, cols]
            push = drive[at, cols]
            return [
                states[n] + jnp.exp2(left * rates[n]) * (push * b_all[at, n * LANES : (n + 1) * LANES])
                for n in range(STATE)
            ]

        states = lax.fori_loop(0, steps, gather, [zero] * STATE, unroll=8)
        sums = [total]
        shift = 1
        while shift < CHUNKS:
            sums.append(sums[-1] + jnp.where(chunk >= shift, pltpu.roll(sums[-1], shift, 0), 0.0))
            shift *= 2
        for n in range(STATE):
            end = states[n]
            shift = 1
            for level in range(len(sums) - 1):
                end = end + jnp.exp2(rates[n] * sums[level]) * jnp.where(
                    chunk >= shift, pltpu.roll(end, shift, 0), 0.0
                )
                shift *= 2
            inside_ref[n, :, cols] = jnp.where(chunk >= 1, pltpu.roll(end, 1, 0), 0.0)
            ends[n : n + 1, cols] = end[CHUNKS - 1 :, :]
        before_ref[:, cols] = jnp.where(chunk >= 1, pltpu.roll(sums[-1], 1, 0), 0.0)
        ends[STATE : STATE + 1, cols] = sums[-1][CHUNKS - 1 :, :]

    copies[1].start()
    copies[2].start()
    me = me_ref[0]
    value = ends[0:STATE, :]
    total = jnp.broadcast_to(ends[STATE : STATE + 1, :], value.shape)
    high = total.astype(BF16).astype(F32)
    first = lax.broadcasted_iota(jnp.int32, value.shape, 0) == 0
    tail = jnp.where(first, high, total - high)
    for target in range(pay_ref.shape[0]):
        use = target > me
        pay_ref[target, 0:16, :] = jnp.where(use, value, 0.0).astype(BF16)
        pay_ref[target, 16:32, :] = jnp.where(use, tail, 0.0).astype(BF16)
    copies[3].start()
    for copy in copies:
        copy.wait()


def local_kernel(
    rank, g_ref, act_ref, rate, vecs_ref, delta_hbm, inside_hbm, before_hbm, gate_hbm,
    y_ref, cum_ref, lit_ref, spread_ref, maps_ref,
    b_all, c_all, delta, inside_ref, before_ref, gate_ref, sems,
):
    rows, width = act_ref.shape
    steps = rows // CHUNKS
    halves = width // LANES
    pairs = ((delta_hbm, delta), (inside_hbm, inside_ref), (before_hbm, before_ref), (gate_hbm, gate_ref))
    copies = [pltpu.make_async_copy(source, target, sems.at[i]) for i, (source, target) in enumerate(pairs)]
    for copy in copies:
        copy.start()
    b_all[...] = jnp.dot(g_ref[:, rank:], spread(0, 2 * STATE), preferred_element_type=F32)
    spread_ref[...] = spread(STATE, 2 * STATE)
    maps_ref[...] = g_ref[:, rank:]
    c_all[...] = jnp.dot(maps_ref[...], spread_ref[...], preferred_element_type=F32)
    for copy in copies:
        copy.wait()
    for half in range(halves):
        cols = slice(half * LANES, (half + 1) * LANES)
        rates = [jnp.broadcast_to(rate[n : n + 1, cols], (CHUNKS, LANES)) for n in range(STATE)]
        gain = vecs_ref[1:2, cols]

        def advance(step, carried, cols=cols, rates=rates, gain=gain):
            states, total = carried
            at = step_rows(step)
            size = delta[at, cols]
            value = act_ref[at, cols]
            push = size * value
            total = total + size
            out = gain * value
            later = []
            for n in range(STATE):
                group = slice(n * LANES, (n + 1) * LANES)
                now = jnp.exp2(size * rates[n]) * states[n] + push * b_all[at, group]
                out = out + c_all[at, group] * now
                later.append(now)
            y_ref[at, cols] = out
            cum_ref[at, cols] = total
            return later, total

        lax.fori_loop(
            0, steps, advance, ([inside_ref[n, :, cols] for n in range(STATE)], before_ref[:, cols]), unroll=4
        )
    lit_ref[...] = silu(gate_ref[...].astype(F32))


def finish_kernel(got_ref, maps_ref, spread_ref, y_ref, cum_ref, rate, lit_ref, out_ref, c_all, carry, ys):
    rows, width = y_ref.shape
    steps = rows // CHUNKS
    halves = width // LANES
    c_all[...] = jnp.dot(maps_ref[...], spread_ref[...], preferred_element_type=F32)
    incoming = jnp.zeros((STATE, width), F32)
    for source in range(got_ref.shape[0] - 1):
        tail = got_ref[source, 16:32, :].astype(F32)
        decay = jnp.exp2(rate[...] * (tail[0:1, :] + tail[1:2, :]))
        incoming = decay * incoming + got_ref[source, 0:16, :].astype(F32)
    carry[...] = incoming
    for half in range(halves):
        cols = slice(half * LANES, (half + 1) * LANES)
        rates = [jnp.broadcast_to(rate[n : n + 1, cols], (CHUNKS, LANES)) for n in range(STATE)]
        entering = [jnp.broadcast_to(carry[n : n + 1, cols], (CHUNKS, LANES)) for n in range(STATE)]

        def correct(step, _, half=half, cols=cols, rates=rates, entering=entering):
            at = step_rows(step)
            total = cum_ref[at, cols]
            out = y_ref[at, cols]
            for n in range(STATE):
                group = slice(n * LANES, (n + 1) * LANES)
                out = out + (c_all[at, group] * entering[n]) * jnp.exp2(total * rates[n])
            ys[half, pl.ds(step, CHUNKS, stride=steps), :] = out
            return 0

        lax.fori_loop(0, steps, correct, 0, unroll=8)
        out_ref[:, cols] = (ys[half] * lit_ref[:, cols]).astype(BF16)


def on_device(
    mamba_in, mamba_gate, conv_weight, conv_bias, proj_delta, proj_select, delta_weight, delta_bias, decay_log, skip_gain,
):
    rows, width = mamba_in.shape
    rank = proj_delta.shape[1]
    maps = proj_select.shape[1]
    halves = width // LANES
    steps = rows // CHUNKS
    n_ctx, n_ch = lax.axis_size("ctx"), lax.axis_size("ch")
    wide = rank + LANES
    me = lax.axis_index("ctx").astype(jnp.int32).reshape(1)
    cells = rows * width * STATE
    tile = jax.ShapeDtypeStruct((rows, width), F32)
    part_shape = jax.ShapeDtypeStruct((rows, wide), BF16)
    big = pltpu.VMEM((rows, STATE * LANES), F32)

    halo = lax.ppermute(mamba_in[rows - 16 :], "ctx", [(i, i + 1) for i in range(n_ctx - 1)])
    act, part, head, pd, sel, taps, dw, rate, vecs = pl.pallas_call(
        project_kernel,
        out_shape=(
            tile,
            part_shape,
            jax.ShapeDtypeStruct((8, width), F32),
            jax.ShapeDtypeStruct(proj_delta.shape, BF16),
            jax.ShapeDtypeStruct((LANES, width), BF16),
            jax.ShapeDtypeStruct((8, width), F32),
            jax.ShapeDtypeStruct(delta_weight.shape, BF16),
            jax.ShapeDtypeStruct((STATE, width), F32),
            jax.ShapeDtypeStruct((8, width), F32),
        ),
        in_specs=hbm(9),
        out_specs=tuple(vmem(9)),
        scratch_shapes=[
            pltpu.VMEM((rows, width), BF16),
            pltpu.VMEM((STATE, width), F32),
            pltpu.VMEM((KWIDTH, width), F32),
            pltpu.VMEM((1, width), F32),
            pltpu.VMEM((maps, width), BF16),
            pltpu.VMEM((halves, rows + 8, LANES), F32),
            pltpu.VMEM((halves, (steps + KWIDTH - 1) * CHUNKS, LANES), F32),
            pltpu.VMEM((rows, width), BF16),
            pltpu.SemaphoreType.DMA((9,)),
        ],
        compiler_params=pltpu.CompilerParams(vmem_limit_bytes=16 * MIB),
        cost_estimate=pl.CostEstimate(
            flops=2 * rows * width * wide, bytes_accessed=2 * rows * width * 8, transcendentals=rows * width
        ),
        name="project",
    )(
        *stay(
            mamba_in, proj_delta, proj_select.T, conv_weight, conv_bias[None, :],
            delta_weight, decay_log, delta_bias[None, :], skip_gain[None, :],
        )
    )
    act, part = pl.pallas_call(
        functools.partial(head_kernel, maps),
        out_shape=(tile, part_shape),
        in_specs=vmem(7),
        out_specs=tuple(vmem(2)),
        scratch_shapes=[pltpu.VMEM((16, width), F32)],
        compiler_params=pltpu.CompilerParams(vmem_limit_bytes=16 * MIB),
        name="first_rows",
    )(halo, head, taps, pd, sel, act, part)

    parts = lax.all_to_all(part.reshape(n_ch, rows // n_ch, wide), "ch", 0, 0)
    totals = pl.pallas_call(
        functools.partial(total_kernel, rank, maps),
        out_shape=jax.ShapeDtypeStruct(parts.shape, BF16),
        in_specs=vmem(1),
        out_specs=vmem(1)[0],
        compiler_params=pltpu.CompilerParams(vmem_limit_bytes=16 * MIB),
        name="total",
    )(parts)
    gathered = lax.all_to_all(totals, "ch", 0, 0).reshape(rows, wide)

    sent = (
        ((rows, width), F32),
        ((STATE, CHUNKS, width), F32),
        ((CHUNKS, width), F32),
        ((n_ctx, 2 * STATE, width), BF16),
    )
    delta, inside, before, pay = pl.pallas_call(
        functools.partial(ends_kernel, rank),
        out_shape=tuple(pltpu.HBM(*kept) for kept in sent),
        in_specs=[pl.BlockSpec(memory_space=pltpu.SMEM)] + vmem(5),
        out_specs=tuple(hbm(4)),
        scratch_shapes=[
            *(pltpu.VMEM(*kept) for kept in sent),
            pltpu.VMEM((rows, width), F32),
            big,
            pltpu.VMEM((rows, width), F32),
            pltpu.VMEM((STATE + 8, width), F32),
            pltpu.SemaphoreType.DMA((4,)),
        ],
        compiler_params=pltpu.CompilerParams(vmem_limit_bytes=16 * MIB),
        name="ends",
    )(me, gathered, act, dw, vecs, rate)

    got = lax.all_to_all(pay, "ctx", 0, 0)
    y_local, cum, lit, spread_c, maps_all = pl.pallas_call(
        functools.partial(local_kernel, rank),
        out_shape=(
            tile,
            tile,
            tile,
            jax.ShapeDtypeStruct((LANES, STATE * LANES), BF16),
            jax.ShapeDtypeStruct((rows, LANES), BF16),
        ),
        in_specs=vmem(4) + hbm(4),
        out_specs=tuple(vmem(5)),
        scratch_shapes=[
            big,
            big,
            *(pltpu.VMEM(*kept) for kept in sent[:3]),
            pltpu.VMEM((rows, width), BF16),
            pltpu.SemaphoreType.DMA((4,)),
        ],
        compiler_params=pltpu.CompilerParams(vmem_limit_bytes=24 * MIB),
        cost_estimate=pl.CostEstimate(flops=6 * cells, bytes_accessed=8 * rows * width * 4, transcendentals=cells),
        name="local_scan",
    )(gathered, act, rate, vecs, *stay(delta, inside, before, mamba_gate))
    return pl.pallas_call(
        finish_kernel,
        out_shape=jax.ShapeDtypeStruct((rows, width), BF16),
        in_specs=vmem(7),
        out_specs=vmem(1)[0],
        scratch_shapes=[
            big,
            pltpu.VMEM((STATE, width), F32),
            pltpu.VMEM((halves, rows, LANES), F32),
        ],
        compiler_params=pltpu.CompilerParams(vmem_limit_bytes=16 * MIB),
        name="finish",
    )(got, maps_all, spread_c, y_local, cum, rate, lit)


def solution(mesh):
    return jax.shard_map(
        on_device,
        mesh=mesh,
        in_specs=(
            P("ctx", "ch"),
            P("ctx", "ch"),
            P(None, "ch"),
            P("ch"),
            P("ch", None),
            P("ch", None),
            P(None, "ch"),
            P("ch"),
            P(None, "ch"),
            P("ch"),
        ),
        out_specs=P("ctx", "ch"),
        check_vma=False,
    )
```

time: 107 us -> 99.3 us (0.928)
  blocking collectives: 51.1 us -> 40.6 us
  starting transfers between devices: 11.5 us -> 16.7 us
  local copies, waits for them, and re-layouts: 4.11 us -> 1.4 us
  Pallas kernels: 12.8 us -> 14.9 us
  waiting for transfers between devices: 26.5 us -> 25.1 us
    all_to_all x1 -> x0, blocking collectives: 12.1 us -> none  [on_device(): got = lax.all_to_all(pay, 'ctx', 0, 0)]
    all_to_all x0 -> x1, starting transfers between devices: none -> 5.7 us  [on_device(): got = lax.all_to_all(pay, 'ctx', 0, 0)]
    unnamed x21 -> x4, local copies, waits for them, and re-layouts: 3.4 us -> 0.7 us
    pallas_call x3 -> x5, Pallas kernels: 11.7 us -> 13.8 us  [the longest x1 4.91 us: on_device(): pl.pallas_call(functools.partial(local_kernel, rank), out_shape=(tile, ti...]
    ppermute x1, waiting for transfers between devices: 3.27 us -> 1.35 us  [on_device(): lax.ppermute(mamba_in[rows - 16:], 'ctx', [(i, i + 1) for i in range(n_ct...]
    all_to_all x1, blocking collectives: 39 us -> 40.6 us  [on_device(): parts = lax.all_to_all(part.reshape(n_ch, rows // n_ch, wide), 'ch', 0, 0)]
  transfers between devices with their start and end apart: 2 -> 3, of which waited for: 2 -> 3; matrix products, arithmetic and copies ran while one was open for 0% -> 0% of each run, Pallas kernels for 0% -> 7%
where the time goes in v2:
time: 99.3 us; the launch traced here: 98.8 us
  blocking collectives  40.6 us (41%)
  waiting for transfers between devices  25.1 us (25%)
  starting transfers between devices  16.7 us (17%)
  Pallas kernels  14.9 us (15%)
  local copies, waits for them, and re-layouts  1.4 us (1%)
    all_to_all x1, blocking collectives, on_device(): parts = lax.all_to_all(part.reshape(n_ch, rows // n_ch, wide), 'ch', 0, 0)  40.6 us
    all_to_all x1, waiting for transfers between devices, on_device(): gathered = lax.all_to_all(totals, 'ch', 0, 0).reshape(rows, wide)  23.6 us
    all_to_all x1, starting transfers between devices, on_device(): got = lax.all_to_all(pay, 'ctx', 0, 0)  5.7 us
    all_to_all x1, starting transfers between devices, on_device(): gathered = lax.all_to_all(totals, 'ch', 0, 0).reshape(rows, wide)  5.59 us
    ppermute x1, starting transfers between devices, on_device(): lax.ppermute(mamba_in[rows - 16:], 'ctx', [(i, i + 1) for i in range(n_ct...  5.38 us
    pallas_call x1, Pallas kernels, on_device(): pl.pallas_call(functools.partial(local_kernel, rank), out_shape=(tile, ti...  4.91 us
    pallas_call x1, Pallas kernels, on_device(): pl.pallas_call(functools.partial(ends_kernel, rank), out_shape=tuple((plt...  3.53 us
    pallas_call x1, Pallas kernels, on_device(): pl.pallas_call(finish_kernel, out_shape=jax.ShapeDtypeStruct((rows, width...  3.1 us
  transfers between devices with their start and end apart: 3, of which 3 were waited for; matrix products, arithmetic and copies ran while one was open for 0% of the time, Pallas kernels for 7%

profile of v2, /device:TPU:1, one launch (start us, length us, event | category | flops | bytes accessed | tf_op | source)
XLA Modules:
  0.0 98.8 jit_solution(9293686448762909453)
XLA Ops:
  0.0 0.7 slice.3
  0.7 5.4 %collective-permute-start = (bf16[16,256]{1,0:T(8,128)(2,1)S(1)}, bf16[16,256]{1,0:T(8,128)(2,1)S(1)}, u32[]{:S(2)}, u32[]{:S(2)}) collective-permute-start(bf16[16,256]{1,0:T(8,128)(2,1)S(1)} %slice.3), channel_id=1, source_target_pairs={{0,64},{64,128},{128,192},{192,256},{256,320},{320,384},{384,448},... | collective-permute-start | bytes 24584 | tf_op jit(solution)/shard_map/ppermute | solution.py:315
  6.1 2.1 %project.1 = (f32[512,256]{1,0:T(8,128)S(1)}, bf16[512,640]{1,0:T(8,128)(2,1)S(1)}, f32[8,256]{1,0:T(8,128)S(1)}, bf16[256,512]{1,0:T(8,128)(2,1)S(1)}, bf16[128...) custom-call(bf16[512,256]{1,0:T(8,128)(2,1)} %x_hbm.1, ...), custom_call_target="tpu_custom_call" | custom-call | flops 167772160 | bytes 2097152 | tf_op jit(solution)/shard_map/project/pallas_call | solution.py:316
  8.1 0.0 copy-start
  8.2 1.4 %collective-permute-done.halo_ref = bf16[16,256]{1,0:T(8,128)(2,1)S(1)} collective-permute-done((bf16[16,256]{1,0:T(8,128)(2,1)S(1)}, bf16[16,256]{1,0:T(8,128)(2,1)S(1)}, u32[]{:S(2)}, u32[]{:S(2)}) %collective-permute-start) | collective-permute-done | bytes 8224 | tf_op jit(solution)/shard_map/ppermute | solution.py:315
  9.5 0.2 first_rows.1
  9.7 40.6 %all_to_all.15.parts_ref = bf16[64,8,640]{2,1,0:T(8,128)(2,1)S(1)} all-to-all(bf16[64,8,640]{2,1,0:T(8,128)(2,1)S(1)} %bitcast.9), channel_id=1, replica_groups=mesh['ctx'=8,'ch'=64] {'ch'}, dimensions={0} | all-to-all | bytes 1310720 | tf_op jit(solution)/shard_map/all_to_all | solution.py:363
  50.4 1.1 %total.1 = bf16[64,8,640]{2,1,0:T(8,128)(2,1)} custom-call(bf16[64,8,640]{2,1,0:T(8,128)(2,1)S(1)} %all_to_all.15.parts_ref), custom_call_target="tpu_custom_call" | custom-call | tf_op jit(solution)/shard_map/total/pallas_call | solution.py:364
  51.4 5.6 %all-to-all-start.1 = ((bf16[64,8,640]{2,1,0:T(8,128)(2,1)}), bf16[64,8,640]{2,1,0:T(8,128)(2,1)S(1)}, u32[]{:S(2)}, u32[]{:S(2)}) async-start(bf16[64,8,640]{2,1,0:T(8,128)(2,1)} %total.1), calls=%async_computation.1 | async-start | bytes 1310720 | tf_op jit(solution)/shard_map/all_to_all | solution.py:372
  57.0 23.6 %all-to-all-done.1 = bf16[64,8,640]{2,1,0:T(8,128)(2,1)S(1)} async-done(((bf16[64,8,640]{2,1,0:T(8,128)(2,1)}), bf16[64,8,640]{2,1,0:T(8,128)(2,1)S(1)}, u32[]{:S(2)}, u32[]{:S(2)}) %all-to-all-start.1) | async-done | bytes 655392 | tf_op jit(solution)/shard_map/all_to_all | solution.py:372
  80.6 0.0 copy-done
  80.6 3.5 %ends.1 = (f32[512,256]{1,0:T(8,128)}, f32[16,8,256]{2,1,0:T(8,128)}, f32[8,256]{1,0:T(8,128)}, bf16[8,32,256]{2,1,0:T(8,128)(2,1)}) custom-call(s32[1]{0:T(128)} %bitcast.me_ref, bf16[512,640]{1,0:T(8,128)(2,1)S(1)} %bitcast.7, f32[512,256]{1,0:T(8,128)S(1)} %get-tuple-element.32.act_ref, bf16[512,256]{1,0:T(8,128)(2,1)S(1)} %get-tuple-element.33.dw_ref, ...), custom_call_target="tpu_custom_call" | custom-call | tf_op jit(solution)/shard_map/ends/pallas_call | solution.py:380
  84.2 5.7 %all-to-all-start.2 = ((bf16[8,32,256]{2,1,0:T(8,128)(2,1)}), bf16[8,32,256]{2,1,0:T(8,128)(2,1)S(1)}, u32[]{:S(2)}, u32[]{:S(2)}) async-start(bf16[8,32,256]{2,1,0:T(8,128)(2,1)} %get-tuple-element.36), calls=%async_computation.2 | async-start | bytes 262144 | tf_op jit(solution)/shard_map/all_to_all | solution.py:397
  89.9 0.0 copy-start.1
  89.9 0.7 copy-done.1
  90.6 4.9 %local_scan.1 = (f32[512,256]{1,0:T(8,128)S(1)}, f32[512,256]{1,0:T(8,128)S(1)}, f32[512,256]{1,0:T(8,128)S(1)}, bf16[128,2048]{1,0:T(8,128)(2,1)S(1)}, bf16[512,128]{1,0:T(8,128)(2,1)S(1)}) custom-call(bf16[512,640]{1,0:T(8,128)(2,1)S(1)} %bitcast.8, f32[512,256]{1,0:T(8,128)S(1)} %get-tuple-element.32.act_ref, f32[16,256]{1,0:T(8,128)S(1)} %get-tuple-element.35.rate, ...), custom_call_target="tpu_custom_call" | custom-call | flops 12582912 | bytes 4194304 | tf_op jit(solution)/shard_map/local_scan/pallas_call | solution.py:398
  95.5 0.2 all-to-all-done.2.got_ref
  95.7 3.1 %finish.1 = bf16[512,256]{1,0:T(8,128)(2,1)} custom-call(bf16[8,32,256]{2,1,0:T(8,128)(2,1)S(1)} %all-to-all-done.2.got_ref, bf16[512,128]{1,0:T(8,128)(2,1)S(1)} %get-tuple-element.40.maps_ref, bf16[128,2048]{1,0:T(8,128)(2,1)S(1)} %get-tuple-element.41.spread_ref, f32[512,256]{1,0:T(8,128)S(1)} %get-tuple-element.42.y_ref, ...), custom_call_target="tpu_custom_call" | custom-call | tf_op jit(solution)/shard_map/finish/pallas_call | solution.py:420
Async XLA Ops:
  0.7 8.8 %collective-permute-start = (bf16[16,256]{1,0:T(8,128)(2,1)S(1)}, bf16[16,256]{1,0:T(8,128)(2,1)S(1)}, u32[]{:S(2)}, u32[]{:S(2)}) collective-permute-start(bf16[16,256]{1,0:T(8,128)(2,1)S(1)} %slice.3), channel_id=1, source_target_pairs={{0,64},{64,128},{128,192},{192,256},{256,320},{320,384},{384,448},... | collective-permute-start | bytes 24584 | tf_op jit(solution)/shard_map/ppermute | solution.py:315
  8.1 72.5 %copy-start = (f32[8,256]{1,0:T(8,128)}, f32[8,256]{1,0:T(8,128)S(1)}, u32[]{:S(2)}) copy-start(f32[8,256]{1,0:T(8,128)S(1)} %get-tuple-element.34.vecs_ref) | copy-start | bytes 24580
  51.4 29.2 %all-to-all-start.1 = ((bf16[64,8,640]{2,1,0:T(8,128)(2,1)}), bf16[64,8,640]{2,1,0:T(8,128)(2,1)S(1)}, u32[]{:S(2)}, u32[]{:S(2)}) async-start(bf16[64,8,640]{2,1,0:T(8,128)(2,1)} %total.1), calls=%async_computation.1 | async-start | bytes 1310720 | tf_op jit(solution)/shard_map/all_to_all | solution.py:372
  84.2 11.5 %all-to-all-start.2 = ((bf16[8,32,256]{2,1,0:T(8,128)(2,1)}), bf16[8,32,256]{2,1,0:T(8,128)(2,1)S(1)}, u32[]{:S(2)}, u32[]{:S(2)}) async-start(bf16[8,32,256]{2,1,0:T(8,128)(2,1)} %get-tuple-element.36), calls=%async_computation.2 | async-start | bytes 262144 | tf_op jit(solution)/shard_map/all_to_all | solution.py:397
  89.9 0.7 copy-start.1

commit v3 on v2

--- a/solution.py
+++ b/solution.py
@@ -130,12 +130,12 @@
         out_ref[target] = row
 
 
-def spread(first, maps):
-    shape = (LANES, STATE * LANES)
-    source = lax.broadcasted_iota(jnp.int32, shape, 0)
-    group = lax.broadcasted_iota(jnp.int32, shape, 1) >> 7
-    hit = (source == group + first) | (source == group + (first + maps))
-    return jnp.where(hit, 1.0, 0.0).astype(BF16)
+def ready_kernel(gate_ref, lit_ref, spread_ref):
+    lit_ref[...] = silu(gate_ref[...].astype(F32))
+    source = lax.broadcasted_iota(jnp.int32, spread_ref.shape, 0)
+    group = lax.broadcasted_iota(jnp.int32, spread_ref.shape, 1) >> 7
+    hit = (source == group) | (source == group + 2 * STATE)
+    spread_ref[...] = jnp.where(hit, 1.0, 0.0).astype(BF16)
 
 
 def step_rows(step):
@@ -143,7 +143,7 @@
 
 
 def ends_kernel(
-    rank, me_ref, g_ref, act_ref, dw_ref, vecs_ref, rate,
+    rank, me_ref, g_ref, act_ref, dw_ref, vecs_ref, rate, spread_ref,
     delta_hbm, inside_hbm, before_hbm, pay_hbm,
     delta, inside_ref, before_ref, pay_ref, drive, b_all, cum_ref, ends, sems,
 ):
@@ -157,7 +157,7 @@
     copies = [pltpu.make_async_copy(source, target, sems.at[i]) for i, (source, target) in enumerate(pairs)]
     copies[0].start()
     drive[...] = step_size * act_ref[...]
-    b_all[...] = jnp.dot(g_ref[:, rank:], spread(0, 2 * STATE), preferred_element_type=F32)
+    b_all[...] = jnp.dot(g_ref[:, rank:], spread_ref[...], preferred_element_type=F32)
     chunk = lax.broadcasted_iota(jnp.int32, (CHUNKS, LANES), 0)
     zero = jnp.zeros((CHUNKS, LANES), F32)
 
@@ -219,36 +219,45 @@
         copy.wait()
 
 
-def local_kernel(
-    rank, g_ref, act_ref, rate, vecs_ref, delta_hbm, inside_hbm, before_hbm, gate_hbm,
-    y_ref, cum_ref, lit_ref, spread_ref, maps_ref,
-    b_all, c_all, delta, inside_ref, before_ref, gate_ref, sems,
+def finish_kernel(
+    rank, got_ref, g_ref, act_ref, rate, vecs_ref, lit_ref, spread_ref, delta_hbm, inside_hbm, before_hbm,
+    out_hbm,
+    delta, inside_ref, before_ref, b_all, c_all, carry, ys, out_ref, sems,
 ):
     rows, width = act_ref.shape
     steps = rows // CHUNKS
     halves = width // LANES
-    pairs = ((delta_hbm, delta), (inside_hbm, inside_ref), (before_hbm, before_ref), (gate_hbm, gate_ref))
+    pairs = ((delta_hbm, delta), (inside_hbm, inside_ref), (before_hbm, before_ref))
     copies = [pltpu.make_async_copy(source, target, sems.at[i]) for i, (source, target) in enumerate(pairs)]
     for copy in copies:
         copy.start()
-    b_all[...] = jnp.dot(g_ref[:, rank:], spread(0, 2 * STATE), preferred_element_type=F32)
-    spread_ref[...] = spread(STATE, 2 * STATE)
-    maps_ref[...] = g_ref[:, rank:]
-    c_all[...] = jnp.dot(maps_ref[...], spread_ref[...], preferred_element_type=F32)
+    maps = g_ref[:, rank:]
+    b_all[...] = jnp.dot(maps, spread_ref[...], preferred_element_type=F32)
+    maps = pltpu.roll(maps.astype(F32), LANES - STATE, 1).astype(BF16)
+    c_all[...] = jnp.dot(maps, spread_ref[...], preferred_element_type=F32)
+    incoming = jnp.zeros((STATE, width), F32)
+    for source in range(got_ref.shape[0] - 1):
+        tail = got_ref[source, 16:32, :].astype(F32)
+        decay = jnp.exp2(rate[...] * (tail[0:1, :] + tail[1:2, :]))
+        incoming = decay * incoming + got_ref[source, 0:16, :].astype(F32)
+    carry[...] = incoming
     for copy in copies:
         copy.wait()
+    leaving = []
     for half in range(halves):
         cols = slice(half * LANES, (half + 1) * LANES)
         rates = [jnp.broadcast_to(rate[n : n + 1, cols], (CHUNKS, LANES)) for n in range(STATE)]
         gain = vecs_ref[1:2, cols]
-
-        def advance(step, carried, cols=cols, rates=rates, gain=gain):
-            states, total = carried
+        before = before_ref[:, cols]
+        entering = [
+            inside_ref[n, :, cols] + jnp.exp2(rates[n] * before) * carry[n : n + 1, cols] for n in range(STATE)
+        ]
+
+        def advance(step, states, half=half, cols=cols, rates=rates, gain=gain):
             at = step_rows(step)
             size = delta[at, cols]
             value = act_ref[at, cols]
             push = size * value
-            total = total + size
             out = gain * value
             later = []
             for n in range(STATE):
@@ -256,44 +265,16 @@
                 now = jnp.exp2(size * rates[n]) * states[n] + push * b_all[at, group]
                 out = out + c_all[at, group] * now
                 later.append(now)
-            y_ref[at, cols] = out
-            cum_ref[at, cols] = total
-            return later, total
-
-        lax.fori_loop(
-            0, steps, advance, ([inside_ref[n, :, cols] for n in range(STATE)], before_ref[:, cols]), unroll=4
-        )
-    lit_ref[...] = silu(gate_ref[...].astype(F32))
-
-
-def finish_kernel(got_ref, maps_ref, spread_ref, y_ref, cum_ref, rate, lit_ref, out_ref, c_all, carry, ys):
-    rows, width = y_ref.shape
-    steps = rows // CHUNKS
-    halves = width // LANES
-    c_all[...] = jnp.dot(maps_ref[...], spread_ref[...], preferred_element_type=F32)
-    incoming = jnp.zeros((STATE, width), F32)
-    for source in range(got_ref.shape[0] - 1):
-        tail = got_ref[source, 16:32, :].astype(F32)
-        decay = jnp.exp2(rate[...] * (tail[0:1, :] + tail[1:2, :]))
-        incoming = decay * incoming + got_ref[source, 0:16, :].astype(F32)
-    carry[...] = incoming
-    for half in range(halves):
-        cols = slice(half * LANES, (half + 1) * LANES)
-        rates = [jnp.broadcast_to(rate[n : n + 1, cols], (CHUNKS, LANES)) for n in range(STATE)]
-        entering = [jnp.broadcast_to(carry[n : n + 1, cols], (CHUNKS, LANES)) for n in range(STATE)]
-
-        def correct(step, _, half=half, cols=cols, rates=rates, entering=entering):
-            at = step_rows(step)
-            total = cum_ref[at, cols]
-            out = y_ref[at, cols]
-            for n in range(STATE):
-                group = slice(n * LANES, (n + 1) * LANES)
-                out = out + (c_all[at, group] * entering[n]) * jnp.exp2(total * rates[n])
             ys[half, pl.ds(step, CHUNKS, stride=steps), :] = out
-            return 0
-
-        lax.fori_loop(0, steps, correct, 0, unroll=8)
-        out_ref[:, cols] = (ys[half] * lit_ref[:, cols]).astype(BF16)
+            return later
+
+        lax.fori_loop(0, steps, advance, entering, unroll=8)
+        out_ref[half] = (ys[half] * lit_ref[:, cols]).astype(BF16)
+        copy = pltpu.make_async_copy(out_ref.at[half], out_hbm.at[:, cols], sems.at[len(pairs) + half])
+        copy.start()
+        leaving.append(copy)
+    for copy in leaving:
+        copy.wait()
 
 
 def on_device(
@@ -307,7 +288,6 @@
     n_ctx, n_ch = lax.axis_size("ctx"), lax.axis_size("ch")
     wide = rank + LANES
     me = lax.axis_index("ctx").astype(jnp.int32).reshape(1)
-    cells = rows * width * STATE
     tile = jax.ShapeDtypeStruct((rows, width), F32)
     part_shape = jax.ShapeDtypeStruct((rows, wide), BF16)
     big = pltpu.VMEM((rows, STATE * LANES), F32)
@@ -360,6 +340,17 @@
         name="first_rows",
     )(halo, head, taps, pd, sel, act, part)
 
+    lit, spread = pl.pallas_call(
+        ready_kernel,
+        out_shape=(tile, jax.ShapeDtypeStruct((LANES, STATE * LANES), BF16)),
+        in_specs=vmem(1),
+        out_specs=tuple(vmem(2)),
+        compiler_params=pltpu.CompilerParams(vmem_limit_bytes=16 * MIB),
+        cost_estimate=pl.CostEstimate(
+            flops=16 * rows * width, bytes_accessed=8 * rows * width, transcendentals=rows * width
+        ),
+        name="ready",
+    )(mamba_gate)
     parts = lax.all_to_all(part.reshape(n_ch, rows // n_ch, wide), "ch", 0, 0)
     totals = pl.pallas_call(
         functools.partial(total_kernel, rank, maps),
@@ -380,7 +371,7 @@
     delta, inside, before, pay = pl.pallas_call(
         functools.partial(ends_kernel, rank),
         out_shape=tuple(pltpu.HBM(*kept) for kept in sent),
-        in_specs=[pl.BlockSpec(memory_space=pltpu.SMEM)] + vmem(5),
+        in_specs=[pl.BlockSpec(memory_space=pltpu.SMEM)] + vmem(6),
         out_specs=tuple(hbm(4)),
         scratch_shapes=[
             *(pltpu.VMEM(*kept) for kept in sent),
@@ -392,44 +383,26 @@
         ],
         compiler_params=pltpu.CompilerParams(vmem_limit_bytes=16 * MIB),
         name="ends",
-    )(me, gathered, act, dw, vecs, rate)
+    )(me, gathered, act, dw, vecs, rate, spread)
 
     got = lax.all_to_all(pay, "ctx", 0, 0)
-    y_local, cum, lit, spread_c, maps_all = pl.pallas_call(
-        functools.partial(local_kernel, rank),
-        out_shape=(
-            tile,
-            tile,
-            tile,
-            jax.ShapeDtypeStruct((LANES, STATE * LANES), BF16),
-            jax.ShapeDtypeStruct((rows, LANES), BF16),
-        ),
-        in_specs=vmem(4) + hbm(4),
-        out_specs=tuple(vmem(5)),
+    return pl.pallas_call(
+        functools.partial(finish_kernel, rank),
+        out_shape=jax.ShapeDtypeStruct((rows, width), BF16),
+        in_specs=vmem(7) + hbm(3),
+        out_specs=hbm(1)[0],
         scratch_shapes=[
+            *(pltpu.VMEM(*kept) for kept in sent[:3]),
             big,
-            big,
-            *(pltpu.VMEM(*kept) for kept in sent[:3]),
-            pltpu.VMEM((rows, width), BF16),
-            pltpu.SemaphoreType.DMA((4,)),
-        ],
-        compiler_params=pltpu.CompilerParams(vmem_limit_bytes=24 * MIB),
-        cost_estimate=pl.CostEstimate(flops=6 * cells, bytes_accessed=8 * rows * width * 4, transcendentals=cells),
-        name="local_scan",
-    )(gathered, act, rate, vecs, *stay(delta, inside, before, mamba_gate))
-    return pl.pallas_call(
-        finish_kernel,
-        out_shape=jax.ShapeDtypeStruct((rows, width), BF16),
-        in_specs=vmem(7),
-        out_specs=vmem(1)[0],
-        scratch_shapes=[
             big,
             pltpu.VMEM((STATE, width), F32),
             pltpu.VMEM((halves, rows, LANES), F32),
+            pltpu.VMEM((halves, rows, LANES), BF16),
+            pltpu.SemaphoreType.DMA((3 + halves,)),
         ],
-        compiler_params=pltpu.CompilerParams(vmem_limit_bytes=16 * MIB),
+        compiler_params=pltpu.CompilerParams(vmem_limit_bytes=24 * MIB),
         name="finish",
-    )(got, maps_all, spread_c, y_local, cum, rate, lit)
+    )(got, gathered, act, rate, vecs, lit, spread, *stay(delta, inside, before))
 
 
 def solution(mesh):

time: 99.3 us -> 101 us (1.017)
  blocking collectives: 40.6 us -> 52.1 us
  starting transfers between devices: 16.7 us -> 11.1 us
  Pallas kernels: 14.9 us -> 11.9 us
    all_to_all x0 -> x1, blocking collectives: none -> 11.5 us  [on_device(): got = lax.all_to_all(pay, 'ctx', 0, 0)]
    all_to_all x1 -> x0, starting transfers between devices: 5.7 us -> none  [on_device(): got = lax.all_to_all(pay, 'ctx', 0, 0)]
    pallas_call x2, Pallas kernels: 8.01 us -> 5.11 us  [the longest x1 4.82 us: on_device(): pl.pallas_call(functools.partial(finish_kernel, rank), out_shape=jax.Shap...]
  transfers between devices with their start and end apart: 3 -> 2, of which waited for: 3 -> 2; matrix products, arithmetic and copies ran while one was open for 0% -> 0% of each run, Pallas kernels for 7% -> 2%
where the time goes in v3:
time: 101 us
  blocking collectives  52.1 us (52%)
  waiting for transfers between devices  24.6 us (24%)
  Pallas kernels  11.9 us (12%)
  starting transfers between devices  11.1 us (11%)
    all_to_all x1, blocking collectives, on_device(): parts = lax.all_to_all(part.reshape(n_ch, rows // n_ch, wide), 'ch', 0, 0)  40.6 us
    all_to_all x1, waiting for transfers between devices, on_device(): gathered = lax.all_to_all(totals, 'ch', 0, 0).reshape(rows, wide)  23.3 us
    all_to_all x1, blocking collectives, on_device(): got = lax.all_to_all(pay, 'ctx', 0, 0)  11.5 us
    all_to_all x1, starting transfers between devices, on_device(): gathered = lax.all_to_all(totals, 'ch', 0, 0).reshape(rows, wide)  5.72 us
    ppermute x1, starting transfers between devices, on_device(): lax.ppermute(mamba_in[rows - 16:], 'ctx', [(i, i + 1) for i in range(n_ct...  5.38 us
    pallas_call x1, Pallas kernels, on_device(): pl.pallas_call(functools.partial(finish_kernel, rank), out_shape=jax.Shap...  4.82 us
    pallas_call x1, Pallas kernels, on_device(): pl.pallas_call(functools.partial(ends_kernel, rank), out_shape=tuple((plt...  3.5 us
    pallas_call x1, Pallas kernels, on_device(): pl.pallas_call(project_kernel, out_shape=(tile, part_shape, jax.ShapeDtyp...  2.05 us
  transfers between devices with their start and end apart: 2, of which 2 were waited for; matrix products, arithmetic and copies ran while one was open for 0% of the time, Pallas kernels for 2%

profile of v3, /device:TPU:1, one launch (start us, length us, event | category | flops | bytes accessed | tf_op | source)
XLA Modules:
  0.0 100.6 jit_solution(15075248366852116484)
XLA Ops:
  0.0 0.7 slice.3
  0.7 5.4 %collective-permute-start = (bf16[16,256]{1,0:T(8,128)(2,1)S(1)}, bf16[16,256]{1,0:T(8,128)(2,1)S(1)}, u32[]{:S(2)}, u32[]{:S(2)}) collective-permute-start(bf16[16,256]{1,0:T(8,128)(2,1)S(1)} %slice.3), channel_id=1, source_target_pairs={{0,64},{64,128},{128,192},{192,256},{256,320},{320,384},{384,448},... | collective-permute-start | bytes 24584 | tf_op jit(solution)/shard_map/ppermute | solution.py:295
  6.1 2.1 %project.1 = (f32[512,256]{1,0:T(8,128)S(1)}, bf16[512,640]{1,0:T(8,128)(2,1)S(1)}, f32[8,256]{1,0:T(8,128)S(1)}, bf16[256,512]{1,0:T(8,128)(2,1)S(1)}, bf16[128...) custom-call(bf16[512,256]{1,0:T(8,128)(2,1)} %x_hbm.1, ...), custom_call_target="tpu_custom_call" | custom-call | flops 167772160 | bytes 2097152 | tf_op jit(solution)/shard_map/project/pallas_call | solution.py:296
  8.1 1.4 %collective-permute-done.halo_ref = bf16[16,256]{1,0:T(8,128)(2,1)S(1)} collective-permute-done((bf16[16,256]{1,0:T(8,128)(2,1)S(1)}, bf16[16,256]{1,0:T(8,128)(2,1)S(1)}, u32[]{:S(2)}, u32[]{:S(2)}) %collective-permute-start) | collective-permute-done | bytes 8224 | tf_op jit(solution)/shard_map/ppermute | solution.py:295
  9.5 0.2 first_rows.1
  9.7 40.6 %all_to_all.15.parts_ref = bf16[64,8,640]{2,1,0:T(8,128)(2,1)S(1)} all-to-all(bf16[64,8,640]{2,1,0:T(8,128)(2,1)S(1)} %bitcast.9), channel_id=1, replica_groups=mesh['ctx'=8,'ch'=64] {'ch'}, dimensions={0} | all-to-all | bytes 1310720 | tf_op jit(solution)/shard_map/all_to_all | solution.py:354
  50.4 1.1 %total.1 = bf16[64,8,640]{2,1,0:T(8,128)(2,1)} custom-call(bf16[64,8,640]{2,1,0:T(8,128)(2,1)S(1)} %all_to_all.15.parts_ref), custom_call_target="tpu_custom_call" | custom-call | tf_op jit(solution)/shard_map/total/pallas_call | solution.py:355
  51.4 0.0 copy-start
  51.4 5.7 %all-to-all-start.1 = ((bf16[64,8,640]{2,1,0:T(8,128)(2,1)}), bf16[64,8,640]{2,1,0:T(8,128)(2,1)S(1)}, u32[]{:S(2)}, u32[]{:S(2)}) async-start(bf16[64,8,640]{2,1,0:T(8,128)(2,1)} %total.1), calls=%async_computation.1 | async-start | bytes 1310720 | tf_op jit(solution)/shard_map/all_to_all | solution.py:363
  57.1 0.0 copy-done
  57.2 0.3 ready.1
  57.4 23.3 %all-to-all-done.1 = bf16[64,8,640]{2,1,0:T(8,128)(2,1)S(1)} async-done(((bf16[64,8,640]{2,1,0:T(8,128)(2,1)}), bf16[64,8,640]{2,1,0:T(8,128)(2,1)S(1)}, u32[]{:S(2)}, u32[]{:S(2)}) %all-to-all-start.1) | async-done | bytes 655392 | tf_op jit(solution)/shard_map/all_to_all | solution.py:363
  80.7 3.5 %ends.1 = (f32[512,256]{1,0:T(8,128)}, f32[16,8,256]{2,1,0:T(8,128)}, f32[8,256]{1,0:T(8,128)}, bf16[8,32,256]{2,1,0:T(8,128)(2,1)}) custom-call(s32[1]{0:T(128)} %bitcast.me_ref, bf16[512,640]{1,0:T(8,128)(2,1)S(1)} %bitcast.7, f32[512,256]{1,0:T(8,128)S(1)} %get-tuple-element.29.act_ref, bf16[512,256]{1,0:T(8,128)(2,1)S(1)} %get-tuple-element.30.dw_ref, ...), custom_call_target="tpu_custom_call" | custom-call | tf_op jit(solution)/shard_map/ends/pallas_call | solution.py:371
  84.2 11.5 %all_to_all.16.got_ref = bf16[8,32,256]{2,1,0:T(8,128)(2,1)S(1)} all-to-all(bf16[8,32,256]{2,1,0:T(8,128)(2,1)} %get-tuple-element.34), channel_id=1, replica_groups=mesh['ctx'=8,'ch'=64] {'ctx'}, dimensions={0} | all-to-all | bytes 262144 | tf_op jit(solution)/shard_map/all_to_all | solution.py:388
  95.8 4.8 %finish.1 = bf16[512,256]{1,0:T(8,128)(2,1)} custom-call(bf16[8,32,256]{2,1,0:T(8,128)(2,1)S(1)} %all_to_all.16.got_ref, bf16[512,640]{1,0:T(8,128)(2,1)S(1)} %bitcast.8, f32[512,256]{1,0:T(8,128)S(1)} %get-tuple-element.29.act_ref, f32[16,256]{1,0:T(8,128)S(1)} %get-tuple-element.32.rate, f32[8,256]{1,0:T(8,128)S(1)} %get-tuple-element.31.vecs_ref, ...), custom_call_target="tpu_custom_call" | custom-call | tf_op jit(solution)/shard_map/finish/pallas_call | solution.py:389
Async XLA Ops:
  0.7 8.8 %collective-permute-start = (bf16[16,256]{1,0:T(8,128)(2,1)S(1)}, bf16[16,256]{1,0:T(8,128)(2,1)S(1)}, u32[]{:S(2)}, u32[]{:S(2)}) collective-permute-start(bf16[16,256]{1,0:T(8,128)(2,1)S(1)} %slice.3), channel_id=1, source_target_pairs={{0,64},{64,128},{128,192},{192,256},{256,320},{320,384},{384,448},... | collective-permute-start | bytes 24584 | tf_op jit(solution)/shard_map/ppermute | solution.py:295
  51.4 5.7 %copy-start = (bf16[512,256]{1,0:T(8,128)(2,1)S(1)}, bf16[512,256]{1,0:T(8,128)(2,1)}, u32[]{:S(2)}) copy-start(bf16[512,256]{1,0:T(8,128)(2,1)} %gate_ref.1) | copy-start | bytes 786436
  51.4 29.3 %all-to-all-start.1 = ((bf16[64,8,640]{2,1,0:T(8,128)(2,1)}), bf16[64,8,640]{2,1,0:T(8,128)(2,1)S(1)}, u32[]{:S(2)}, u32[]{:S(2)}) async-start(bf16[64,8,640]{2,1,0:T(8,128)(2,1)} %total.1), calls=%async_computation.1 | async-start | bytes 1310720 | tf_op jit(solution)/shard_map/all_to_all | solution.py:363

commit v4 on v2

--- a/solution.py
+++ b/solution.py
@@ -143,7 +143,7 @@
 
 
 def ends_kernel(
-    rank, me_ref, g_ref, act_ref, dw_ref, vecs_ref, rate,
+    rank, g_ref, act_ref, dw_ref, vecs_ref, rate,
     delta_hbm, inside_hbm, before_hbm, pay_hbm,
     delta, inside_ref, before_ref, pay_ref, drive, b_all, cum_ref, ends, sems,
 ):
@@ -204,7 +204,7 @@
 
     copies[1].start()
     copies[2].start()
-    me = me_ref[0]
+    me = lax.axis_index("ctx")
     value = ends[0:STATE, :]
     total = jnp.broadcast_to(ends[STATE : STATE + 1, :], value.shape)
     high = total.astype(BF16).astype(F32)
@@ -266,7 +266,7 @@
     lit_ref[...] = silu(gate_ref[...].astype(F32))
 
 
-def finish_kernel(got_ref, maps_ref, spread_ref, y_ref, cum_ref, rate, lit_ref, out_ref, c_all, carry, ys):
+def finish_kernel(got_ref, maps_ref, spread_ref, y_ref, cum_ref, rate, lit_ref, out_hbm, c_all, carry, ys, out_ref, sems):
     rows, width = y_ref.shape
     steps = rows // CHUNKS
     halves = width // LANES
@@ -277,6 +277,7 @@
         decay = jnp.exp2(rate[...] * (tail[0:1, :] + tail[1:2, :]))
         incoming = decay * incoming + got_ref[source, 0:16, :].astype(F32)
     carry[...] = incoming
+    leaving = []
     for half in range(halves):
         cols = slice(half * LANES, (half + 1) * LANES)
         rates = [jnp.broadcast_to(rate[n : n + 1, cols], (CHUNKS, LANES)) for n in range(STATE)]
@@ -293,7 +294,12 @@
             return 0
 
         lax.fori_loop(0, steps, correct, 0, unroll=8)
-        out_ref[:, cols] = (ys[half] * lit_ref[:, cols]).astype(BF16)
+        out_ref[half] = (ys[half] * lit_ref[:, cols]).astype(BF16)
+        copy = pltpu.make_async_copy(out_ref.at[half], out_hbm.at[:, cols], sems.at[half])
+        copy.start()
+        leaving.append(copy)
+    for copy in leaving:
+        copy.wait()
 
 
 def on_device(
@@ -306,7 +312,6 @@
     steps = rows // CHUNKS
     n_ctx, n_ch = lax.axis_size("ctx"), lax.axis_size("ch")
     wide = rank + LANES
-    me = lax.axis_index("ctx").astype(jnp.int32).reshape(1)
     cells = rows * width * STATE
     tile = jax.ShapeDtypeStruct((rows, width), F32)
     part_shape = jax.ShapeDtypeStruct((rows, wide), BF16)
@@ -380,7 +385,7 @@
     delta, inside, before, pay = pl.pallas_call(
         functools.partial(ends_kernel, rank),
         out_shape=tuple(pltpu.HBM(*kept) for kept in sent),
-        in_specs=[pl.BlockSpec(memory_space=pltpu.SMEM)] + vmem(5),
+        in_specs=vmem(5),
         out_specs=tuple(hbm(4)),
         scratch_shapes=[
             *(pltpu.VMEM(*kept) for kept in sent),
@@ -392,7 +397,7 @@
         ],
         compiler_params=pltpu.CompilerParams(vmem_limit_bytes=16 * MIB),
         name="ends",
-    )(me, gathered, act, dw, vecs, rate)
+    )(gathered, act, dw, vecs, rate)
 
     got = lax.all_to_all(pay, "ctx", 0, 0)
     y_local, cum, lit, spread_c, maps_all = pl.pallas_call(
@@ -421,11 +426,13 @@
         finish_kernel,
         out_shape=jax.ShapeDtypeStruct((rows, width), BF16),
         in_specs=vmem(7),
-        out_specs=vmem(1)[0],
+        out_specs=hbm(1)[0],
         scratch_shapes=[
             big,
             pltpu.VMEM((STATE, width), F32),
             pltpu.VMEM((halves, rows, LANES), F32),
+            pltpu.VMEM((halves, rows, LANES), BF16),
+            pltpu.SemaphoreType.DMA((halves,)),
         ],
         compiler_params=pltpu.CompilerParams(vmem_limit_bytes=16 * MIB),
         name="finish",

time: 99.3 us -> 98.1 us (0.988)
  blocking collectives: 40.6 us -> 69.6 us
  waiting for transfers between devices: 25.1 us -> 1.54 us
  starting transfers between devices: 16.7 us -> 11.1 us
    all_to_all x0 -> x1, blocking collectives: none -> 29 us  [on_device(): gathered = lax.all_to_all(totals, 'ch', 0, 0).reshape(rows, wide)]
    all_to_all x1 -> x0, waiting for transfers between devices: 23.6 us -> none  [on_device(): gathered = lax.all_to_all(totals, 'ch', 0, 0).reshape(rows, wide)]
    all_to_all x1 -> x0, starting transfers between devices: 5.59 us -> none  [on_device(): gathered = lax.all_to_all(totals, 'ch', 0, 0).reshape(rows, wide)]
  transfers between devices with their start and end apart: 3 -> 2, of which waited for: 3 -> 2; matrix products, arithmetic and copies ran while one was open for 0% -> 0% of each run, Pallas kernels for 7% -> 7%
where the time goes in v4:
time: 98.1 us; the launch traced here: 97.7 us
  blocking collectives  69.6 us (71%)
  Pallas kernels  14 us (14%)
  starting transfers between devices  11.1 us (11%)
  waiting for transfers between devices  1.54 us (2%)
  local copies, waits for them, and re-layouts  1.4 us (1%)
    all_to_all x1, blocking collectives, on_device(): parts = lax.all_to_all(part.reshape(n_ch, rows // n_ch, wide), 'ch', 0, 0)  40.6 us
    all_to_all x1, blocking collectives, on_device(): gathered = lax.all_to_all(totals, 'ch', 0, 0).reshape(rows, wide)  29 us
    all_to_all x1, starting transfers between devices, on_device(): got = lax.all_to_all(pay, 'ctx', 0, 0)  5.7 us
    ppermute x1, starting transfers between devices, on_device(): lax.ppermute(mamba_in[rows - 16:], 'ctx', [(i, i + 1) for i in range(n_ct...  5.38 us
    pallas_call x1, Pallas kernels, on_device(): pl.pallas_call(functools.partial(local_kernel, rank), out_shape=(tile, ti...  4.91 us
    pallas_call x1, Pallas kernels, on_device(): pl.pallas_call(functools.partial(ends_kernel, rank), out_shape=tuple((plt...  3.54 us
    pallas_call x1, Pallas kernels, on_device(): pl.pallas_call(finish_kernel, out_shape=jax.ShapeDtypeStruct((rows, width...  3.06 us
    pallas_call x1, Pallas kernels, on_device(): pl.pallas_call(project_kernel, out_shape=(tile, part_shape, jax.ShapeDtyp...  2.05 us
  transfers between devices with their start and end apart: 2, of which 2 were waited for; matrix products, arithmetic and copies ran while one was open for 0% of the time, Pallas kernels for 7%

profile of v4, /device:TPU:1, one launch (start us, length us, event | category | flops | bytes accessed | tf_op | source)
XLA Modules:
  0.0 97.7 jit_solution(12302325869780146299)
XLA Ops:
  0.0 0.7 slice.3
  0.7 5.4 %collective-permute-start = (bf16[16,256]{1,0:T(8,128)(2,1)S(1)}, bf16[16,256]{1,0:T(8,128)(2,1)S(1)}, u32[]{:S(2)}, u32[]{:S(2)}) collective-permute-start(bf16[16,256]{1,0:T(8,128)(2,1)S(1)} %slice.3), channel_id=1, source_target_pairs={{0,64},{64,128},{128,192},{192,256},{256,320},{320,384},{384,448},... | collective-permute-start | bytes 24584 | tf_op jit(solution)/shard_map/ppermute | solution.py:320
  6.1 2.1 %project.1 = (f32[512,256]{1,0:T(8,128)S(1)}, bf16[512,640]{1,0:T(8,128)(2,1)S(1)}, f32[8,256]{1,0:T(8,128)S(1)}, bf16[256,512]{1,0:T(8,128)(2,1)S(1)}, bf16[128...) custom-call(bf16[512,256]{1,0:T(8,128)(2,1)} %x_hbm.1, ...), custom_call_target="tpu_custom_call" | custom-call | flops 167772160 | bytes 2097152 | tf_op jit(solution)/shard_map/project/pallas_call | solution.py:321
  8.1 0.0 copy-start
  8.2 1.4 %collective-permute-done.halo_ref = bf16[16,256]{1,0:T(8,128)(2,1)S(1)} collective-permute-done((bf16[16,256]{1,0:T(8,128)(2,1)S(1)}, bf16[16,256]{1,0:T(8,128)(2,1)S(1)}, u32[]{:S(2)}, u32[]{:S(2)}) %collective-permute-start) | collective-permute-done | bytes 8224 | tf_op jit(solution)/shard_map/ppermute | solution.py:320
  9.5 0.2 first_rows.1
  9.7 40.6 %all_to_all.15.parts_ref = bf16[64,8,640]{2,1,0:T(8,128)(2,1)S(1)} all-to-all(bf16[64,8,640]{2,1,0:T(8,128)(2,1)S(1)} %bitcast.8), channel_id=1, replica_groups=mesh['ctx'=8,'ch'=64] {'ch'}, dimensions={0} | all-to-all | bytes 1310720 | tf_op jit(solution)/shard_map/all_to_all | solution.py:368
  50.4 0.2 total.1
  50.6 29.0 %all_to_all.16 = bf16[64,8,640]{2,1,0:T(8,128)(2,1)S(1)} all-to-all(bf16[64,8,640]{2,1,0:T(8,128)(2,1)S(1)} %total.1), channel_id=1, replica_groups=mesh['ctx'=8,'ch'=64] {'ch'}, dimensions={0} | all-to-all | bytes 1310720 | tf_op jit(solution)/shard_map/all_to_all | solution.py:377
  79.6 0.0 copy-done
  79.6 3.5 %ends.1 = (f32[512,256]{1,0:T(8,128)}, f32[16,8,256]{2,1,0:T(8,128)}, f32[8,256]{1,0:T(8,128)}, bf16[8,32,256]{2,1,0:T(8,128)(2,1)}) custom-call(bf16[512,640]{1,0:T(8,128)(2,1)S(1)} %bitcast.6, f32[512,256]{1,0:T(8,128)S(1)} %get-tuple-element.32.act_ref, bf16[512,256]{1,0:T(8,128)(2,1)S(1)} %get-tuple-element.33.dw_ref, ...), custom_call_target="tpu_custom_call" | custom-call | tf_op jit(solution)/shard_map/ends/pallas_call | solution.py:385
  83.1 5.7 %all-to-all-start.2 = ((bf16[8,32,256]{2,1,0:T(8,128)(2,1)}), bf16[8,32,256]{2,1,0:T(8,128)(2,1)S(1)}, u32[]{:S(2)}, u32[]{:S(2)}) async-start(bf16[8,32,256]{2,1,0:T(8,128)(2,1)} %get-tuple-element.36), calls=%async_computation.2 | async-start | bytes 262144 | tf_op jit(solution)/shard_map/all_to_all | solution.py:402
  88.8 0.0 copy-start.1
  88.8 0.7 copy-done.1
  89.5 4.9 %local_scan.1 = (f32[512,256]{1,0:T(8,128)S(1)}, f32[512,256]{1,0:T(8,128)S(1)}, f32[512,256]{1,0:T(8,128)S(1)}, bf16[128,2048]{1,0:T(8,128)(2,1)S(1)}, bf16[512,128]{1,0:T(8,128)(2,1)S(1)}) custom-call(bf16[512,640]{1,0:T(8,128)(2,1)S(1)} %bitcast.7, f32[512,256]{1,0:T(8,128)S(1)} %get-tuple-element.32.act_ref, f32[16,256]{1,0:T(8,128)S(1)} %get-tuple-element.35.rate, ...), custom_call_target="tpu_custom_call" | custom-call | flops 12582912 | bytes 4194304 | tf_op jit(solution)/shard_map/local_scan/pallas_call | solution.py:403
  94.4 0.2 all-to-all-done.2.got_ref
  94.6 3.1 %finish.1 = bf16[512,256]{1,0:T(8,128)(2,1)} custom-call(bf16[8,32,256]{2,1,0:T(8,128)(2,1)S(1)} %all-to-all-done.2.got_ref, bf16[512,128]{1,0:T(8,128)(2,1)S(1)} %get-tuple-element.40.maps_ref, bf16[128,2048]{1,0:T(8,128)(2,1)S(1)} %get-tuple-element.41.spread_ref, f32[512,256]{1,0:T(8,128)S(1)} %get-tuple-element.42.y_ref, ...), custom_call_target="tpu_custom_call" | custom-call | tf_op jit(solution)/shard_map/finish/pallas_call | solution.py:425
Async XLA Ops:
  0.7 8.8 %collective-permute-start = (bf16[16,256]{1,0:T(8,128)(2,1)S(1)}, bf16[16,256]{1,0:T(8,128)(2,1)S(1)}, u32[]{:S(2)}, u32[]{:S(2)}) collective-permute-start(bf16[16,256]{1,0:T(8,128)(2,1)S(1)} %slice.3), channel_id=1, source_target_pairs={{0,64},{64,128},{128,192},{192,256},{256,320},{320,384},{384,448},... | collective-permute-start | bytes 24584 | tf_op jit(solution)/shard_map/ppermute | solution.py:320
  8.1 71.4 %copy-start = (f32[8,256]{1,0:T(8,128)}, f32[8,256]{1,0:T(8,128)S(1)}, u32[]{:S(2)}) copy-start(f32[8,256]{1,0:T(8,128)S(1)} %get-tuple-element.34.vecs_ref) | copy-start | bytes 24580
  83.1 11.5 %all-to-all-start.2 = ((bf16[8,32,256]{2,1,0:T(8,128)(2,1)}), bf16[8,32,256]{2,1,0:T(8,128)(2,1)S(1)}, u32[]{:S(2)}, u32[]{:S(2)}) async-start(bf16[8,32,256]{2,1,0:T(8,128)(2,1)} %get-tuple-element.36), calls=%async_computation.2 | async-start | bytes 262144 | tf_op jit(solution)/shard_map/all_to_all | solution.py:402
  88.8 0.7 copy-start.1

commit v5 on v4

--- a/solution.py
+++ b/solution.py
@@ -113,11 +113,15 @@
     put_products(low, pd_ref[...], sel_ref[...], maps, rank, part_ref, slice(0, HEAD))
 
 
-def total_kernel(rank, maps, parts_ref, out_ref):
-    devices, rows, width = parts_ref.shape
+def total_kernel(parts_ref, out_ref):
     total = parts_ref[0].astype(F32)
-    for source in range(1, devices):
+    for source in range(1, parts_ref.shape[0]):
         total = total + parts_ref[source].astype(F32)
+    out_ref[...] = total
+
+
+def share_kernel(rank, maps, mine_ref, other_ref, out_ref):
+    total = mine_ref[...] + other_ref[...]
     chosen = total[:, rank:]
     lane = lax.broadcasted_iota(jnp.int32, chosen.shape, 1)
     summed = chosen + pltpu.roll(chosen, LANES - maps, 1)
@@ -126,7 +130,7 @@
     rest = jnp.where(lane < 2 * maps, twice - high, 0.0)
     mixed = jnp.where(lane < maps, high, rest)
     row = jnp.concatenate([total[:, :rank], mixed], axis=1).astype(BF16)
-    for target in range(devices):
+    for target in range(out_ref.shape[0]):
         out_ref[target] = row
 
 
@@ -365,16 +369,28 @@
         name="first_rows",
     )(halo, head, taps, pd, sel, act, part)
 
-    parts = lax.all_to_all(part.reshape(n_ch, rows // n_ch, wide), "ch", 0, 0)
-    totals = pl.pallas_call(
-        functools.partial(total_kernel, rank, maps),
-        out_shape=jax.ShapeDtypeStruct(parts.shape, BF16),
+    near = n_ch // 2
+    groups = [list(range(near)), list(range(near, n_ch))]
+    own = rows // near
+    parts = lax.all_to_all(part.reshape(near, own, wide), "ch", 0, 0, axis_index_groups=groups)
+    mine = pl.pallas_call(
+        total_kernel,
+        out_shape=jax.ShapeDtypeStruct((own, wide), F32),
         in_specs=vmem(1),
         out_specs=vmem(1)[0],
         compiler_params=pltpu.CompilerParams(vmem_limit_bytes=16 * MIB),
         name="total",
     )(parts)
-    gathered = lax.all_to_all(totals, "ch", 0, 0).reshape(rows, wide)
+    other = lax.ppermute(mine, "ch", [(i, (i + near) % n_ch) for i in range(n_ch)])
+    totals = pl.pallas_call(
+        functools.partial(share_kernel, rank, maps),
+        out_shape=jax.ShapeDtypeStruct(parts.shape, BF16),
+        in_specs=vmem(2),
+        out_specs=vmem(1)[0],
+        compiler_params=pltpu.CompilerParams(vmem_limit_bytes=16 * MIB),
+        name="share",
+    )(mine, other)
+    gathered = lax.all_to_all(totals, "ch", 0, 0, axis_index_groups=groups).reshape(rows, wide)
 
     sent = (
         ((rows, width), F32),

time: 98.1 us -> 93.1 us (0.949)
  blocking collectives: 69.6 us -> 49.6 us
  starting transfers between devices: 11.1 us -> 24.3 us
  waiting for transfers between devices: 1.54 us -> 3.25 us
    all_to_all x2, blocking collectives: 69.6 us -> 49.6 us  [the longest x1 27.4 us: on_device(): lax.all_to_all(part.reshape(near, own, wide), 'ch', 0, 0, axis_index_grou...]
    ppermute x0 -> x1, starting transfers between devices: none -> 9.6 us  [on_device(): lax.ppermute(mine, 'ch', [(i, (i + near) % n_ch) for i in range(n_ch)])]
    all_to_all x1, starting transfers between devices: 5.7 us -> 9.29 us  [on_device(): got = lax.all_to_all(pay, 'ctx', 0, 0)]
    ppermute x0 -> x1, waiting for transfers between devices: none -> 1.71 us  [on_device(): lax.ppermute(mine, 'ch', [(i, (i + near) % n_ch) for i in range(n_ch)])]
  transfers between devices with their start and end apart: 2 -> 3, of which waited for: 2 -> 3; matrix products, arithmetic and copies ran while one was open for 0% -> 0% of each run, Pallas kernels for 7% -> 8%
where the time goes in v5:
time: 93.1 us; the launch traced here: 92.6 us
  blocking collectives  49.6 us (53%)
  starting transfers between devices  24.3 us (26%)
  Pallas kernels  14 us (15%)
  waiting for transfers between devices  3.25 us (3%)
  local copies, waits for them, and re-layouts  1.4 us (2%)
    all_to_all x1, blocking collectives, on_device(): lax.all_to_all(part.reshape(near, own, wide), 'ch', 0, 0, axis_index_grou...  27.4 us
    all_to_all x1, blocking collectives, on_device(): lax.all_to_all(totals, 'ch', 0, 0, axis_index_groups=groups)  22.2 us
    ppermute x1, starting transfers between devices, on_device(): lax.ppermute(mine, 'ch', [(i, (i + near) % n_ch) for i in range(n_ch)])  9.6 us
    all_to_all x1, starting transfers between devices, on_device(): got = lax.all_to_all(pay, 'ctx', 0, 0)  9.29 us
    ppermute x1, starting transfers between devices, on_device(): lax.ppermute(mamba_in[rows - 16:], 'ctx', [(i, i + 1) for i in range(n_ct...  5.38 us
    pallas_call x1, Pallas kernels, on_device(): pl.pallas_call(functools.partial(local_kernel, rank), out_shape=(tile, ti...  4.91 us
    pallas_call x1, Pallas kernels, on_device(): pl.pallas_call(functools.partial(ends_kernel, rank), out_shape=tuple((plt...  3.53 us
    pallas_call x1, Pallas kernels, on_device(): pl.pallas_call(finish_kernel, out_shape=jax.ShapeDtypeStruct((rows, width...  3.06 us
  transfers between devices with their start and end apart: 3, of which 3 were waited for; matrix products, arithmetic and copies ran while one was open for 0% of the time, Pallas kernels for 8%

profile of v5, /device:TPU:1, one launch (start us, length us, event | category | flops | bytes accessed | tf_op | source)
XLA Modules:
  0.0 92.6 jit_solution(12959651131063770201)
XLA Ops:
  0.0 0.7 slice.3
  0.7 5.4 %collective-permute-start = (bf16[16,256]{1,0:T(8,128)(2,1)S(1)}, bf16[16,256]{1,0:T(8,128)(2,1)S(1)}, u32[]{:S(2)}, u32[]{:S(2)}) collective-permute-start(bf16[16,256]{1,0:T(8,128)(2,1)S(1)} %slice.3), channel_id=1, source_target_pairs={{0,64},{64,128},{128,192},{192,256},{256,320},{320,384},{384,448},... | collective-permute-start | bytes 24584 | tf_op jit(solution)/shard_map/ppermute | solution.py:324
  6.1 2.1 %project.1 = (f32[512,256]{1,0:T(8,128)S(1)}, bf16[512,640]{1,0:T(8,128)(2,1)S(1)}, f32[8,256]{1,0:T(8,128)S(1)}, bf16[256,512]{1,0:T(8,128)(2,1)S(1)}, bf16[128...) custom-call(bf16[512,256]{1,0:T(8,128)(2,1)} %x_hbm.1, ...), custom_call_target="tpu_custom_call" | custom-call | flops 167772160 | bytes 2097152 | tf_op jit(solution)/shard_map/project/pallas_call | solution.py:325
  8.1 0.0 copy-start
  8.2 1.4 %collective-permute-done.halo_ref = bf16[16,256]{1,0:T(8,128)(2,1)S(1)} collective-permute-done((bf16[16,256]{1,0:T(8,128)(2,1)S(1)}, bf16[16,256]{1,0:T(8,128)(2,1)S(1)}, u32[]{:S(2)}, u32[]{:S(2)}) %collective-permute-start) | collective-permute-done | bytes 8224 | tf_op jit(solution)/shard_map/ppermute | solution.py:324
  9.5 0.2 first_rows.1
  9.7 27.4 %all_to_all.15.parts_ref = bf16[32,16,640]{2,1,0:T(8,128)(2,1)S(1)} all-to-all(bf16[32,16,640]{2,1,0:T(8,128)(2,1)S(1)} %bitcast.8), channel_id=1, replica_groups={{0,1,2,3,4,5,6,7,8,9,10,11,12,13,14,15,16,17,18,19,20,21,22,23,24,25,26..., dimensions={0} | all-to-all | bytes 1310720 | tf_op jit(solution)/shard_map/all_to_all | solution.py:375
  37.1 0.1 total.1.mine_ref
  37.2 9.6 %collective-permute-start.1 = (f32[16,640]{1,0:T(8,128)S(1)}, f32[16,640]{1,0:T(8,128)S(1)}, u32[]{:S(2)}, u32[]{:S(2)}) collective-permute-start(f32[16,640]{1,0:T(8,128)S(1)} %total.1.mine_ref), channel_id=1, source_target_pairs={{0,32},{1,33},{2,34},{3,35},{4,36},{5,37},{6,38},{7,39},{8,40},{9,... | collective-permute-start | bytes 122888 | tf_op jit(solution)/shard_map/ppermute | solution.py:384
  46.8 1.7 %collective-permute-done.1.other_ref = f32[16,640]{1,0:T(8,128)S(1)} collective-permute-done((f32[16,640]{1,0:T(8,128)S(1)}, f32[16,640]{1,0:T(8,128)S(1)}, u32[]{:S(2)}, u32[]{:S(2)}) %collective-permute-start.1) | collective-permute-done | bytes 40992 | tf_op jit(solution)/shard_map/ppermute | solution.py:384
  48.5 0.2 share.1
  48.7 22.2 %all_to_all.16 = bf16[32,16,640]{2,1,0:T(8,128)(2,1)S(1)} all-to-all(bf16[32,16,640]{2,1,0:T(8,128)(2,1)S(1)} %share.1), channel_id=1, replica_groups={{0,1,2,3,4,5,6,7,8,9,10,11,12,13,14,15,16,17,18,19,20,21,22,23,24,25,26..., dimensions={0} | all-to-all | bytes 1310720 | tf_op jit(solution)/shard_map/all_to_all | solution.py:393
  70.9 0.0 copy-done
  70.9 3.5 %ends.1 = (f32[512,256]{1,0:T(8,128)}, f32[16,8,256]{2,1,0:T(8,128)}, f32[8,256]{1,0:T(8,128)}, bf16[8,32,256]{2,1,0:T(8,128)(2,1)}) custom-call(bf16[512,640]{1,0:T(8,128)(2,1)S(1)} %bitcast.6, f32[512,256]{1,0:T(8,128)S(1)} %get-tuple-element.32.act_ref, bf16[512,256]{1,0:T(8,128)(2,1)S(1)} %get-tuple-element.33.dw_ref, ...), custom_call_target="tpu_custom_call" | custom-call | tf_op jit(solution)/shard_map/ends/pallas_call | solution.py:401
  74.4 9.3 %all-to-all-start.2 = ((bf16[8,32,256]{2,1,0:T(8,128)(2,1)}), bf16[8,32,256]{2,1,0:T(8,128)(2,1)S(1)}, u32[]{:S(2)}, u32[]{:S(2)}) async-start(bf16[8,32,256]{2,1,0:T(8,128)(2,1)} %get-tuple-element.36), calls=%async_computation.2 | async-start | bytes 262144 | tf_op jit(solution)/shard_map/all_to_all | solution.py:418
  83.7 0.0 copy-start.1
  83.7 0.7 copy-done.1
  84.4 4.9 %local_scan.1 = (f32[512,256]{1,0:T(8,128)S(1)}, f32[512,256]{1,0:T(8,128)S(1)}, f32[512,256]{1,0:T(8,128)S(1)}, bf16[128,2048]{1,0:T(8,128)(2,1)S(1)}, bf16[512,128]{1,0:T(8,128)(2,1)S(1)}) custom-call(bf16[512,640]{1,0:T(8,128)(2,1)S(1)} %bitcast.7, f32[512,256]{1,0:T(8,128)S(1)} %get-tuple-element.32.act_ref, f32[16,256]{1,0:T(8,128)S(1)} %get-tuple-element.35.rate, ...), custom_call_target="tpu_custom_call" | custom-call | flops 12582912 | bytes 4194304 | tf_op jit(solution)/shard_map/local_scan/pallas_call | solution.py:419
  89.3 0.2 all-to-all-done.2.got_ref
  89.5 3.1 %finish.1 = bf16[512,256]{1,0:T(8,128)(2,1)} custom-call(bf16[8,32,256]{2,1,0:T(8,128)(2,1)S(1)} %all-to-all-done.2.got_ref, bf16[512,128]{1,0:T(8,128)(2,1)S(1)} %get-tuple-element.40.maps_ref, bf16[128,2048]{1,0:T(8,128)(2,1)S(1)} %get-tuple-element.41.spread_ref, f32[512,256]{1,0:T(8,128)S(1)} %get-tuple-element.42.y_ref, ...), custom_call_target="tpu_custom_call" | custom-call | tf_op jit(solution)/shard_map/finish/pallas_call | solution.py:441
Async XLA Ops:
  0.7 8.8 %collective-permute-start = (bf16[16,256]{1,0:T(8,128)(2,1)S(1)}, bf16[16,256]{1,0:T(8,128)(2,1)S(1)}, u32[]{:S(2)}, u32[]{:S(2)}) collective-permute-start(bf16[16,256]{1,0:T(8,128)(2,1)S(1)} %slice.3), channel_id=1, source_target_pairs={{0,64},{64,128},{128,192},{192,256},{256,320},{320,384},{384,448},... | collective-permute-start | bytes 24584 | tf_op jit(solution)/shard_map/ppermute | solution.py:324
  8.1 62.7 %copy-start = (f32[8,256]{1,0:T(8,128)}, f32[8,256]{1,0:T(8,128)S(1)}, u32[]{:S(2)}) copy-start(f32[8,256]{1,0:T(8,128)S(1)} %get-tuple-element.34.vecs_ref) | copy-start | bytes 24580
  37.2 11.3 %collective-permute-start.1 = (f32[16,640]{1,0:T(8,128)S(1)}, f32[16,640]{1,0:T(8,128)S(1)}, u32[]{:S(2)}, u32[]{:S(2)}) collective-permute-start(f32[16,640]{1,0:T(8,128)S(1)} %total.1.mine_ref), channel_id=1, source_target_pairs={{0,32},{1,33},{2,34},{3,35},{4,36},{5,37},{6,38},{7,39},{8,40},{9,... | collective-permute-start | bytes 122888 | tf_op jit(solution)/shard_map/ppermute | solution.py:384
  74.4 15.1 %all-to-all-start.2 = ((bf16[8,32,256]{2,1,0:T(8,128)(2,1)}), bf16[8,32,256]{2,1,0:T(8,128)(2,1)S(1)}, u32[]{:S(2)}, u32[]{:S(2)}) async-start(bf16[8,32,256]{2,1,0:T(8,128)(2,1)} %get-tuple-element.36), calls=%async_computation.2 | async-start | bytes 262144 | tf_op jit(solution)/shard_map/all_to_all | solution.py:418
  83.7 0.7 copy-start.1

commit v6 on v5

--- a/solution.py
+++ b/solution.py
@@ -44,7 +44,7 @@
 
 
 def project_kernel(
-    x_hbm, pd_hbm, ps_hbm, weight_hbm, bias_hbm, dw_hbm, log_hbm, dbias_hbm, gain_hbm,
+    x_hbm, pd_hbm, ps_hbm, weight_hbm, bias_hbm, dw_hbm, log_hbm, dbias_hbm,
     act_ref, part_ref, head_ref, pd_ref, sel_ref, taps_ref, dw_ref, rate_ref, vecs_ref,
     x_ref, log_ref, weight_ref, bias_ref, ps_ref, xs, xp, low, sems,
 ):
@@ -55,7 +55,7 @@
     halves = width // LANES
     pairs = (
         (x_hbm, x_ref), (weight_hbm, weight_ref), (bias_hbm, bias_ref), (ps_hbm, ps_ref), (pd_hbm, pd_ref),
-        (log_hbm, log_ref), (dw_hbm, dw_ref), (dbias_hbm, vecs_ref.at[0:1]), (gain_hbm, vecs_ref.at[1:2]),
+        (log_hbm, log_ref), (dw_hbm, dw_ref), (dbias_hbm, vecs_ref.at[0:1]),
     )
     copies = [pltpu.make_async_copy(source, target, sems.at[i]) for i, (source, target) in enumerate(pairs)]
     for copy in copies:
@@ -113,33 +113,49 @@
     put_products(low, pd_ref[...], sel_ref[...], maps, rank, part_ref, slice(0, HEAD))
 
 
-def total_kernel(parts_ref, out_ref):
+def fold(chosen, maps):
+    lane = lax.broadcasted_iota(jnp.int32, chosen.shape, 1)
+    summed = chosen + pltpu.roll(chosen, LANES - maps, 1)
+    twice = jnp.where(lane < maps, summed, pltpu.roll(summed, maps, 1))
+    return jnp.where(lane < 2 * maps, twice, 0.0)
+
+
+def parted(twice, maps):
+    lane = lax.broadcasted_iota(jnp.int32, twice.shape, 1)
+    high = twice.astype(BF16).astype(F32)
+    return jnp.where(lane < maps, high, twice - high).astype(BF16)
+
+
+def total_kernel(rank, maps, parts_ref, mine_ref, send_ref):
     total = parts_ref[0].astype(F32)
     for source in range(1, parts_ref.shape[0]):
         total = total + parts_ref[source].astype(F32)
-    out_ref[...] = total
-
-
-def share_kernel(rank, maps, mine_ref, other_ref, out_ref):
-    total = mine_ref[...] + other_ref[...]
-    chosen = total[:, rank:]
-    lane = lax.broadcasted_iota(jnp.int32, chosen.shape, 1)
-    summed = chosen + pltpu.roll(chosen, LANES - maps, 1)
-    twice = jnp.where(lane < maps, summed, pltpu.roll(summed, maps, 1))
-    high = twice.astype(BF16).astype(F32)
-    rest = jnp.where(lane < 2 * maps, twice - high, 0.0)
-    mixed = jnp.where(lane < maps, high, rest)
-    row = jnp.concatenate([total[:, :rank], mixed], axis=1).astype(BF16)
+    twice = fold(total[:, rank:], maps)
+    mine_ref[:, :rank] = total[:, :rank]
+    mine_ref[:, rank:] = twice
+    send_ref[:, :rank] = total[:, :rank].astype(BF16)
+    send_ref[:, rank:] = parted(twice, maps)
+
+
+def share_kernel(rank, maps, mine_ref, other_ref, ready_ref, out_ref):
+    other = other_ref[...].astype(F32)
+    low = (mine_ref[:, :rank] + other[:, :rank]).astype(BF16)
+    chosen = parted(mine_ref[:, rank:] + fold(other[:, rank:], maps), maps)
     for target in range(out_ref.shape[0]):
-        out_ref[target] = row
-
-
-def spread(first, maps):
-    shape = (LANES, STATE * LANES)
-    source = lax.broadcasted_iota(jnp.int32, shape, 0)
-    group = lax.broadcasted_iota(jnp.int32, shape, 1) >> 7
-    hit = (source == group + first) | (source == group + (first + maps))
-    return jnp.where(hit, 1.0, 0.0).astype(BF16)
+        out_ref[target, :, :rank] = low
+        out_ref[target, :, rank:] = chosen
+
+
+def ready_kernel(mine_ref, gate_hbm, lit_ref, spread_ref, done_ref, gate_ref, sem):
+    copy = pltpu.make_async_copy(gate_hbm, gate_ref, sem)
+    copy.start()
+    source = lax.broadcasted_iota(jnp.int32, spread_ref.shape, 0)
+    group = lax.broadcasted_iota(jnp.int32, spread_ref.shape, 1) >> 7
+    hit = (source == group) | (source == group + 2 * STATE)
+    spread_ref[...] = jnp.where(hit, 1.0, 0.0).astype(BF16)
+    done_ref[...] = jnp.zeros_like(done_ref)
+    copy.wait()
+    lit_ref[...] = silu(gate_ref[...].astype(F32))
 
 
 def step_rows(step):
@@ -147,7 +163,7 @@
 
 
 def ends_kernel(
-    rank, g_ref, act_ref, dw_ref, vecs_ref, rate,
+    rank, g_ref, act_ref, dw_ref, vecs_ref, rate, spread_ref,
     delta_hbm, inside_hbm, before_hbm, pay_hbm,
     delta, inside_ref, before_ref, pay_ref, drive, b_all, cum_ref, ends, sems,
 ):
@@ -161,7 +177,7 @@
     copies = [pltpu.make_async_copy(source, target, sems.at[i]) for i, (source, target) in enumerate(pairs)]
     copies[0].start()
     drive[...] = step_size * act_ref[...]
-    b_all[...] = jnp.dot(g_ref[:, rank:], spread(0, 2 * STATE), preferred_element_type=F32)
+    b_all[...] = jnp.dot(g_ref[:, rank:], spread_ref[...], preferred_element_type=F32)
     chunk = lax.broadcasted_iota(jnp.int32, (CHUNKS, LANES), 0)
     zero = jnp.zeros((CHUNKS, LANES), F32)
 
@@ -224,27 +240,27 @@
 
 
 def local_kernel(
-    rank, g_ref, act_ref, rate, vecs_ref, delta_hbm, inside_hbm, before_hbm, gate_hbm,
-    y_ref, cum_ref, lit_ref, spread_ref, maps_ref,
-    b_all, c_all, delta, inside_ref, before_ref, gate_ref, sems,
+    rank, g_ref, act_ref, rate, spread_ref, delta_hbm, inside_hbm, before_hbm, gain_hbm,
+    y_ref, cum_ref, maps_ref,
+    b_all, c_all, delta, inside_ref, before_ref, gain_ref, sems,
 ):
     rows, width = act_ref.shape
     steps = rows // CHUNKS
     halves = width // LANES
-    pairs = ((delta_hbm, delta), (inside_hbm, inside_ref), (before_hbm, before_ref), (gate_hbm, gate_ref))
+    pairs = ((delta_hbm, delta), (inside_hbm, inside_ref), (before_hbm, before_ref), (gain_hbm, gain_ref))
     copies = [pltpu.make_async_copy(source, target, sems.at[i]) for i, (source, target) in enumerate(pairs)]
     for copy in copies:
         copy.start()
-    b_all[...] = jnp.dot(g_ref[:, rank:], spread(0, 2 * STATE), preferred_element_type=F32)
-    spread_ref[...] = spread(STATE, 2 * STATE)
-    maps_ref[...] = g_ref[:, rank:]
+    maps = g_ref[:, rank:]
+    b_all[...] = jnp.dot(maps, spread_ref[...], preferred_element_type=F32)
+    maps_ref[...] = pltpu.roll(maps.astype(F32), LANES - STATE, 1).astype(BF16)
     c_all[...] = jnp.dot(maps_ref[...], spread_ref[...], preferred_element_type=F32)
     for copy in copies:
         copy.wait()
     for half in range(halves):
         cols = slice(half * LANES, (half + 1) * LANES)
         rates = [jnp.broadcast_to(rate[n : n + 1, cols], (CHUNKS, LANES)) for n in range(STATE)]
-        gain = vecs_ref[1:2, cols]
+        gain = gain_ref[:, cols]
 
         def advance(step, carried, cols=cols, rates=rates, gain=gain):
             states, total = carried
@@ -265,9 +281,8 @@
             return later, total
 
         lax.fori_loop(
-            0, steps, advance, ([inside_ref[n, :, cols] for n in range(STATE)], before_ref[:, cols]), unroll=4
+            0, steps, advance, ([inside_ref[n, :, cols] for n in range(STATE)], before_ref[:, cols]), unroll=8
         )
-    lit_ref[...] = silu(gate_ref[...].astype(F32))
 
 
 def finish_kernel(got_ref, maps_ref, spread_ref, y_ref, cum_ref, rate, lit_ref, out_hbm, c_all, carry, ys, out_ref, sems):
@@ -335,7 +350,7 @@
             jax.ShapeDtypeStruct((STATE, width), F32),
             jax.ShapeDtypeStruct((8, width), F32),
         ),
-        in_specs=hbm(9),
+        in_specs=hbm(8),
         out_specs=tuple(vmem(9)),
         scratch_shapes=[
             pltpu.VMEM((rows, width), BF16),
@@ -346,7 +361,7 @@
             pltpu.VMEM((halves, rows + 8, LANES), F32),
             pltpu.VMEM((halves, (steps + KWIDTH - 1) * CHUNKS, LANES), F32),
             pltpu.VMEM((rows, width), BF16),
-            pltpu.SemaphoreType.DMA((9,)),
+            pltpu.SemaphoreType.DMA((8,)),
         ],
         compiler_params=pltpu.CompilerParams(vmem_limit_bytes=16 * MIB),
         cost_estimate=pl.CostEstimate(
@@ -356,7 +371,7 @@
     )(
         *stay(
             mamba_in, proj_delta, proj_select.T, conv_weight, conv_bias[None, :],
-            delta_weight, decay_log, delta_bias[None, :], skip_gain[None, :],
+            delta_weight, decay_log, delta_bias[None, :],
         )
     )
     act, part = pl.pallas_call(
@@ -373,23 +388,39 @@
     groups = [list(range(near)), list(range(near, n_ch))]
     own = rows // near
     parts = lax.all_to_all(part.reshape(near, own, wide), "ch", 0, 0, axis_index_groups=groups)
-    mine = pl.pallas_call(
-        total_kernel,
-        out_shape=jax.ShapeDtypeStruct((own, wide), F32),
+    mine, send = pl.pallas_call(
+        functools.partial(total_kernel, rank, maps),
+        out_shape=(jax.ShapeDtypeStruct((own, wide), F32), jax.ShapeDtypeStruct((own, wide), BF16)),
         in_specs=vmem(1),
-        out_specs=vmem(1)[0],
+        out_specs=tuple(vmem(2)),
         compiler_params=pltpu.CompilerParams(vmem_limit_bytes=16 * MIB),
         name="total",
     )(parts)
-    other = lax.ppermute(mine, "ch", [(i, (i + near) % n_ch) for i in range(n_ch)])
+    other = lax.ppermute(send, "ch", [(i, (i + near) % n_ch) for i in range(n_ch)])
+    lit, spread, done = pl.pallas_call(
+        ready_kernel,
+        out_shape=(
+            tile,
+            jax.ShapeDtypeStruct((LANES, STATE * LANES), BF16),
+            jax.ShapeDtypeStruct((8, LANES), F32),
+        ),
+        in_specs=vmem(1) + hbm(1),
+        out_specs=tuple(vmem(3)),
+        scratch_shapes=[pltpu.VMEM((rows, width), BF16), pltpu.SemaphoreType.DMA],
+        compiler_params=pltpu.CompilerParams(vmem_limit_bytes=16 * MIB),
+        cost_estimate=pl.CostEstimate(
+            flops=16 * rows * width, bytes_accessed=8 * rows * width, transcendentals=rows * width
+        ),
+        name="ready",
+    )(mine, *stay(mamba_gate))
     totals = pl.pallas_call(
         functools.partial(share_kernel, rank, maps),
         out_shape=jax.ShapeDtypeStruct(parts.shape, BF16),
-        in_specs=vmem(2),
+        in_specs=vmem(3),
         out_specs=vmem(1)[0],
         compiler_params=pltpu.CompilerParams(vmem_limit_bytes=16 * MIB),
         name="share",
-    )(mine, other)
+    )(mine, other, done)
     gathered = lax.all_to_all(totals, "ch", 0, 0, axis_index_groups=groups).reshape(rows, wide)
 
     sent = (
@@ -401,7 +432,7 @@
     delta, inside, before, pay = pl.pallas_call(
         functools.partial(ends_kernel, rank),
         out_shape=tuple(pltpu.HBM(*kept) for kept in sent),
-        in_specs=vmem(5),
+        in_specs=vmem(6),
         out_specs=tuple(hbm(4)),
         scratch_shapes=[
             *(pltpu.VMEM(*kept) for kept in sent),
@@ -413,31 +444,29 @@
         ],
         compiler_params=pltpu.CompilerParams(vmem_limit_bytes=16 * MIB),
         name="ends",
-    )(gathered, act, dw, vecs, rate)
+    )(gathered, act, dw, vecs, rate, spread)
 
     got = lax.all_to_all(pay, "ctx", 0, 0)
-    y_local, cum, lit, spread_c, maps_all = pl.pallas_call(
+    y_local, cum, maps_all = pl.pallas_call(
         functools.partial(local_kernel, rank),
         out_shape=(
             tile,
             tile,
-            tile,
-            jax.ShapeDtypeStruct((LANES, STATE * LANES), BF16),
             jax.ShapeDtypeStruct((rows, LANES), BF16),
         ),
         in_specs=vmem(4) + hbm(4),
-        out_specs=tuple(vmem(5)),
+        out_specs=tuple(vmem(3)),
         scratch_shapes=[
             big,
             big,
             *(pltpu.VMEM(*kept) for kept in sent[:3]),
-            pltpu.VMEM((rows, width), BF16),
+            pltpu.VMEM((1, width), F32),
             pltpu.SemaphoreType.DMA((4,)),
         ],
         compiler_params=pltpu.CompilerParams(vmem_limit_bytes=24 * MIB),
         cost_estimate=pl.CostEstimate(flops=6 * cells, bytes_accessed=8 * rows * width * 4, transcendentals=cells),
         name="local_scan",
-    )(gathered, act, rate, vecs, *stay(delta, inside, before, mamba_gate))
+    )(gathered, act, rate, spread, *stay(delta, inside, before, skip_gain[None, :]))
     return pl.pallas_call(
         finish_kernel,
         out_shape=jax.ShapeDtypeStruct((rows, width), BF16),
@@ -452,7 +481,7 @@
         ],
         compiler_params=pltpu.CompilerParams(vmem_limit_bytes=16 * MIB),
         name="finish",
-    )(got, maps_all, spread_c, y_local, cum, rate, lit)
+    )(got, maps_all, spread, y_local, cum, rate, lit)
 
 
 def solution(mesh):

time: 93.1 us -> 91.9 us (0.987)
    ppermute x1, waiting for transfers between devices: 1.71 us -> 0.04 us  [on_device(): lax.ppermute(send, 'ch', [(i, (i + near) % n_ch) for i in range(n_ch)])]
    pallas_call x1 -> x2, Pallas kernels: 0.1 us -> 1.29 us  [the longest x1 1.11 us: on_device(): pl.pallas_call(ready_kernel, out_shape=(tile, jax.ShapeDtypeStruct((LANES...]
    all_to_all x1, waiting for transfers between devices: 0.19 us -> 1.31 us  [on_device(): got = lax.all_to_all(pay, 'ctx', 0, 0)]
  transfers between devices with their start and end apart: 3 -> 3, of which waited for: 3 -> 2; matrix products, arithmetic and copies ran while one was open for 0% -> 0% of each run, Pallas kernels for 8% -> 8%
where the time goes in v6:
time: 91.9 us; the launch traced here: 91.5 us
  blocking collectives  49.7 us (54%)
  starting transfers between devices  23.6 us (26%)
  Pallas kernels  14.8 us (16%)
  waiting for transfers between devices  2.73 us (3%)
    all_to_all x1, blocking collectives, on_device(): lax.all_to_all(part.reshape(near, own, wide), 'ch', 0, 0, axis_index_grou...  27.4 us
    all_to_all x1, blocking collectives, on_device(): lax.all_to_all(totals, 'ch', 0, 0, axis_index_groups=groups)  22.3 us
    ppermute x1, starting transfers between devices, on_device(): lax.ppermute(send, 'ch', [(i, (i + near) % n_ch) for i in range(n_ch)])  9.59 us
    all_to_all x1, starting transfers between devices, on_device(): got = lax.all_to_all(pay, 'ctx', 0, 0)  8.59 us
    ppermute x1, starting transfers between devices, on_device(): lax.ppermute(mamba_in[rows - 16:], 'ctx', [(i, i + 1) for i in range(n_ct...  5.38 us
    pallas_call x1, Pallas kernels, on_device(): pl.pallas_call(functools.partial(local_kernel, rank), out_shape=(tile, ti...  4.49 us
    pallas_call x1, Pallas kernels, on_device(): pl.pallas_call(functools.partial(ends_kernel, rank), out_shape=tuple((plt...  3.49 us
    pallas_call x1, Pallas kernels, on_device(): pl.pallas_call(finish_kernel, out_shape=jax.ShapeDtypeStruct((rows, width...  3.06 us
  transfers between devices with their start and end apart: 3, of which 2 were waited for; matrix products, arithmetic and copies ran while one was open for 0% of the time, Pallas kernels for 8%

profile of v6, /device:TPU:1, one launch (start us, length us, event | category | flops | bytes accessed | tf_op | source)
XLA Modules:
  0.0 91.5 jit_solution(3877273965880208148)
XLA Ops:
  0.0 0.7 slice.3
  0.7 5.4 %collective-permute-start = (bf16[16,256]{1,0:T(8,128)(2,1)S(1)}, bf16[16,256]{1,0:T(8,128)(2,1)S(1)}, u32[]{:S(2)}, u32[]{:S(2)}) collective-permute-start(bf16[16,256]{1,0:T(8,128)(2,1)S(1)} %slice.3), channel_id=1, source_target_pairs={{0,64},{64,128},{128,192},{192,256},{256,320},{320,384},{384,448},... | collective-permute-start | bytes 24584 | tf_op jit(solution)/shard_map/ppermute | solution.py:339
  6.1 2.0 %project.1 = (f32[512,256]{1,0:T(8,128)S(1)}, bf16[512,640]{1,0:T(8,128)(2,1)S(1)}, f32[8,256]{1,0:T(8,128)S(1)}, bf16[256,512]{1,0:T(8,128)(2,1)S(1)}, bf16[128...) custom-call(bf16[512,256]{1,0:T(8,128)(2,1)} %x_hbm.1, ...), custom_call_target="tpu_custom_call" | custom-call | flops 167772160 | bytes 2097152 | tf_op jit(solution)/shard_map/project/pallas_call | solution.py:340
  8.1 1.4 %collective-permute-done.halo_ref = bf16[16,256]{1,0:T(8,128)(2,1)S(1)} collective-permute-done((bf16[16,256]{1,0:T(8,128)(2,1)S(1)}, bf16[16,256]{1,0:T(8,128)(2,1)S(1)}, u32[]{:S(2)}, u32[]{:S(2)}) %collective-permute-start) | collective-permute-done | bytes 8224 | tf_op jit(solution)/shard_map/ppermute | solution.py:339
  9.5 0.2 first_rows.1
  9.7 27.4 %all_to_all.15.parts_ref = bf16[32,16,640]{2,1,0:T(8,128)(2,1)S(1)} all-to-all(bf16[32,16,640]{2,1,0:T(8,128)(2,1)S(1)} %bitcast.8), channel_id=1, replica_groups={{0,1,2,3,4,5,6,7,8,9,10,11,12,13,14,15,16,17,18,19,20,21,22,23,24,25,26..., dimensions={0} | all-to-all | bytes 1310720 | tf_op jit(solution)/shard_map/all_to_all | solution.py:390
  37.1 0.2 total.1
  37.3 9.6 %collective-permute-start.1 = (bf16[16,640]{1,0:T(8,128)(2,1)S(1)}, bf16[16,640]{1,0:T(8,128)(2,1)S(1)}, u32[]{:S(2)}, u32[]{:S(2)}) collective-permute-start(bf16[16,640]{1,0:T(8,128)(2,1)S(1)} %get-tuple-element.36), channel_id=1, source_target_pairs={{0,32},{1,33},{2,34},{3,35},{4,36},{5,37},{6,38},{7,39},{8,40},{9,... | collective-permute-start | bytes 61448 | tf_op jit(solution)/shard_map/ppermute | solution.py:399
  46.9 1.1 %ready.1 = (f32[512,256]{1,0:T(8,128)S(1)}, bf16[128,2048]{1,0:T(8,128)(2,1)S(1)}, f32[8,128]{1,0:T(8,128)S(1)}) custom-call(f32[16,640]{1,0:T(8,128)S(1)} %get-tuple-element.35.mine_ref, bf16[512,256]{1,0:T(8,128)(2,1)} %gate_hbm.1), custom_call_target="tpu_custom_call" | custom-call | flops 2097152 | bytes 1048576 | tf_op jit(solution)/shard_map/ready/pallas_call | solution.py:400
  48.0 0.0 collective-permute-done.1.other_ref
  48.0 0.2 share.1
  48.2 22.3 %all_to_all.16 = bf16[32,16,640]{2,1,0:T(8,128)(2,1)S(1)} all-to-all(bf16[32,16,640]{2,1,0:T(8,128)(2,1)S(1)} %share.1), channel_id=1, replica_groups={{0,1,2,3,4,5,6,7,8,9,10,11,12,13,14,15,16,17,18,19,20,21,22,23,24,25,26..., dimensions={0} | all-to-all | bytes 1310720 | tf_op jit(solution)/shard_map/all_to_all | solution.py:424
  70.5 3.5 %ends.1 = (f32[512,256]{1,0:T(8,128)}, f32[16,8,256]{2,1,0:T(8,128)}, f32[8,256]{1,0:T(8,128)}, bf16[8,32,256]{2,1,0:T(8,128)(2,1)}) custom-call(bf16[512,640]{1,0:T(8,128)(2,1)S(1)} %bitcast.6, f32[512,256]{1,0:T(8,128)S(1)} %get-tuple-element.38.act_ref, bf16[512,256]{1,0:T(8,128)(2,1)S(1)} %get-tuple-element.39.dw_ref, ...), custom_call_target="tpu_custom_call" | custom-call | tf_op jit(solution)/shard_map/ends/pallas_call | solution.py:432
  74.0 8.6 %all-to-all-start.2 = ((bf16[8,32,256]{2,1,0:T(8,128)(2,1)}), bf16[8,32,256]{2,1,0:T(8,128)(2,1)S(1)}, u32[]{:S(2)}, u32[]{:S(2)}) async-start(bf16[8,32,256]{2,1,0:T(8,128)(2,1)} %get-tuple-element.43), calls=%async_computation.2 | async-start | bytes 262144 | tf_op jit(solution)/shard_map/all_to_all | solution.py:449
  82.6 4.5 %local_scan.1 = (f32[512,256]{1,0:T(8,128)S(1)}, f32[512,256]{1,0:T(8,128)S(1)}, bf16[512,128]{1,0:T(8,128)(2,1)S(1)}) custom-call(bf16[512,640]{1,0:T(8,128)(2,1)S(1)} %bitcast.7, f32[512,256]{1,0:T(8,128)S(1)} %get-tuple-element.38.act_ref, f32[16,256]{1,0:T(8,128)S(1)} %get-tuple-element.41.rate, bf16[128,2048]{1,0:T(8,128)(2,1)S(1)} %get-tuple-element.42.spread_ref, ...), custom_call_target="tpu_custom_call" | custom-call | flops 12582912 | bytes 4194304 | tf_op jit(solution)/shard_map/local_scan/pallas_call | solution.py:450
  87.1 1.3 %all-to-all-done.2.got_ref = bf16[8,32,256]{2,1,0:T(8,128)(2,1)S(1)} async-done(((bf16[8,32,256]{2,1,0:T(8,128)(2,1)}), bf16[8,32,256]{2,1,0:T(8,128)(2,1)S(1)}, u32[]{:S(2)}, u32[]{:S(2)}) %all-to-all-start.2) | async-done | bytes 131104 | tf_op jit(solution)/shard_map/all_to_all | solution.py:449
  88.4 3.1 %finish.1 = bf16[512,256]{1,0:T(8,128)(2,1)} custom-call(bf16[8,32,256]{2,1,0:T(8,128)(2,1)S(1)} %all-to-all-done.2.got_ref, bf16[512,128]{1,0:T(8,128)(2,1)S(1)} %get-tuple-element.47.maps_ref, bf16[128,2048]{1,0:T(8,128)(2,1)S(1)} %get-tuple-element.42.spread_ref, f32[512,256]{1,0:T(8,128)S(1)} %get-tuple-element.48.y_ref, ...), custom_call_target="tpu_custom_call" | custom-call | tf_op jit(solution)/shard_map/finish/pallas_call | solution.py:470
Async XLA Ops:
  0.7 8.8 %collective-permute-start = (bf16[16,256]{1,0:T(8,128)(2,1)S(1)}, bf16[16,256]{1,0:T(8,128)(2,1)S(1)}, u32[]{:S(2)}, u32[]{:S(2)}) collective-permute-start(bf16[16,256]{1,0:T(8,128)(2,1)S(1)} %slice.3), channel_id=1, source_target_pairs={{0,64},{64,128},{128,192},{192,256},{256,320},{320,384},{384,448},... | collective-permute-start | bytes 24584 | tf_op jit(solution)/shard_map/ppermute | solution.py:339
  37.3 10.8 %collective-permute-start.1 = (bf16[16,640]{1,0:T(8,128)(2,1)S(1)}, bf16[16,640]{1,0:T(8,128)(2,1)S(1)}, u32[]{:S(2)}, u32[]{:S(2)}) collective-permute-start(bf16[16,640]{1,0:T(8,128)(2,1)S(1)} %get-tuple-element.36), channel_id=1, source_target_pairs={{0,32},{1,33},{2,34},{3,35},{4,36},{5,37},{6,38},{7,39},{8,40},{9,... | collective-permute-start | bytes 61448 | tf_op jit(solution)/shard_map/ppermute | solution.py:399
  74.0 14.4 %all-to-all-start.2 = ((bf16[8,32,256]{2,1,0:T(8,128)(2,1)}), bf16[8,32,256]{2,1,0:T(8,128)(2,1)S(1)}, u32[]{:S(2)}, u32[]{:S(2)}) async-start(bf16[8,32,256]{2,1,0:T(8,128)(2,1)} %get-tuple-element.43), calls=%async_computation.2 | async-start | bytes 262144 | tf_op jit(solution)/shard_map/all_to_all | solution.py:449

commit v7 on v6

--- a/solution.py
+++ b/solution.py
@@ -12,6 +12,7 @@
 KWIDTH = 4
 LANES = 128
 CHUNKS = 8
+OWN = 16
 HEAD = 32
 LOG2E = 1.0 / math.log(2.0)
 MIB = 1 << 20
@@ -35,22 +36,32 @@
     return value / (1.0 + jnp.exp(-value))
 
 
-def put_products(low, pd, sel, maps, rank, part_ref, rows):
-    part_ref[rows, 0:rank] = jnp.dot(low, pd, preferred_element_type=F32).astype(BF16)
+def pack(low, first, second):
+    pieces = [low[:, at : at + LANES] for at in range(0, low.shape[1], LANES)]
+    return jnp.concatenate(pieces + [first + pltpu.roll(second, LANES // 2, 1)], axis=0).astype(BF16)
+
+
+def put_products(low, pd, sel, maps, part_ref, products, chosen):
+    rows = low.shape[0]
+    products[0:rows, :] = jnp.dot(low, pd, preferred_element_type=F32)
     both = lax.dot_general(low, sel, (((1,), (1,)), ((), ())), preferred_element_type=F32)
     high = both.astype(BF16).astype(F32)
     lane = lax.broadcasted_iota(jnp.int32, both.shape, 1)
-    part_ref[rows, rank : rank + LANES] = jnp.where(lane < maps, high, both - high).astype(BF16)
+    chosen[0:rows, :] = jnp.where(lane < maps, high, both - high)
+    for block in range(rows // OWN):
+        at = block * OWN
+        part_ref[block] = pack(
+            products[at : at + OWN, :], chosen[at : at + OWN // 2, :], chosen[at + OWN // 2 : at + OWN, :]
+        )
 
 
 def project_kernel(
     x_hbm, pd_hbm, ps_hbm, weight_hbm, bias_hbm, dw_hbm, log_hbm, dbias_hbm,
     act_ref, part_ref, head_ref, pd_ref, sel_ref, taps_ref, dw_ref, rate_ref, vecs_ref,
-    x_ref, log_ref, weight_ref, bias_ref, ps_ref, xs, xp, low, sems,
+    x_ref, log_ref, weight_ref, bias_ref, ps_ref, xs, xp, low, products, chosen, sems,
 ):
     rows, width = x_ref.shape
     steps = rows // CHUNKS
-    rank = pd_ref.shape[1]
     maps = ps_ref.shape[0]
     halves = width // LANES
     pairs = (
@@ -89,15 +100,14 @@
     sel_ref[0:maps, :] = ps_ref[...]
     sel_ref[maps : 2 * maps, :] = ps_ref[...]
     copies[4].wait()
-    put_products(low[...], pd_ref[...], sel_ref[...], maps, rank, part_ref, slice(0, rows))
+    put_products(low[...], pd_ref[...], sel_ref[...], maps, part_ref, products, chosen)
     copies[5].wait()
     rate_ref[...] = -jnp.exp(log_ref[...]) * LOG2E
     for copy in copies[6:]:
         copy.wait()
 
 
-def head_kernel(maps, halo_ref, head_ref, taps_ref, pd_ref, sel_ref, act_in, part_in, act_ref, part_ref, ext):
-    rank = pd_ref.shape[1]
+def head_kernel(maps, halo_ref, head_ref, taps_ref, pd_ref, sel_ref, act_in, part_in, act_ref, part_ref, ext, products, chosen):
     ext[0:8, :] = halo_ref[...].astype(F32)[-8:, :]
     ext[8:16, :] = head_ref[...]
     value = taps_ref[KWIDTH : KWIDTH + 1, :]
@@ -110,7 +120,7 @@
     for token in range(KWIDTH - 1):
         act_ref[token * CHUNKS : token * CHUNKS + 1, :] = value[token : token + 1, :]
     low = act_ref[0:HEAD, :].astype(BF16)
-    put_products(low, pd_ref[...], sel_ref[...], maps, rank, part_ref, slice(0, HEAD))
+    put_products(low, pd_ref[...], sel_ref[...], maps, part_ref, products, chosen)
 
 
 def fold(chosen, maps):
@@ -123,27 +133,29 @@
 def parted(twice, maps):
     lane = lax.broadcasted_iota(jnp.int32, twice.shape, 1)
     high = twice.astype(BF16).astype(F32)
-    return jnp.where(lane < maps, high, twice - high).astype(BF16)
-
-
-def total_kernel(rank, maps, parts_ref, mine_ref, send_ref):
+    return jnp.where(lane < maps, high, twice - high)
+
+
+def total_kernel(maps, parts_ref, mine_ref, send_ref):
     total = parts_ref[0].astype(F32)
     for source in range(1, parts_ref.shape[0]):
         total = total + parts_ref[source].astype(F32)
-    twice = fold(total[:, rank:], maps)
-    mine_ref[:, :rank] = total[:, :rank]
-    mine_ref[:, rank:] = twice
-    send_ref[:, :rank] = total[:, :rank].astype(BF16)
-    send_ref[:, rank:] = parted(twice, maps)
-
-
-def share_kernel(rank, maps, mine_ref, other_ref, ready_ref, out_ref):
+    cut = total.shape[0] - OWN // 2
+    low, packed = total[:cut, :], total[cut:, :]
+    twice = jnp.concatenate([fold(packed, maps), fold(pltpu.roll(packed, LANES // 2, 1), maps)], axis=0)
+    mine_ref[...] = jnp.concatenate([low, twice], axis=0)
+    send_ref[...] = jnp.concatenate([low, parted(twice, maps)], axis=0).astype(BF16)
+
+
+def share_kernel(maps, mine_ref, other_ref, ready_ref, out_ref):
+    cut = mine_ref.shape[0] - OWN
     other = other_ref[...].astype(F32)
-    low = (mine_ref[:, :rank] + other[:, :rank]).astype(BF16)
-    chosen = parted(mine_ref[:, rank:] + fold(other[:, rank:], maps), maps)
+    low = mine_ref[:cut, :] + other[:cut, :]
+    twice = parted(mine_ref[cut:, :] + fold(other[cut:, :], maps), maps)
+    packed = twice[: OWN // 2, :] + pltpu.roll(twice[OWN // 2 :, :], LANES // 2, 1)
+    block = jnp.concatenate([low, packed], axis=0).astype(BF16)
     for target in range(out_ref.shape[0]):
-        out_ref[target, :, :rank] = low
-        out_ref[target, :, rank:] = chosen
+        out_ref[target] = block
 
 
 def ready_kernel(mine_ref, gate_hbm, lit_ref, spread_ref, done_ref, gate_ref, sem):
@@ -163,21 +175,31 @@
 
 
 def ends_kernel(
-    rank, g_ref, act_ref, dw_ref, vecs_ref, rate, spread_ref,
-    delta_hbm, inside_hbm, before_hbm, pay_hbm,
-    delta, inside_ref, before_ref, pay_ref, drive, b_all, cum_ref, ends, sems,
+    g_ref, act_ref, dw_ref, vecs_ref, rate, spread_ref,
+    delta_hbm, inside_hbm, before_hbm, maps_hbm, pay_hbm,
+    delta, inside_ref, before_ref, maps_ref, pay_ref, low, drive, b_all, cum_ref, ends, sems,
 ):
     rows, width = act_ref.shape
     steps = rows // CHUNKS
     halves = width // LANES
-    z = jnp.dot(g_ref[:, :rank], dw_ref[...], preferred_element_type=F32) + vecs_ref[0:1, :]
+    for block in range(g_ref.shape[0]):
+        at = slice(block * OWN, (block + 1) * OWN)
+        for piece in range(low.shape[1] // LANES):
+            low[at, piece * LANES : (piece + 1) * LANES] = g_ref[block, piece * OWN : (piece + 1) * OWN, :]
+        packed = g_ref[block].astype(F32)[-(OWN // 2) :, :]
+        maps_ref[at, :] = jnp.concatenate([packed, pltpu.roll(packed, LANES // 2, 1)], axis=0).astype(BF16)
+    z = jnp.dot(low[...], dw_ref[...], preferred_element_type=F32) + vecs_ref[0:1, :]
     step_size = jnp.maximum(z, 0.0) + jnp.log1p(jnp.exp(-jnp.abs(z)))
     delta[...] = step_size
-    pairs = ((delta, delta_hbm), (inside_ref, inside_hbm), (before_ref, before_hbm), (pay_ref, pay_hbm))
+    pairs = (
+        (delta, delta_hbm), (maps_ref, maps_hbm),
+        (inside_ref, inside_hbm), (before_ref, before_hbm), (pay_ref, pay_hbm),
+    )
     copies = [pltpu.make_async_copy(source, target, sems.at[i]) for i, (source, target) in enumerate(pairs)]
     copies[0].start()
+    copies[1].start()
     drive[...] = step_size * act_ref[...]
-    b_all[...] = jnp.dot(g_ref[:, rank:], spread_ref[...], preferred_element_type=F32)
+    b_all[...] = jnp.dot(maps_ref[...], spread_ref[...], preferred_element_type=F32)
     chunk = lax.broadcasted_iota(jnp.int32, (CHUNKS, LANES), 0)
     zero = jnp.zeros((CHUNKS, LANES), F32)
 
@@ -222,8 +244,8 @@
         before_ref[:, cols] = jnp.where(chunk >= 1, pltpu.roll(sums[-1], 1, 0), 0.0)
         ends[STATE : STATE + 1, cols] = sums[-1][CHUNKS - 1 :, :]
 
-    copies[1].start()
     copies[2].start()
+    copies[3].start()
     me = lax.axis_index("ctx")
     value = ends[0:STATE, :]
     total = jnp.broadcast_to(ends[STATE : STATE + 1, :], value.shape)
@@ -234,28 +256,32 @@
         use = target > me
         pay_ref[target, 0:16, :] = jnp.where(use, value, 0.0).astype(BF16)
         pay_ref[target, 16:32, :] = jnp.where(use, tail, 0.0).astype(BF16)
-    copies[3].start()
+    copies[4].start()
     for copy in copies:
         copy.wait()
 
 
 def local_kernel(
-    rank, g_ref, act_ref, rate, spread_ref, delta_hbm, inside_hbm, before_hbm, gain_hbm,
+    act_ref, rate, spread_ref, delta_hbm, inside_hbm, before_hbm, maps_hbm, gain_hbm,
     y_ref, cum_ref, maps_ref,
-    b_all, c_all, delta, inside_ref, before_ref, gain_ref, sems,
+    b_all, c_all, delta, inside_ref, before_ref, both_ref, gain_ref, sems,
 ):
     rows, width = act_ref.shape
     steps = rows // CHUNKS
     halves = width // LANES
-    pairs = ((delta_hbm, delta), (inside_hbm, inside_ref), (before_hbm, before_ref), (gain_hbm, gain_ref))
+    pairs = (
+        (maps_hbm, both_ref), (delta_hbm, delta),
+        (inside_hbm, inside_ref), (before_hbm, before_ref), (gain_hbm, gain_ref),
+    )
     copies = [pltpu.make_async_copy(source, target, sems.at[i]) for i, (source, target) in enumerate(pairs)]
     for copy in copies:
         copy.start()
-    maps = g_ref[:, rank:]
+    copies[0].wait()
+    maps = both_ref[...]
     b_all[...] = jnp.dot(maps, spread_ref[...], preferred_element_type=F32)
     maps_ref[...] = pltpu.roll(maps.astype(F32), LANES - STATE, 1).astype(BF16)
     c_all[...] = jnp.dot(maps_ref[...], spread_ref[...], preferred_element_type=F32)
-    for copy in copies:
+    for copy in copies[1:]:
         copy.wait()
     for half in range(halves):
         cols = slice(half * LANES, (half + 1) * LANES)
@@ -333,7 +359,9 @@
     wide = rank + LANES
     cells = rows * width * STATE
     tile = jax.ShapeDtypeStruct((rows, width), F32)
-    part_shape = jax.ShapeDtypeStruct((rows, wide), BF16)
+    near = n_ch // 2
+    tall = OWN * rank // LANES + OWN // 2
+    part_shape = jax.ShapeDtypeStruct((near, tall, LANES), BF16)
     big = pltpu.VMEM((rows, STATE * LANES), F32)
 
     halo = lax.ppermute(mamba_in[rows - 16 :], "ctx", [(i, i + 1) for i in range(n_ctx - 1)])
@@ -361,6 +389,8 @@
             pltpu.VMEM((halves, rows + 8, LANES), F32),
             pltpu.VMEM((halves, (steps + KWIDTH - 1) * CHUNKS, LANES), F32),
             pltpu.VMEM((rows, width), BF16),
+            pltpu.VMEM((rows, rank), F32),
+            pltpu.VMEM((rows, LANES), F32),
             pltpu.SemaphoreType.DMA((8,)),
         ],
         compiler_params=pltpu.CompilerParams(vmem_limit_bytes=16 * MIB),
@@ -379,18 +409,20 @@
         out_shape=(tile, part_shape),
         in_specs=vmem(7),
         out_specs=tuple(vmem(2)),
-        scratch_shapes=[pltpu.VMEM((16, width), F32)],
+        scratch_shapes=[
+            pltpu.VMEM((16, width), F32),
+            pltpu.VMEM((HEAD, rank), F32),
+            pltpu.VMEM((HEAD, LANES), F32),
+        ],
         compiler_params=pltpu.CompilerParams(vmem_limit_bytes=16 * MIB),
         name="first_rows",
     )(halo, head, taps, pd, sel, act, part)
 
-    near = n_ch // 2
     groups = [list(range(near)), list(range(near, n_ch))]
-    own = rows // near
-    parts = lax.all_to_all(part.reshape(near, own, wide), "ch", 0, 0, axis_index_groups=groups)
+    parts = lax.all_to_all(part, "ch", 0, 0, axis_index_groups=groups)
     mine, send = pl.pallas_call(
-        functools.partial(total_kernel, rank, maps),
-        out_shape=(jax.ShapeDtypeStruct((own, wide), F32), jax.ShapeDtypeStruct((own, wide), BF16)),
+        functools.partial(total_kernel, maps),
+        out_shape=tuple(jax.ShapeDtypeStruct((tall + OWN // 2, LANES), kind) for kind in (F32, BF16)),
         in_specs=vmem(1),
         out_specs=tuple(vmem(2)),
         compiler_params=pltpu.CompilerParams(vmem_limit_bytes=16 * MIB),
@@ -414,59 +446,61 @@
         name="ready",
     )(mine, *stay(mamba_gate))
     totals = pl.pallas_call(
-        functools.partial(share_kernel, rank, maps),
+        functools.partial(share_kernel, maps),
         out_shape=jax.ShapeDtypeStruct(parts.shape, BF16),
         in_specs=vmem(3),
         out_specs=vmem(1)[0],
         compiler_params=pltpu.CompilerParams(vmem_limit_bytes=16 * MIB),
         name="share",
     )(mine, other, done)
-    gathered = lax.all_to_all(totals, "ch", 0, 0, axis_index_groups=groups).reshape(rows, wide)
+    gathered = lax.all_to_all(totals, "ch", 0, 0, axis_index_groups=groups)
 
     sent = (
         ((rows, width), F32),
         ((STATE, CHUNKS, width), F32),
         ((CHUNKS, width), F32),
+        ((rows, LANES), BF16),
         ((n_ctx, 2 * STATE, width), BF16),
     )
-    delta, inside, before, pay = pl.pallas_call(
-        functools.partial(ends_kernel, rank),
+    delta, inside, before, maps_all, pay = pl.pallas_call(
+        ends_kernel,
         out_shape=tuple(pltpu.HBM(*kept) for kept in sent),
         in_specs=vmem(6),
-        out_specs=tuple(hbm(4)),
+        out_specs=tuple(hbm(5)),
         scratch_shapes=[
             *(pltpu.VMEM(*kept) for kept in sent),
+            pltpu.VMEM((rows, rank), BF16),
             pltpu.VMEM((rows, width), F32),
             big,
             pltpu.VMEM((rows, width), F32),
             pltpu.VMEM((STATE + 8, width), F32),
-            pltpu.SemaphoreType.DMA((4,)),
+            pltpu.SemaphoreType.DMA((5,)),
         ],
         compiler_params=pltpu.CompilerParams(vmem_limit_bytes=16 * MIB),
         name="ends",
     )(gathered, act, dw, vecs, rate, spread)
 
     got = lax.all_to_all(pay, "ctx", 0, 0)
-    y_local, cum, maps_all = pl.pallas_call(
-        functools.partial(local_kernel, rank),
+    y_local, cum, turned = pl.pallas_call(
+        local_kernel,
         out_shape=(
             tile,
             tile,
             jax.ShapeDtypeStruct((rows, LANES), BF16),
         ),
-        in_specs=vmem(4) + hbm(4),
+        in_specs=vmem(3) + hbm(5),
         out_specs=tuple(vmem(3)),
         scratch_shapes=[
             big,
             big,
-            *(pltpu.VMEM(*kept) for kept in sent[:3]),
+            *(pltpu.VMEM(*kept) for kept in sent[:4]),
             pltpu.VMEM((1, width), F32),
-            pltpu.SemaphoreType.DMA((4,)),
+            pltpu.SemaphoreType.DMA((5,)),
         ],
         compiler_params=pltpu.CompilerParams(vmem_limit_bytes=24 * MIB),
         cost_estimate=pl.CostEstimate(flops=6 * cells, bytes_accessed=8 * rows * width * 4, transcendentals=cells),
         name="local_scan",
-    )(gathered, act, rate, spread, *stay(delta, inside, before, skip_gain[None, :]))
+    )(act, rate, spread, *stay(delta, inside, before, maps_all, skip_gain[None, :]))
     return pl.pallas_call(
         finish_kernel,
         out_shape=jax.ShapeDtypeStruct((rows, width), BF16),
@@ -481,7 +515,7 @@
         ],
         compiler_params=pltpu.CompilerParams(vmem_limit_bytes=16 * MIB),
         name="finish",
-    )(got, maps_all, spread, y_local, cum, rate, lit)
+    )(got, turned, spread, y_local, cum, rate, lit)
 
 
 def solution(mesh):

time: 91.9 us -> 89.2 us (0.971)
  blocking collectives: 49.7 us -> 46.8 us
    all_to_all x2, blocking collectives: 49.7 us -> 46.8 us  [the longest x1 25.5 us: on_device(): parts = lax.all_to_all(part, 'ch', 0, 0, axis_index_groups=groups)]
  transfers between devices with their start and end apart: 3 -> 3, of which waited for: 2 -> 2; matrix products, arithmetic and copies ran while one was open for 0% -> 0% of each run, Pallas kernels for 8% -> 9%
where the time goes in v7:
time: 89.2 us; the launch traced here: 88.8 us
  blocking collectives  46.8 us (52%)
  starting transfers between devices  23.4 us (26%)
  Pallas kernels  15.1 us (17%)
  waiting for transfers between devices  2.69 us (3%)
    all_to_all x1, blocking collectives, on_device(): parts = lax.all_to_all(part, 'ch', 0, 0, axis_index_groups=groups)  25.5 us
    all_to_all x1, blocking collectives, on_device(): gathered = lax.all_to_all(totals, 'ch', 0, 0, axis_index_groups=groups)  21.3 us
    ppermute x1, starting transfers between devices, on_device(): lax.ppermute(send, 'ch', [(i, (i + near) % n_ch) for i in range(n_ch)])  10.2 us
    all_to_all x1, starting transfers between devices, on_device(): got = lax.all_to_all(pay, 'ctx', 0, 0)  7.88 us
    ppermute x1, starting transfers between devices, on_device(): lax.ppermute(mamba_in[rows - 16:], 'ctx', [(i, i + 1) for i in range(n_ct...  5.38 us
    pallas_call x1, Pallas kernels, on_device(): pl.pallas_call(local_kernel, out_shape=(tile, tile, jax.ShapeDtypeStruct(...  4.46 us
    pallas_call x1, Pallas kernels, on_device(): pl.pallas_call(ends_kernel, out_shape=tuple((pltpu.HBM(*kept) for kept in...  3.56 us
    pallas_call x1, Pallas kernels, on_device(): pl.pallas_call(finish_kernel, out_shape=jax.ShapeDtypeStruct((rows, width...  3.06 us
  transfers between devices with their start and end apart: 3, of which 2 were waited for; matrix products, arithmetic and copies ran while one was open for 0% of the time, Pallas kernels for 9%

profile of v7, /device:TPU:1, one launch (start us, length us, event | category | flops | bytes accessed | tf_op | source)
XLA Modules:
  0.0 88.8 jit_solution(4292078828313833961)
XLA Ops:
  0.0 0.7 slice.3
  0.7 5.4 %collective-permute-start = (bf16[16,256]{1,0:T(8,128)(2,1)S(1)}, bf16[16,256]{1,0:T(8,128)(2,1)S(1)}, u32[]{:S(2)}, u32[]{:S(2)}) collective-permute-start(bf16[16,256]{1,0:T(8,128)(2,1)S(1)} %slice.3), channel_id=1, source_target_pairs={{0,64},{64,128},{128,192},{192,256},{256,320},{320,384},{384,448},... | collective-permute-start | bytes 24584 | tf_op jit(solution)/shard_map/ppermute | solution.py:367
  6.1 2.1 %project.1 = (f32[512,256]{1,0:T(8,128)S(1)}, bf16[32,72,128]{2,1,0:T(8,128)(2,1)S(1)}, f32[8,256]{1,0:T(8,128)S(1)}, bf16[256,512]{1,0:T(8,128)(2,1)S(1)}, bf16...) custom-call(bf16[512,256]{1,0:T(8,128)(2,1)} %x_hbm.1, ...), custom_call_target="tpu_custom_call" | custom-call | flops 167772160 | bytes 2097152 | tf_op jit(solution)/shard_map/project/pallas_call | solution.py:368
  8.2 1.3 %collective-permute-done.halo_ref = bf16[16,256]{1,0:T(8,128)(2,1)S(1)} collective-permute-done((bf16[16,256]{1,0:T(8,128)(2,1)S(1)}, bf16[16,256]{1,0:T(8,128)(2,1)S(1)}, u32[]{:S(2)}, u32[]{:S(2)}) %collective-permute-start) | collective-permute-done | bytes 8224 | tf_op jit(solution)/shard_map/ppermute | solution.py:367
  9.5 0.3 first_rows.1
  9.8 25.5 %all_to_all.15.parts_ref = bf16[32,72,128]{2,1,0:T(8,128)(2,1)S(1)} all-to-all(bf16[32,72,128]{2,1,0:T(8,128)(2,1)S(1)} %get-tuple-element.35), channel_id=1, replica_groups={{0,1,2,3,4,5,6,7,8,9,10,11,12,13,14,15,16,17,18,19,20,21,22,23,24,25,26..., dimensions={0} | all-to-all | bytes 1179648 | tf_op jit(solution)/shard_map/all_to_all | solution.py:422
  35.3 0.2 total.1
  35.5 10.2 %collective-permute-start.1 = (bf16[80,128]{1,0:T(8,128)(2,1)S(1)}, bf16[80,128]{1,0:T(8,128)(2,1)S(1)}, u32[]{:S(2)}, u32[]{:S(2)}) collective-permute-start(bf16[80,128]{1,0:T(8,128)(2,1)S(1)} %get-tuple-element.37), channel_id=1, source_target_pairs={{0,32},{1,33},{2,34},{3,35},{4,36},{5,37},{6,38},{7,39},{8,40},{9,... | collective-permute-start | bytes 61448 | tf_op jit(solution)/shard_map/ppermute | solution.py:431
  45.7 1.1 %ready.1 = (f32[512,256]{1,0:T(8,128)S(1)}, bf16[128,2048]{1,0:T(8,128)(2,1)S(1)}, f32[8,128]{1,0:T(8,128)S(1)}) custom-call(f32[80,128]{1,0:T(8,128)S(1)} %get-tuple-element.36.mine_ref, bf16[512,256]{1,0:T(8,128)(2,1)} %gate_hbm.1), custom_call_target="tpu_custom_call" | custom-call | flops 2097152 | bytes 1048576 | tf_op jit(solution)/shard_map/ready/pallas_call | solution.py:432
  46.8 0.0 collective-permute-done.1.other_ref
  46.9 0.2 share.1
  47.1 21.3 %all_to_all.16.g_ref = bf16[32,72,128]{2,1,0:T(8,128)(2,1)S(1)} all-to-all(bf16[32,72,128]{2,1,0:T(8,128)(2,1)S(1)} %share.1), channel_id=1, replica_groups={{0,1,2,3,4,5,6,7,8,9,10,11,12,13,14,15,16,17,18,19,20,21,22,23,24,25,26..., dimensions={0} | all-to-all | bytes 1179648 | tf_op jit(solution)/shard_map/all_to_all | solution.py:456
  68.4 3.6 %ends.1 = (f32[512,256]{1,0:T(8,128)}, f32[16,8,256]{2,1,0:T(8,128)}, f32[8,256]{1,0:T(8,128)}, bf16[512,128]{1,0:T(8,128)(2,1)}, bf16[8,32,256]{2,1,0:T(8,128)(2,1)}) custom-call(bf16[32,72,128]{2,1,0:T(8,128)(2,1)S(1)} %all_to_all.16.g_ref, f32[512,256]{1,0:T(8,128)S(1)} %get-tuple-element.39.act_ref, bf16[512,256]{1,0:T(8,128)(2,1)S(1)} %get-tuple-element.40.dw_ref, ...), custom_call_target="tpu_custom_call" | custom-call | tf_op jit(solution)/shard_map/ends/pallas_call | solution.py:465
  72.0 7.9 %all-to-all-start.2 = ((bf16[8,32,256]{2,1,0:T(8,128)(2,1)}), bf16[8,32,256]{2,1,0:T(8,128)(2,1)S(1)}, u32[]{:S(2)}, u32[]{:S(2)}) async-start(bf16[8,32,256]{2,1,0:T(8,128)(2,1)} %get-tuple-element.44), calls=%async_computation.2 | async-start | bytes 262144 | tf_op jit(solution)/shard_map/all_to_all | solution.py:483
  79.9 4.5 %local_scan.1 = (f32[512,256]{1,0:T(8,128)S(1)}, f32[512,256]{1,0:T(8,128)S(1)}, bf16[512,128]{1,0:T(8,128)(2,1)S(1)}) custom-call(f32[512,256]{1,0:T(8,128)S(1)} %get-tuple-element.39.act_ref, f32[16,256]{1,0:T(8,128)S(1)} %get-tuple-element.42.rate, bf16[128,2048]{1,0:T(8,128)(2,1)S(1)} %get-tuple-element.43.spread_ref, ...), custom_call_target="tpu_custom_call" | custom-call | flops 12582912 | bytes 4194304 | tf_op jit(solution)/shard_map/local_scan/pallas_call | solution.py:484
  84.4 1.3 %all-to-all-done.2.got_ref = bf16[8,32,256]{2,1,0:T(8,128)(2,1)S(1)} async-done(((bf16[8,32,256]{2,1,0:T(8,128)(2,1)}), bf16[8,32,256]{2,1,0:T(8,128)(2,1)S(1)}, u32[]{:S(2)}, u32[]{:S(2)}) %all-to-all-start.2) | async-done | bytes 131104 | tf_op jit(solution)/shard_map/all_to_all | solution.py:483
  85.7 3.1 %finish.1 = bf16[512,256]{1,0:T(8,128)(2,1)} custom-call(bf16[8,32,256]{2,1,0:T(8,128)(2,1)S(1)} %all-to-all-done.2.got_ref, bf16[512,128]{1,0:T(8,128)(2,1)S(1)} %get-tuple-element.49.maps_ref, bf16[128,2048]{1,0:T(8,128)(2,1)S(1)} %get-tuple-element.43.spread_ref, f32[512,256]{1,0:T(8,128)S(1)} %get-tuple-element.50.y_ref, ...), custom_call_target="tpu_custom_call" | custom-call | tf_op jit(solution)/shard_map/finish/pallas_call | solution.py:504
Async XLA Ops:
  0.7 8.8 %collective-permute-start = (bf16[16,256]{1,0:T(8,128)(2,1)S(1)}, bf16[16,256]{1,0:T(8,128)(2,1)S(1)}, u32[]{:S(2)}, u32[]{:S(2)}) collective-permute-start(bf16[16,256]{1,0:T(8,128)(2,1)S(1)} %slice.3), channel_id=1, source_target_pairs={{0,64},{64,128},{128,192},{192,256},{256,320},{320,384},{384,448},... | collective-permute-start | bytes 24584 | tf_op jit(solution)/shard_map/ppermute | solution.py:367
  35.5 11.3 %collective-permute-start.1 = (bf16[80,128]{1,0:T(8,128)(2,1)S(1)}, bf16[80,128]{1,0:T(8,128)(2,1)S(1)}, u32[]{:S(2)}, u32[]{:S(2)}) collective-permute-start(bf16[80,128]{1,0:T(8,128)(2,1)S(1)} %get-tuple-element.37), channel_id=1, source_target_pairs={{0,32},{1,33},{2,34},{3,35},{4,36},{5,37},{6,38},{7,39},{8,40},{9,... | collective-permute-start | bytes 61448 | tf_op jit(solution)/shard_map/ppermute | solution.py:431
  72.0 13.7 %all-to-all-start.2 = ((bf16[8,32,256]{2,1,0:T(8,128)(2,1)}), bf16[8,32,256]{2,1,0:T(8,128)(2,1)S(1)}, u32[]{:S(2)}, u32[]{:S(2)}) async-start(bf16[8,32,256]{2,1,0:T(8,128)(2,1)} %get-tuple-element.44), calls=%async_computation.2 | async-start | bytes 262144 | tf_op jit(solution)/shard_map/all_to_all | solution.py:483

commit v8 on v7

--- a/solution.py
+++ b/solution.py
@@ -56,9 +56,9 @@
 
 
 def project_kernel(
-    x_hbm, pd_hbm, ps_hbm, weight_hbm, bias_hbm, dw_hbm, log_hbm, dbias_hbm,
-    act_ref, part_ref, head_ref, pd_ref, sel_ref, taps_ref, dw_ref, rate_ref, vecs_ref,
-    x_ref, log_ref, weight_ref, bias_ref, ps_ref, xs, xp, low, products, chosen, sems,
+    x_hbm, pd_hbm, ps_hbm, weight_hbm, bias_hbm,
+    act_ref, part_ref, head_ref, pd_ref, sel_ref, taps_ref,
+    x_ref, weight_ref, bias_ref, ps_ref, xs, xp, low, products, chosen, sems,
 ):
     rows, width = x_ref.shape
     steps = rows // CHUNKS
@@ -66,7 +66,6 @@
     halves = width // LANES
     pairs = (
         (x_hbm, x_ref), (weight_hbm, weight_ref), (bias_hbm, bias_ref), (ps_hbm, ps_ref), (pd_hbm, pd_ref),
-        (log_hbm, log_ref), (dw_hbm, dw_ref), (dbias_hbm, vecs_ref.at[0:1]),
     )
     copies = [pltpu.make_async_copy(source, target, sems.at[i]) for i, (source, target) in enumerate(pairs)]
     for copy in copies:
@@ -101,10 +100,6 @@
     sel_ref[maps : 2 * maps, :] = ps_ref[...]
     copies[4].wait()
     put_products(low[...], pd_ref[...], sel_ref[...], maps, part_ref, products, chosen)
-    copies[5].wait()
-    rate_ref[...] = -jnp.exp(log_ref[...]) * LOG2E
-    for copy in copies[6:]:
-        copy.wait()
 
 
 def head_kernel(maps, halo_ref, head_ref, taps_ref, pd_ref, sel_ref, act_in, part_in, act_ref, part_ref, ext, products, chosen):
@@ -158,15 +153,23 @@
         out_ref[target] = block
 
 
-def ready_kernel(mine_ref, gate_hbm, lit_ref, spread_ref, done_ref, gate_ref, sem):
-    copy = pltpu.make_async_copy(gate_hbm, gate_ref, sem)
-    copy.start()
+def ready_kernel(
+    mine_ref, gate_hbm, dw_hbm, log_hbm, bias_hbm,
+    lit_ref, spread_ref, done_ref, dw_ref, rate_ref, bias_ref,
+    gate_ref, log_ref, sems,
+):
+    pairs = ((gate_hbm, gate_ref), (dw_hbm, dw_ref), (log_hbm, log_ref), (bias_hbm, bias_ref.at[0:1]))
+    copies = [pltpu.make_async_copy(source, target, sems.at[i]) for i, (source, target) in enumerate(pairs)]
+    for copy in copies:
+        copy.start()
     source = lax.broadcasted_iota(jnp.int32, spread_ref.shape, 0)
     group = lax.broadcasted_iota(jnp.int32, spread_ref.shape, 1) >> 7
     hit = (source == group) | (source == group + 2 * STATE)
     spread_ref[...] = jnp.where(hit, 1.0, 0.0).astype(BF16)
     done_ref[...] = jnp.zeros_like(done_ref)
-    copy.wait()
+    for copy in copies:
+        copy.wait()
+    rate_ref[...] = -jnp.exp(log_ref[...]) * LOG2E
     lit_ref[...] = silu(gate_ref[...].astype(F32))
 
 
@@ -225,7 +228,7 @@
                 for n in range(STATE)
             ]
 
-        states = lax.fori_loop(0, steps, gather, [zero] * STATE, unroll=8)
+        states = lax.fori_loop(0, steps, gather, [zero] * STATE, unroll=16)
         sums = [total]
         shift = 1
         while shift < CHUNKS:
@@ -247,15 +250,17 @@
     copies[2].start()
     copies[3].start()
     me = lax.axis_index("ctx")
-    value = ends[0:STATE, :]
-    total = jnp.broadcast_to(ends[STATE : STATE + 1, :], value.shape)
-    high = total.astype(BF16).astype(F32)
-    first = lax.broadcasted_iota(jnp.int32, value.shape, 0) == 0
-    tail = jnp.where(first, high, total - high)
+    row = lax.broadcasted_iota(jnp.int32, (CHUNKS, LANES), 0)
+    pieces, tail = [], zero
+    for half in range(halves):
+        cols = slice(half * LANES, (half + 1) * LANES)
+        pieces.append(ends[0:STATE, cols])
+        total = jnp.broadcast_to(ends[STATE : STATE + 1, cols], tail.shape)
+        high = total.astype(BF16).astype(F32)
+        tail = jnp.where(row == 2 * half, high, jnp.where(row == 2 * half + 1, total - high, tail))
+    block = jnp.concatenate(pieces + [tail], axis=0)
     for target in range(pay_ref.shape[0]):
-        use = target > me
-        pay_ref[target, 0:16, :] = jnp.where(use, value, 0.0).astype(BF16)
-        pay_ref[target, 16:32, :] = jnp.where(use, tail, 0.0).astype(BF16)
+        pay_ref[target] = jnp.where(target > me, block, 0.0).astype(BF16)
     copies[4].start()
     for copy in copies:
         copy.wait()
@@ -316,12 +321,16 @@
     steps = rows // CHUNKS
     halves = width // LANES
     c_all[...] = jnp.dot(maps_ref[...], spread_ref[...], preferred_element_type=F32)
-    incoming = jnp.zeros((STATE, width), F32)
+    incoming = [jnp.zeros((STATE, LANES), F32)] * halves
     for source in range(got_ref.shape[0] - 1):
-        tail = got_ref[source, 16:32, :].astype(F32)
-        decay = jnp.exp2(rate[...] * (tail[0:1, :] + tail[1:2, :]))
-        incoming = decay * incoming + got_ref[source, 0:16, :].astype(F32)
-    carry[...] = incoming
+        block = got_ref[source].astype(F32)
+        tail = block[halves * STATE :, :]
+        for half in range(halves):
+            total = tail[2 * half : 2 * half + 1, :] + tail[2 * half + 1 : 2 * half + 2, :]
+            decay = jnp.exp2(rate[:, half * LANES : (half + 1) * LANES] * total)
+            incoming[half] = decay * incoming[half] + block[half * STATE : (half + 1) * STATE, :]
+    for half in range(halves):
+        carry[:, half * LANES : (half + 1) * LANES] = incoming[half]
     leaving = []
     for half in range(halves):
         cols = slice(half * LANES, (half + 1) * LANES)
@@ -338,7 +347,7 @@
             ys[half, pl.ds(step, CHUNKS, stride=steps), :] = out
             return 0
 
-        lax.fori_loop(0, steps, correct, 0, unroll=8)
+        lax.fori_loop(0, steps, correct, 0, unroll=16)
         out_ref[half] = (ys[half] * lit_ref[:, cols]).astype(BF16)
         copy = pltpu.make_async_copy(out_ref.at[half], out_hbm.at[:, cols], sems.at[half])
         copy.start()
@@ -365,7 +374,7 @@
     big = pltpu.VMEM((rows, STATE * LANES), F32)
 
     halo = lax.ppermute(mamba_in[rows - 16 :], "ctx", [(i, i + 1) for i in range(n_ctx - 1)])
-    act, part, head, pd, sel, taps, dw, rate, vecs = pl.pallas_call(
+    act, part, head, pd, sel, taps = pl.pallas_call(
         project_kernel,
         out_shape=(
             tile,
@@ -374,15 +383,11 @@
             jax.ShapeDtypeStruct(proj_delta.shape, BF16),
             jax.ShapeDtypeStruct((LANES, width), BF16),
             jax.ShapeDtypeStruct((8, width), F32),
-            jax.ShapeDtypeStruct(delta_weight.shape, BF16),
-            jax.ShapeDtypeStruct((STATE, width), F32),
-            jax.ShapeDtypeStruct((8, width), F32),
         ),
-        in_specs=hbm(8),
-        out_specs=tuple(vmem(9)),
+        in_specs=hbm(5),
+        out_specs=tuple(vmem(6)),
         scratch_shapes=[
             pltpu.VMEM((rows, width), BF16),
-            pltpu.VMEM((STATE, width), F32),
             pltpu.VMEM((KWIDTH, width), F32),
             pltpu.VMEM((1, width), F32),
             pltpu.VMEM((maps, width), BF16),
@@ -391,7 +396,7 @@
             pltpu.VMEM((rows, width), BF16),
             pltpu.VMEM((rows, rank), F32),
             pltpu.VMEM((rows, LANES), F32),
-            pltpu.SemaphoreType.DMA((8,)),
+            pltpu.SemaphoreType.DMA((5,)),
         ],
         compiler_params=pltpu.CompilerParams(vmem_limit_bytes=16 * MIB),
         cost_estimate=pl.CostEstimate(
@@ -401,7 +406,6 @@
     )(
         *stay(
             mamba_in, proj_delta, proj_select.T, conv_weight, conv_bias[None, :],
-            delta_weight, decay_log, delta_bias[None, :],
         )
     )
     act, part = pl.pallas_call(
@@ -429,22 +433,29 @@
         name="total",
     )(parts)
     other = lax.ppermute(send, "ch", [(i, (i + near) % n_ch) for i in range(n_ch)])
-    lit, spread, done = pl.pallas_call(
+    lit, spread, done, dw, rate, vecs = pl.pallas_call(
         ready_kernel,
         out_shape=(
             tile,
             jax.ShapeDtypeStruct((LANES, STATE * LANES), BF16),
             jax.ShapeDtypeStruct((8, LANES), F32),
+            jax.ShapeDtypeStruct(delta_weight.shape, BF16),
+            jax.ShapeDtypeStruct((STATE, width), F32),
+            jax.ShapeDtypeStruct((8, width), F32),
         ),
-        in_specs=vmem(1) + hbm(1),
-        out_specs=tuple(vmem(3)),
-        scratch_shapes=[pltpu.VMEM((rows, width), BF16), pltpu.SemaphoreType.DMA],
+        in_specs=vmem(1) + hbm(4),
+        out_specs=tuple(vmem(6)),
+        scratch_shapes=[
+            pltpu.VMEM((rows, width), BF16),
+            pltpu.VMEM((STATE, width), F32),
+            pltpu.SemaphoreType.DMA((4,)),
+        ],
         compiler_params=pltpu.CompilerParams(vmem_limit_bytes=16 * MIB),
         cost_estimate=pl.CostEstimate(
             flops=16 * rows * width, bytes_accessed=8 * rows * width, transcendentals=rows * width
         ),
         name="ready",
-    )(mine, *stay(mamba_gate))
+    )(mine, *stay(mamba_gate, delta_weight, decay_log, delta_bias[None, :]))
     totals = pl.pallas_call(
         functools.partial(share_kernel, maps),
         out_shape=jax.ShapeDtypeStruct(parts.shape, BF16),
@@ -460,7 +471,7 @@
         ((STATE, CHUNKS, width), F32),
         ((CHUNKS, width), F32),
         ((rows, LANES), BF16),
-        ((n_ctx, 2 * STATE, width), BF16),
+        ((n_ctx, halves * STATE + CHUNKS, LANES), BF16),
     )
     delta, inside, before, maps_all, pay = pl.pallas_call(
         ends_kernel,

time: 89.2 us -> 88.3 us (0.990)
  no operation moved by 1% of the time
where the time goes in v8:
time: 88.3 us; the launch traced here: 87.9 us
  blocking collectives  46.7 us (53%)
  starting transfers between devices  23.4 us (27%)
  Pallas kernels  14.9 us (17%)
  waiting for transfers between devices  2.14 us (2%)
    all_to_all x1, blocking collectives, on_device(): parts = lax.all_to_all(part, 'ch', 0, 0, axis_index_groups=groups)  25.5 us
    all_to_all x1, blocking collectives, on_device(): gathered = lax.all_to_all(totals, 'ch', 0, 0, axis_index_groups=groups)  21.2 us
    ppermute x1, starting transfers between devices, on_device(): lax.ppermute(send, 'ch', [(i, (i + near) % n_ch) for i in range(n_ch)])  10.2 us
    all_to_all x1, starting transfers between devices, on_device(): got = lax.all_to_all(pay, 'ctx', 0, 0)  7.86 us
    ppermute x1, starting transfers between devices, on_device(): lax.ppermute(mamba_in[rows - 16:], 'ctx', [(i, i + 1) for i in range(n_ct...  5.38 us
    pallas_call x1, Pallas kernels, on_device(): pl.pallas_call(local_kernel, out_shape=(tile, tile, jax.ShapeDtypeStruct(...  4.46 us
    pallas_call x1, Pallas kernels, on_device(): pl.pallas_call(ends_kernel, out_shape=tuple((pltpu.HBM(*kept) for kept in...  3.46 us
    pallas_call x1, Pallas kernels, on_device(): pl.pallas_call(finish_kernel, out_shape=jax.ShapeDtypeStruct((rows, width...  2.93 us
  transfers between devices with their start and end apart: 3, of which 2 were waited for; matrix products, arithmetic and copies ran while one was open for 0% of the time, Pallas kernels for 9%

profile of v8, /device:TPU:1, one launch (start us, length us, event | category | flops | bytes accessed | tf_op | source)
XLA Modules:
  0.0 87.9 jit_solution(308852912914202643)
XLA Ops:
  0.0 0.7 slice.3
  0.7 5.4 %collective-permute-start = (bf16[16,256]{1,0:T(8,128)(2,1)S(1)}, bf16[16,256]{1,0:T(8,128)(2,1)S(1)}, u32[]{:S(2)}, u32[]{:S(2)}) collective-permute-start(bf16[16,256]{1,0:T(8,128)(2,1)S(1)} %slice.3), channel_id=1, source_target_pairs={{0,64},{64,128},{128,192},{192,256},{256,320},{320,384},{384,448},... | collective-permute-start | bytes 24584 | tf_op jit(solution)/shard_map/ppermute | solution.py:376
  6.1 2.1 %project.1 = (f32[512,256]{1,0:T(8,128)S(1)}, bf16[32,72,128]{2,1,0:T(8,128)(2,1)S(1)}, f32[8,256]{1,0:T(8,128)S(1)}, bf16[256,512]{1,0:T(8,128)(2,1)S(1)}, bf16...) custom-call(bf16[512,256]{1,0:T(8,128)(2,1)} %x_hbm.1, bf16[256,512]{1,0:T(8,128)(2,1)} %pd_hbm.1, ...), custom_call_target="tpu_custom_call" | custom-call | flops 167772160 | bytes 2097152 | tf_op jit(solution)/shard_map/project/pallas_call | solution.py:377
  8.2 1.4 %collective-permute-done.halo_ref = bf16[16,256]{1,0:T(8,128)(2,1)S(1)} collective-permute-done((bf16[16,256]{1,0:T(8,128)(2,1)S(1)}, bf16[16,256]{1,0:T(8,128)(2,1)S(1)}, u32[]{:S(2)}, u32[]{:S(2)}) %collective-permute-start) | collective-permute-done | bytes 8224 | tf_op jit(solution)/shard_map/ppermute | solution.py:376
  9.5 0.3 first_rows.1
  9.8 25.5 %all_to_all.15.parts_ref = bf16[32,72,128]{2,1,0:T(8,128)(2,1)S(1)} all-to-all(bf16[32,72,128]{2,1,0:T(8,128)(2,1)S(1)} %get-tuple-element.35), channel_id=1, replica_groups={{0,1,2,3,4,5,6,7,8,9,10,11,12,13,14,15,16,17,18,19,20,21,22,23,24,25,26..., dimensions={0} | all-to-all | bytes 1179648 | tf_op jit(solution)/shard_map/all_to_all | solution.py:426
  35.3 0.2 total.1
  35.5 10.2 %collective-permute-start.1 = (bf16[80,128]{1,0:T(8,128)(2,1)S(1)}, bf16[80,128]{1,0:T(8,128)(2,1)S(1)}, u32[]{:S(2)}, u32[]{:S(2)}) collective-permute-start(bf16[80,128]{1,0:T(8,128)(2,1)S(1)} %get-tuple-element.37), channel_id=1, source_target_pairs={{0,32},{1,33},{2,34},{3,35},{4,36},{5,37},{6,38},{7,39},{8,40},{9,... | collective-permute-start | bytes 61448 | tf_op jit(solution)/shard_map/ppermute | solution.py:435
  45.7 1.2 %ready.1 = (f32[512,256]{1,0:T(8,128)S(1)}, bf16[128,2048]{1,0:T(8,128)(2,1)S(1)}, f32[8,128]{1,0:T(8,128)S(1)}, bf16[512,256]{1,0:T(8,128)(2,1)S(1)}, f32[16,256]{1,0:T(8,128)S(1)}, /*index=5*/f32[8,256]{1,0:T(8,128)S(1)}) custom-call(f32[80,128]{1,0:T(8,128)S(1)} %get-tuple-element.36.mine_ref, bf16[512,256]{1,0:T(8,128)(2,1)} %gate_hbm.1, ...), custom_call_target="tpu_custom_call" | custom-call | flops 2097152 | bytes 1048576 | tf_op jit(solution)/shard_map/ready/pallas_call | solution.py:436
  46.9 0.0 collective-permute-done.1.other_ref
  46.9 0.2 share.1
  47.2 21.2 %all_to_all.16.g_ref = bf16[32,72,128]{2,1,0:T(8,128)(2,1)S(1)} all-to-all(bf16[32,72,128]{2,1,0:T(8,128)(2,1)S(1)} %share.1), channel_id=1, replica_groups={{0,1,2,3,4,5,6,7,8,9,10,11,12,13,14,15,16,17,18,19,20,21,22,23,24,25,26..., dimensions={0} | all-to-all | bytes 1179648 | tf_op jit(solution)/shard_map/all_to_all | solution.py:467
  68.4 3.5 %ends.1 = (f32[512,256]{1,0:T(8,128)}, f32[16,8,256]{2,1,0:T(8,128)}, f32[8,256]{1,0:T(8,128)}, bf16[512,128]{1,0:T(8,128)(2,1)}, bf16[8,40,128]{2,1,0:T(8,128)(2,1)}) custom-call(bf16[32,72,128]{2,1,0:T(8,128)(2,1)S(1)} %all_to_all.16.g_ref, f32[512,256]{1,0:T(8,128)S(1)} %get-tuple-element.39.act_ref, bf16[512,256]{1,0:T(8,128)(2,1)S(1)} %get-tuple-element.40.dw_ref, ...), custom_call_target="tpu_custom_call" | custom-call | tf_op jit(solution)/shard_map/ends/pallas_call | solution.py:476
  71.9 7.9 %all-to-all-start.2 = ((bf16[8,40,128]{2,1,0:T(8,128)(2,1)}), bf16[8,40,128]{2,1,0:T(8,128)(2,1)S(1)}, u32[]{:S(2)}, u32[]{:S(2)}) async-start(bf16[8,40,128]{2,1,0:T(8,128)(2,1)} %get-tuple-element.44), calls=%async_computation.2 | async-start | bytes 163840 | tf_op jit(solution)/shard_map/all_to_all | solution.py:494
  79.7 4.5 %local_scan.1 = (f32[512,256]{1,0:T(8,128)S(1)}, f32[512,256]{1,0:T(8,128)S(1)}, bf16[512,128]{1,0:T(8,128)(2,1)S(1)}) custom-call(f32[512,256]{1,0:T(8,128)S(1)} %get-tuple-element.39.act_ref, f32[16,256]{1,0:T(8,128)S(1)} %get-tuple-element.42.rate, bf16[128,2048]{1,0:T(8,128)(2,1)S(1)} %get-tuple-element.43.spread_ref, ...), custom_call_target="tpu_custom_call" | custom-call | flops 12582912 | bytes 4194304 | tf_op jit(solution)/shard_map/local_scan/pallas_call | solution.py:495
  84.2 0.8 all-to-all-done.2.got_ref
  85.0 2.9 %finish.1 = bf16[512,256]{1,0:T(8,128)(2,1)} custom-call(bf16[8,40,128]{2,1,0:T(8,128)(2,1)S(1)} %all-to-all-done.2.got_ref, bf16[512,128]{1,0:T(8,128)(2,1)S(1)} %get-tuple-element.49.maps_ref, bf16[128,2048]{1,0:T(8,128)(2,1)S(1)} %get-tuple-element.43.spread_ref, f32[512,256]{1,0:T(8,128)S(1)} %get-tuple-element.50.y_ref, ...), custom_call_target="tpu_custom_call" | custom-call | tf_op jit(solution)/shard_map/finish/pallas_call | solution.py:515
Async XLA Ops:
  0.7 8.8 %collective-permute-start = (bf16[16,256]{1,0:T(8,128)(2,1)S(1)}, bf16[16,256]{1,0:T(8,128)(2,1)S(1)}, u32[]{:S(2)}, u32[]{:S(2)}) collective-permute-start(bf16[16,256]{1,0:T(8,128)(2,1)S(1)} %slice.3), channel_id=1, source_target_pairs={{0,64},{64,128},{128,192},{192,256},{256,320},{320,384},{384,448},... | collective-permute-start | bytes 24584 | tf_op jit(solution)/shard_map/ppermute | solution.py:376
  35.5 11.4 %collective-permute-start.1 = (bf16[80,128]{1,0:T(8,128)(2,1)S(1)}, bf16[80,128]{1,0:T(8,128)(2,1)S(1)}, u32[]{:S(2)}, u32[]{:S(2)}) collective-permute-start(bf16[80,128]{1,0:T(8,128)(2,1)S(1)} %get-tuple-element.37), channel_id=1, source_target_pairs={{0,32},{1,33},{2,34},{3,35},{4,36},{5,37},{6,38},{7,39},{8,40},{9,... | collective-permute-start | bytes 61448 | tf_op jit(solution)/shard_map/ppermute | solution.py:435
  71.9 13.1 %all-to-all-start.2 = ((bf16[8,40,128]{2,1,0:T(8,128)(2,1)}), bf16[8,40,128]{2,1,0:T(8,128)(2,1)S(1)}, u32[]{:S(2)}, u32[]{:S(2)}) async-start(bf16[8,40,128]{2,1,0:T(8,128)(2,1)} %get-tuple-element.44), calls=%async_computation.2 | async-start | bytes 163840 | tf_op jit(solution)/shard_map/all_to_all | solution.py:494

commit v9 on v8

--- a/solution.py
+++ b/solution.py
@@ -177,10 +177,17 @@
     return pl.ds(pl.multiple_of(step * CHUNKS, CHUNKS), CHUNKS)
 
 
+def unpack_maps(g_ref, maps_ref):
+    for block in range(g_ref.shape[0]):
+        packed = g_ref[block].astype(F32)[-(OWN // 2) :, :]
+        both = jnp.concatenate([packed, pltpu.roll(packed, LANES // 2, 1)], axis=0)
+        maps_ref[block * OWN : (block + 1) * OWN, :] = both.astype(BF16)
+
+
 def ends_kernel(
     g_ref, act_ref, dw_ref, vecs_ref, rate, spread_ref,
-    delta_hbm, inside_hbm, before_hbm, maps_hbm, pay_hbm,
-    delta, inside_ref, before_ref, maps_ref, pay_ref, low, drive, b_all, cum_ref, ends, sems,
+    delta_hbm, inside_hbm, before_hbm, pay_hbm,
+    delta, inside_ref, before_ref, pay_ref, maps_ref, low, drive, b_all, cum_ref, ends, sems,
 ):
     rows, width = act_ref.shape
     steps = rows // CHUNKS
@@ -189,18 +196,15 @@
         at = slice(block * OWN, (block + 1) * OWN)
         for piece in range(low.shape[1] // LANES):
             low[at, piece * LANES : (piece + 1) * LANES] = g_ref[block, piece * OWN : (piece + 1) * OWN, :]
-        packed = g_ref[block].astype(F32)[-(OWN // 2) :, :]
-        maps_ref[at, :] = jnp.concatenate([packed, pltpu.roll(packed, LANES // 2, 1)], axis=0).astype(BF16)
+    unpack_maps(g_ref, maps_ref)
     z = jnp.dot(low[...], dw_ref[...], preferred_element_type=F32) + vecs_ref[0:1, :]
     step_size = jnp.maximum(z, 0.0) + jnp.log1p(jnp.exp(-jnp.abs(z)))
     delta[...] = step_size
     pairs = (
-        (delta, delta_hbm), (maps_ref, maps_hbm),
-        (inside_ref, inside_hbm), (before_ref, before_hbm), (pay_ref, pay_hbm),
+        (delta, delta_hbm), (inside_ref, inside_hbm), (before_ref, before_hbm), (pay_ref, pay_hbm),
     )
     copies = [pltpu.make_async_copy(source, target, sems.at[i]) for i, (source, target) in enumerate(pairs)]
     copies[0].start()
-    copies[1].start()
     drive[...] = step_size * act_ref[...]
     b_all[...] = jnp.dot(maps_ref[...], spread_ref[...], preferred_element_type=F32)
     chunk = lax.broadcasted_iota(jnp.int32, (CHUNKS, LANES), 0)
@@ -247,8 +251,8 @@
         before_ref[:, cols] = jnp.where(chunk >= 1, pltpu.roll(sums[-1], 1, 0), 0.0)
         ends[STATE : STATE + 1, cols] = sums[-1][CHUNKS - 1 :, :]
 
+    copies[1].start()
     copies[2].start()
-    copies[3].start()
     me = lax.axis_index("ctx")
     row = lax.broadcasted_iota(jnp.int32, (CHUNKS, LANES), 0)
     pieces, tail = [], zero
@@ -261,13 +265,13 @@
     block = jnp.concatenate(pieces + [tail], axis=0)
     for target in range(pay_ref.shape[0]):
         pay_ref[target] = jnp.where(target > me, block, 0.0).astype(BF16)
-    copies[4].start()
+    copies[3].start()
     for copy in copies:
         copy.wait()
 
 
 def local_kernel(
-    act_ref, rate, spread_ref, delta_hbm, inside_hbm, before_hbm, maps_hbm, gain_hbm,
+    g_ref, act_ref, rate, spread_ref, delta_hbm, inside_hbm, before_hbm, gain_hbm,
     y_ref, cum_ref, maps_ref,
     b_all, c_all, delta, inside_ref, before_ref, both_ref, gain_ref, sems,
 ):
@@ -275,18 +279,17 @@
     steps = rows // CHUNKS
     halves = width // LANES
     pairs = (
-        (maps_hbm, both_ref), (delta_hbm, delta),
-        (inside_hbm, inside_ref), (before_hbm, before_ref), (gain_hbm, gain_ref),
+        (delta_hbm, delta), (inside_hbm, inside_ref), (before_hbm, before_ref), (gain_hbm, gain_ref),
     )
     copies = [pltpu.make_async_copy(source, target, sems.at[i]) for i, (source, target) in enumerate(pairs)]
     for copy in copies:
         copy.start()
-    copies[0].wait()
+    unpack_maps(g_ref, both_ref)
     maps = both_ref[...]
     b_all[...] = jnp.dot(maps, spread_ref[...], preferred_element_type=F32)
     maps_ref[...] = pltpu.roll(maps.astype(F32), LANES - STATE, 1).astype(BF16)
     c_all[...] = jnp.dot(maps_ref[...], spread_ref[...], preferred_element_type=F32)
-    for copy in copies[1:]:
+    for copy in copies:
         copy.wait()
     for half in range(halves):
         cols = slice(half * LANES, (half + 1) * LANES)
@@ -470,22 +473,22 @@
         ((rows, width), F32),
         ((STATE, CHUNKS, width), F32),
         ((CHUNKS, width), F32),
-        ((rows, LANES), BF16),
         ((n_ctx, halves * STATE + CHUNKS, LANES), BF16),
     )
-    delta, inside, before, maps_all, pay = pl.pallas_call(
+    delta, inside, before, pay = pl.pallas_call(
         ends_kernel,
         out_shape=tuple(pltpu.HBM(*kept) for kept in sent),
         in_specs=vmem(6),
-        out_specs=tuple(hbm(5)),
+        out_specs=tuple(hbm(4)),
         scratch_shapes=[
             *(pltpu.VMEM(*kept) for kept in sent),
+            pltpu.VMEM((rows, LANES), BF16),
             pltpu.VMEM((rows, rank), BF16),
             pltpu.VMEM((rows, width), F32),
             big,
             pltpu.VMEM((rows, width), F32),
             pltpu.VMEM((STATE + 8, width), F32),
-            pltpu.SemaphoreType.DMA((5,)),
+            pltpu.SemaphoreType.DMA((4,)),
         ],
         compiler_params=pltpu.CompilerParams(vmem_limit_bytes=16 * MIB),
         name="ends",
@@ -499,19 +502,20 @@
             tile,
             jax.ShapeDtypeStruct((rows, LANES), BF16),
         ),
-        in_specs=vmem(3) + hbm(5),
+        in_specs=vmem(4) + hbm(4),
         out_specs=tuple(vmem(3)),
         scratch_shapes=[
             big,
             big,
-            *(pltpu.VMEM(*kept) for kept in sent[:4]),
+            *(pltpu.VMEM(*kept) for kept in sent[:3]),
+            pltpu.VMEM((rows, LANES), BF16),
             pltpu.VMEM((1, width), F32),
-            pltpu.SemaphoreType.DMA((5,)),
+            pltpu.SemaphoreType.DMA((4,)),
         ],
         compiler_params=pltpu.CompilerParams(vmem_limit_bytes=24 * MIB),
         cost_estimate=pl.CostEstimate(flops=6 * cells, bytes_accessed=8 * rows * width * 4, transcendentals=cells),
         name="local_scan",
-    )(act, rate, spread, *stay(delta, inside, before, maps_all, skip_gain[None, :]))
+    )(gathered, act, rate, spread, *stay(delta, inside, before, skip_gain[None, :]))
     return pl.pallas_call(
         finish_kernel,
         out_shape=jax.ShapeDtypeStruct((rows, width), BF16),

time: 88.3 us -> 88.3 us (level)
  no operation moved by 1% of the time
where the time goes in v9:
time: 88.3 us; the launch traced here: 87.9 us
  blocking collectives  46.7 us (53%)
  starting transfers between devices  23.4 us (27%)
  Pallas kernels  15 us (17%)
  waiting for transfers between devices  2.05 us (2%)
    all_to_all x1, blocking collectives, on_device(): parts = lax.all_to_all(part, 'ch', 0, 0, axis_index_groups=groups)  25.5 us
    all_to_all x1, blocking collectives, on_device(): gathered = lax.all_to_all(totals, 'ch', 0, 0, axis_index_groups=groups)  21.2 us
    ppermute x1, starting transfers between devices, on_device(): lax.ppermute(send, 'ch', [(i, (i + near) % n_ch) for i in range(n_ch)])  10.2 us
    all_to_all x1, starting transfers between devices, on_device(): got = lax.all_to_all(pay, 'ctx', 0, 0)  7.86 us
    ppermute x1, starting transfers between devices, on_device(): lax.ppermute(mamba_in[rows - 16:], 'ctx', [(i, i + 1) for i in range(n_ct...  5.38 us
    pallas_call x1, Pallas kernels, on_device(): pl.pallas_call(local_kernel, out_shape=(tile, tile, jax.ShapeDtypeStruct(...  4.56 us
    pallas_call x1, Pallas kernels, on_device(): pl.pallas_call(ends_kernel, out_shape=tuple((pltpu.HBM(*kept) for kept in...  3.43 us
    pallas_call x1, Pallas kernels, on_device(): pl.pallas_call(finish_kernel, out_shape=jax.ShapeDtypeStruct((rows, width...  2.94 us
  transfers between devices with their start and end apart: 3, of which 2 were waited for; matrix products, arithmetic and copies ran while one was open for 0% of the time, Pallas kernels for 9%

profile of v9, /device:TPU:1, one launch (start us, length us, event | category | flops | bytes accessed | tf_op | source)
XLA Modules:
  0.0 87.9 jit_solution(18380007315435062413)
XLA Ops:
  0.0 0.7 slice.3
  0.7 5.4 %collective-permute-start = (bf16[16,256]{1,0:T(8,128)(2,1)S(1)}, bf16[16,256]{1,0:T(8,128)(2,1)S(1)}, u32[]{:S(2)}, u32[]{:S(2)}) collective-permute-start(bf16[16,256]{1,0:T(8,128)(2,1)S(1)} %slice.3), channel_id=1, source_target_pairs={{0,64},{64,128},{128,192},{192,256},{256,320},{320,384},{384,448},... | collective-permute-start | bytes 24584 | tf_op jit(solution)/shard_map/ppermute | solution.py:379
  6.1 2.1 %project.1 = (f32[512,256]{1,0:T(8,128)S(1)}, bf16[32,72,128]{2,1,0:T(8,128)(2,1)S(1)}, f32[8,256]{1,0:T(8,128)S(1)}, bf16[256,512]{1,0:T(8,128)(2,1)S(1)}, bf16...) custom-call(bf16[512,256]{1,0:T(8,128)(2,1)} %x_hbm.1, bf16[256,512]{1,0:T(8,128)(2,1)} %pd_hbm.1, ...), custom_call_target="tpu_custom_call" | custom-call | flops 167772160 | bytes 2097152 | tf_op jit(solution)/shard_map/project/pallas_call | solution.py:380
  8.2 1.4 %collective-permute-done.halo_ref = bf16[16,256]{1,0:T(8,128)(2,1)S(1)} collective-permute-done((bf16[16,256]{1,0:T(8,128)(2,1)S(1)}, bf16[16,256]{1,0:T(8,128)(2,1)S(1)}, u32[]{:S(2)}, u32[]{:S(2)}) %collective-permute-start) | collective-permute-done | bytes 8224 | tf_op jit(solution)/shard_map/ppermute | solution.py:379
  9.5 0.3 first_rows.1
  9.8 25.5 %all_to_all.15.parts_ref = bf16[32,72,128]{2,1,0:T(8,128)(2,1)S(1)} all-to-all(bf16[32,72,128]{2,1,0:T(8,128)(2,1)S(1)} %get-tuple-element.34), channel_id=1, replica_groups={{0,1,2,3,4,5,6,7,8,9,10,11,12,13,14,15,16,17,18,19,20,21,22,23,24,25,26..., dimensions={0} | all-to-all | bytes 1179648 | tf_op jit(solution)/shard_map/all_to_all | solution.py:429
  35.3 0.2 total.1
  35.5 10.2 %collective-permute-start.1 = (bf16[80,128]{1,0:T(8,128)(2,1)S(1)}, bf16[80,128]{1,0:T(8,128)(2,1)S(1)}, u32[]{:S(2)}, u32[]{:S(2)}) collective-permute-start(bf16[80,128]{1,0:T(8,128)(2,1)S(1)} %get-tuple-element.36), channel_id=1, source_target_pairs={{0,32},{1,33},{2,34},{3,35},{4,36},{5,37},{6,38},{7,39},{8,40},{9,... | collective-permute-start | bytes 61448 | tf_op jit(solution)/shard_map/ppermute | solution.py:438
  45.7 1.2 %ready.1 = (f32[512,256]{1,0:T(8,128)S(1)}, bf16[128,2048]{1,0:T(8,128)(2,1)S(1)}, f32[8,128]{1,0:T(8,128)S(1)}, bf16[512,256]{1,0:T(8,128)(2,1)S(1)}, f32[16,256]{1,0:T(8,128)S(1)}, /*index=5*/f32[8,256]{1,0:T(8,128)S(1)}) custom-call(f32[80,128]{1,0:T(8,128)S(1)} %get-tuple-element.35.mine_ref, bf16[512,256]{1,0:T(8,128)(2,1)} %gate_hbm.1, ...), custom_call_target="tpu_custom_call" | custom-call | flops 2097152 | bytes 1048576 | tf_op jit(solution)/shard_map/ready/pallas_call | solution.py:439
  46.9 0.0 collective-permute-done.1.other_ref
  46.9 0.2 share.1
  47.2 21.2 %all_to_all.16.g_ref = bf16[32,72,128]{2,1,0:T(8,128)(2,1)S(1)} all-to-all(bf16[32,72,128]{2,1,0:T(8,128)(2,1)S(1)} %share.1), channel_id=1, replica_groups={{0,1,2,3,4,5,6,7,8,9,10,11,12,13,14,15,16,17,18,19,20,21,22,23,24,25,26..., dimensions={0} | all-to-all | bytes 1179648 | tf_op jit(solution)/shard_map/all_to_all | solution.py:470
  68.4 3.4 %ends.1 = (f32[512,256]{1,0:T(8,128)}, f32[16,8,256]{2,1,0:T(8,128)}, f32[8,256]{1,0:T(8,128)}, bf16[8,40,128]{2,1,0:T(8,128)(2,1)}) custom-call(bf16[32,72,128]{2,1,0:T(8,128)(2,1)S(1)} %all_to_all.16.g_ref, f32[512,256]{1,0:T(8,128)S(1)} %get-tuple-element.38.act_ref, bf16[512,256]{1,0:T(8,128)(2,1)S(1)} %get-tuple-element.39.dw_ref, ...), custom_call_target="tpu_custom_call" | custom-call | tf_op jit(solution)/shard_map/ends/pallas_call | solution.py:478
  71.8 7.9 %all-to-all-start.2 = ((bf16[8,40,128]{2,1,0:T(8,128)(2,1)}), bf16[8,40,128]{2,1,0:T(8,128)(2,1)S(1)}, u32[]{:S(2)}, u32[]{:S(2)}) async-start(bf16[8,40,128]{2,1,0:T(8,128)(2,1)} %get-tuple-element.43), calls=%async_computation.2 | async-start | bytes 163840 | tf_op jit(solution)/shard_map/all_to_all | solution.py:497
  79.7 4.6 %local_scan.1 = (f32[512,256]{1,0:T(8,128)S(1)}, f32[512,256]{1,0:T(8,128)S(1)}, bf16[512,128]{1,0:T(8,128)(2,1)S(1)}) custom-call(bf16[32,72,128]{2,1,0:T(8,128)(2,1)S(1)} %all_to_all.16.g_ref, f32[512,256]{1,0:T(8,128)S(1)} %get-tuple-element.38.act_ref, f32[16,256]{1,0:T(8,128)S(1)} %get-tuple-element.41.rate, ...), custom_call_target="tpu_custom_call" | custom-call | flops 12582912 | bytes 4194304 | tf_op jit(solution)/shard_map/local_scan/pallas_call | solution.py:498
  84.3 0.7 all-to-all-done.2.got_ref
  85.0 2.9 %finish.1 = bf16[512,256]{1,0:T(8,128)(2,1)} custom-call(bf16[8,40,128]{2,1,0:T(8,128)(2,1)S(1)} %all-to-all-done.2.got_ref, bf16[512,128]{1,0:T(8,128)(2,1)S(1)} %get-tuple-element.47.maps_ref, bf16[128,2048]{1,0:T(8,128)(2,1)S(1)} %get-tuple-element.42.spread_ref, f32[512,256]{1,0:T(8,128)S(1)} %get-tuple-element.48.y_ref, ...), custom_call_target="tpu_custom_call" | custom-call | tf_op jit(solution)/shard_map/finish/pallas_call | solution.py:519
Async XLA Ops:
  0.7 8.8 %collective-permute-start = (bf16[16,256]{1,0:T(8,128)(2,1)S(1)}, bf16[16,256]{1,0:T(8,128)(2,1)S(1)}, u32[]{:S(2)}, u32[]{:S(2)}) collective-permute-start(bf16[16,256]{1,0:T(8,128)(2,1)S(1)} %slice.3), channel_id=1, source_target_pairs={{0,64},{64,128},{128,192},{192,256},{256,320},{320,384},{384,448},... | collective-permute-start | bytes 24584 | tf_op jit(solution)/shard_map/ppermute | solution.py:379
  35.5 11.4 %collective-permute-start.1 = (bf16[80,128]{1,0:T(8,128)(2,1)S(1)}, bf16[80,128]{1,0:T(8,128)(2,1)S(1)}, u32[]{:S(2)}, u32[]{:S(2)}) collective-permute-start(bf16[80,128]{1,0:T(8,128)(2,1)S(1)} %get-tuple-element.36), channel_id=1, source_target_pairs={{0,32},{1,33},{2,34},{3,35},{4,36},{5,37},{6,38},{7,39},{8,40},{9,... | collective-permute-start | bytes 61448 | tf_op jit(solution)/shard_map/ppermute | solution.py:438
  71.8 13.1 %all-to-all-start.2 = ((bf16[8,40,128]{2,1,0:T(8,128)(2,1)}), bf16[8,40,128]{2,1,0:T(8,128)(2,1)S(1)}, u32[]{:S(2)}, u32[]{:S(2)}) async-start(bf16[8,40,128]{2,1,0:T(8,128)(2,1)} %get-tuple-element.43), calls=%async_computation.2 | async-start | bytes 163840 | tf_op jit(solution)/shard_map/all_to_all | solution.py:497
